TPU v7x, 32 devices: a whole 2x2x4 slice. The times are simulated.
32 devices in a mesh: led: 8 (over z, core), tile: 4 (over y, x).
Axes of the slice: x: 2, y: 2, z: 4, core: 2. Of those that a mesh axis runs over, the one named last changes fastest.
Arguments:
- spectrum: float32 [16, 8, 4, 8, 65536], P(None, None, 'tile', 'led'), may hold values from -6 to 6
- intensities: bfloat16 [8, 1024, 1024], P('led', 'tile'), may hold values from 0 to 2
- led_of_slot: int32 [8], replicated, may hold values from 0 to 7, each once
- row_offset: int32 [8], replicated, may hold values from 0 to 120
- col_offset: int32 [8], replicated, may hold values from 0 to 56
- tile_mask: int32 [8, 8, 8], replicated, may hold values 0 or 1
- aberration: float32 [5], replicated, may hold values from -1.5 to 1.5
Outputs:
- updated: float32 [16, 8, 4, 8, 65536], P(None, None, 'tile', 'led')
Inputs may be any that keep to these rules, and one draw needn't show every extreme that they name: `led_of_slot`: every LED is imaged in exactly one slot.
All inputs are finite; a program needn't handle non-finite values.
Results may differ from a plain program's by a relative error of at most 0.0003.
Values sent between devices are 32-bit elements; how exact they have to be, the bound alone decides.
No kernel may reach another device: no remote copies, remote signals or barrier semaphores. Data moves between devices by JAX's collectives and lax.ppermute only.
A program may use at most 192 MiB of HBM per device.

v0:
```python
import math

import jax
import jax.numpy as jnp
from jax import lax
from jax.sharding import PartitionSpec as P

M = 1024
TILE = 128
GR = 16
GC = 8
L_DEV = 1


STEP_SIZE = 0.25
HIGHEST_MODE = lax.Precision.HIGHEST


def aberration_phase(aberration, coord_p, coord_q):
    radial = coord_p * coord_p + coord_q * coord_q
    return (
        aberration[0] * (2.0 * radial - 1.0)
        + aberration[1] * (coord_p * coord_p - coord_q * coord_q)
        + aberration[2] * (2.0 * coord_p * coord_q)
        + aberration[3] * ((3.0 * radial - 2.0) * coord_p)
        + aberration[4] * ((3.0 * radial - 2.0) * coord_q)
    )


def dft_table(length):
    index_run = jnp.arange(length, dtype=jnp.int32)
    column_run = jnp.arange(2 * length, dtype=jnp.int32)
    product_mod = index_run[:, None] * (column_run % length)[None, :] % length
    shifted = (column_run >= length).astype(jnp.float32) * (0.5 * math.pi)
    angles = product_mod.astype(jnp.float32) * (2.0 * math.pi / length) - shifted[None, :]
    return jnp.cos(angles)


def small_tables(rows_len, cols_len, modulus, sign):
    first_run = jnp.arange(rows_len, dtype=jnp.int32)
    second_run = jnp.arange(cols_len, dtype=jnp.int32)
    product_mod = first_run[:, None] * second_run[None, :] % modulus
    angles = product_mod.astype(jnp.float32) * (2.0 * math.pi / modulus)
    return (jnp.cos(angles), sign * jnp.sin(angles))


def factor_dft(real_part, imag_part, sign):
    length = real_part.shape[-1]
    first = 1 << (length.bit_length() - 1) // 2
    second = length // first
    leading = real_part.shape[:-1]
    cos_first, sin_first = small_tables(first, first, first, sign)
    cos_second, sin_second = small_tables(second, second, second, sign)
    twid_cos, twid_sin = small_tables(first, second, length, sign)
    flat_re = real_part.reshape(-1, first, second)
    flat_im = imag_part.reshape(-1, first, second)

    def section_one(data, table):
        return jnp.einsum("rab,ak->rkb", data, table, precision=HIGHEST_MODE)

    def section_two(data, table):
        return jnp.einsum("rkb,bl->rlk", data, table, precision=HIGHEST_MODE)

    mid_re = section_one(flat_re, cos_first) - section_one(flat_im, sin_first)
    mid_im = section_one(flat_im, cos_first) + section_one(flat_re, sin_first)
    turned_re = mid_re * twid_cos[None] - mid_im * twid_sin[None]
    turned_im = mid_re * twid_sin[None] + mid_im * twid_cos[None]
    out_re = section_two(turned_re, cos_second) - section_two(turned_im, sin_second)
    out_im = section_two(turned_im, cos_second) + section_two(turned_re, sin_second)
    return (out_re.reshape(leading + (length,)), out_im.reshape(leading + (length,)))


def times_table(operand, transform):
    return jnp.dot(operand, transform, precision=HIGHEST_MODE, preferred_element_type=jnp.float32)


def pupil_parts(aberration, tile_gate, row_window, col_window):
    halfway = M // 2
    coord_p = ((row_window - halfway).astype(jnp.float32) / halfway)[:, None]
    coord_q = ((col_window - halfway).astype(jnp.float32) / halfway)[None, :]
    phase_map = aberration_phase(aberration, coord_p, coord_q)
    tiles_side = tile_gate.shape[0]
    tile_ids = jnp.arange(tiles_side, dtype=jnp.int32)
    pick_rows = ((row_window // TILE)[:, None] == tile_ids[None, :]).astype(jnp.float32)
    pick_cols = (tile_ids[:, None] == (col_window // TILE)[None, :]).astype(jnp.float32)
    gate_map = times_table(times_table(pick_rows, tile_gate.astype(jnp.float32)), pick_cols)
    return (gate_map * jnp.cos(phase_map), gate_map * jnp.sin(phase_map))


def stack_blocks(real_part, imag_part, tile_count, band_rows):
    slots_now = real_part.shape[0]
    rows_now = real_part.shape[1]
    stacked = jnp.stack(
        [
            real_part.reshape(slots_now, rows_now, tile_count, band_rows),
            imag_part.reshape(slots_now, rows_now, tile_count, band_rows),
        ],
        axis=3,
    )
    return stacked.reshape(slots_now, rows_now, tile_count, 2 * band_rows)


def finish_rows(rows_back, pupil_re, pupil_im, row_first, row_count, led_count, unit_cols):
    image_side = rows_back.shape[0]
    part_re = jnp.transpose(rows_back[:, 0, row_first : row_first + row_count])
    part_im = jnp.transpose(rows_back[:, 1, row_first : row_first + row_count])
    grad_re, grad_im = factor_dft(part_re, part_im, -1.0)
    grad_re = grad_re / image_side
    grad_im = grad_im / image_side
    out_re = pupil_re * grad_re + pupil_im * grad_im
    out_im = pupil_re * grad_im - pupil_im * grad_re
    stacked = jnp.stack([out_re, out_im]).reshape(2, row_count, led_count, unit_cols)
    return jnp.transpose(stacked, (2, 0, 1, 3)).reshape(led_count, 2 * row_count * unit_cols)


def shards(spectrum, intensities, led_of_slot, row_offset, col_offset, tile_mask, aberration):
    tile_count = lax.axis_size("tile")
    led_count = lax.axis_size("led")
    band_rows = M // tile_count
    unit_cols = M // led_count
    piece_cells = band_rows * unit_cols
    led_here = lax.axis_index("led")
    tile_here = lax.axis_index("tile")
    transform = dft_table(M)
    row_start = row_offset[led_of_slot] * TILE
    col_start = col_offset[led_of_slot] * TILE
    row_pos = tile_here * band_rows + jnp.arange(band_rows, dtype=jnp.int32)
    first_col_here = led_here * unit_cols
    row_group = (row_start[:, None] + (row_pos[None, :] - row_start[:, None]) % M) // M
    col_group = (col_start + (first_col_here - col_start) % M) // M
    row_group = row_group.reshape(led_count, L_DEV, band_rows)
    col_group = col_group.reshape(led_count, L_DEV, 1)
    line_ids = (
        (row_group * GC + col_group) * band_rows
        + jnp.arange(band_rows, dtype=jnp.int32)[None, None, :]
    ).reshape(-1)
    local_lines = jnp.transpose(
        spectrum.reshape(GR, GC, 2, band_rows, unit_cols), (0, 1, 3, 2, 4)
    ).reshape(GR * GC * band_rows, 2 * unit_cols)
    taken = local_lines[line_ids].reshape(led_count, L_DEV, band_rows, 2, unit_cols)
    outgoing = jnp.transpose(taken, (0, 1, 3, 2, 4)).reshape(led_count, L_DEV, 2 * piece_cells)
    incoming = lax.all_to_all(outgoing, "led", split_axis=0, concat_axis=0, tiled=True)
    col_all = jnp.arange(M, dtype=jnp.int32)
    slot_index = led_here * L_DEV + 0
    led_index = led_of_slot[slot_index]
    first_row = row_offset[led_index] * TILE
    first_col = col_offset[led_index] * TILE
    pupil_re, pupil_im = pupil_parts(
        aberration, tile_mask[led_index], (row_pos - first_row) % M, (col_all - first_col) % M
    )
    window = incoming[:, 0].reshape(led_count, 2, band_rows, unit_cols)
    window = jnp.transpose(window, (1, 2, 0, 3)).reshape(2, band_rows, M)
    field_re = pupil_re * window[0] - pupil_im * window[1]
    field_im = pupil_re * window[1] + pupil_im * window[0]
    fields = [jnp.stack([field_re, field_im])]
    pupils = (pupil_re, pupil_im)
    stacked_fields = jnp.stack(fields).reshape(L_DEV * 2 * band_rows, M)
    mixed = times_table(stacked_fields, transform).reshape(L_DEV, 2, band_rows, 2 * M)
    along_re = mixed[:, 0, :, :M] - mixed[:, 1, :, M:]
    along_im = mixed[:, 0, :, M:] + mixed[:, 1, :, :M]
    outbound = stack_blocks(along_re, along_im, tile_count, band_rows)
    columns = lax.all_to_all(outbound, "tile", split_axis=2, concat_axis=1, tiled=True).reshape(
        L_DEV, M, 2 * band_rows
    )
    flipped = jnp.swapaxes(columns, 1, 2)
    wave_re, wave_im = factor_dft(flipped[:, :band_rows], flipped[:, band_rows:], 1.0)
    wave_re = wave_re / M
    wave_im = wave_im / M
    measured = intensities.astype(jnp.float32)
    excess = wave_re * wave_re + wave_im * wave_im - measured
    back_re, back_im = factor_dft(excess * wave_re, excess * wave_im, -1.0)
    inbound = stack_blocks(back_re, back_im, tile_count, band_rows)
    rows_back = lax.all_to_all(inbound, "tile", split_axis=2, concat_axis=1, tiled=True).reshape(
        L_DEV, M, 2, band_rows
    )
    outgoing_all = jnp.stack(
        [finish_rows(rows_back[0], pupils[0], pupils[1], 0, band_rows, led_count, unit_cols)],
        axis=1,
    )
    received = lax.all_to_all(outgoing_all, "led", split_axis=0, concat_axis=0, tiled=True)
    grad_lines = jnp.transpose(
        received.reshape(led_count, L_DEV, 2, band_rows, unit_cols), (0, 1, 3, 2, 4)
    ).reshape(led_count * L_DEV * band_rows, 2 * unit_cols)
    grad_sum = jax.ops.segment_sum(grad_lines, line_ids, num_segments=GR * GC * band_rows)
    grad_sum = jnp.transpose(grad_sum.reshape(GR, GC, band_rows, 2, unit_cols), (0, 1, 3, 2, 4))
    updated = spectrum - STEP_SIZE * grad_sum.reshape(spectrum.shape)
    return updated


def solution(mesh):
    placed = (P(None, None, "tile", "led", None), P("led", "tile", None), P(), P(), P(), P(), P())
    return jax.shard_map(
        shards,
        mesh=mesh,
        in_specs=placed,
        out_specs=P(None, None, "tile", "led", None),
        check_vma=False,
    )
```

profile of v0, /device:TPU:11, one launch (start us, length us, event | category | flops | bytes accessed | tf_op | source)
XLA Modules:
  0.0 634.1 jit_solution(13607130324908814314)
XLA Ops:
  8.6 54.9 %copy.123 = f32[16,8,2,256,128]{4,2,3,1,0:T(2,128)} copy(f32[16,8,2,256,128]{4,3,2,1,0:T(8,128)} %bitcast.252) | data formatting | bytes 67108864 | tf_op jit(solution)/shard_map/reshape | solution.py:138
  63.4 25.0 %copy.260 = f32[4096,8,2,128]{3,1,2,0:T(8,128)} copy(f32[4096,8,2,128]{3,2,1,0:T(2,128)} %bitcast.254) | data formatting | bytes 67108864
  88.6 17.2 %gather_fusion.2 = f32[2048,256]{1,0:T(8,128)S(1)} fusion(f32[32768,256]{1,0:T(8,128)} %bitcast.255, s32[2048]{0:T(1024)S(1)} %broadcast_clamp_fusion), kind=kCustom, calls=%fused_computation.2 | custom fusion | bytes 4202496 | tf_op jit(solution)/shard_map/gather | solution.py:140
  105.8 2.1 reshape.564
  107.9 3.1 copy.124
  111.0 6.0 all-to-all-start
  120.6 41.8 %all-to-all-done = f32[8,1,65536]{2,1,0:T(1,128)} async-done(((f32[8,1,65536]{2,1,0:T(1,128)}), f32[8,1,65536]{2,1,0:T(1,128)}, u32[]{:S(2)}, u32[]{:S(2)}) %all-to-all-start) | async-done | bytes 2097184 | tf_op jit(solution)/shard_map/all_to_all | solution.py:142
  165.4 8.1 %fusion.51 = (f32[1,256,1024]{2,1,0:T(8,128)S(1)}, f32[1,256,1024]{2,1,0:T(8,128)S(1)}) fusion(f32[32,8,8,128]{3,2,1,0:T(8,128)S(1)} %bitcast.279, f32[32,8,8,128]{3,2,1,0:T(8,128)S(1)} %bitcast.280, f32[256,1024]{1,0:T(8,128)S(1)} %fusion.94, f32[]{:T(128)} %bitcast.10, f32[256]{0:T(256)S(1)} %get-tuple-element.35, f32[]{:T(128)} %bitcast.9, ...), kind=kLoop, calls=%fused_computation.76 | loop fusion | flops 6815744 | bytes 5254164 | tf_op jit(solution)/shard_map/stack | solution.py:155
  173.8 44.9 %fusion.21 = f32[1,2,256,2048]{3,2,1,0:T(8,128)S(1)} fusion(f32[2048]{0:T(1024)S(1)} %fusion.180, s32[2048]{0:T(1024)S(1)} %add_select_fusion.3, f32[2,256,1024]{2,1,0:T(8,128)S(1)} %fusion.328), kind=kOutput, calls=%fused_computation.29 | convolution fusion | flops 12916359168 | bytes 6307840 | tf_op jit(solution)/shard_map/dot_general | solution.py:74
  222.9 2.7 pad_maximum_fusion
  225.7 4.8 all-to-all-start.1
  230.8 23.9 %all-to-all-done.1 = f32[1,256,4,512]{1,3,0,2:T(8,128)} async-done(((f32[1,256,4,512]{1,3,0,2:T(8,128)}), f32[1,256,4,512]{1,3,0,2:T(8,128)}, u32[]{:S(2)}, u32[]{:S(2)}) %all-to-all-start.1) | async-done | bytes 2097184 | tf_op jit(solution)/shard_map/all_to_all | solution.py:162
  254.8 3.3 copy.130
  264.6 2.0 subtract_bitcast_fusion.3
  279.5 2.0 subtract_bitcast_fusion.2
  283.1 2.2 fusion.72
  290.1 26.6 %all_to_all.40 = f32[1,256,4,512]{1,3,0,2:T(8,128)} all-to-all(f32[1,256,4,512]{1,3,0,2:T(8,128)S(1)} %bitcast.272), channel_id=1, replica_groups=mesh['led'=8,'tile'=4] {'tile'}, dimensions={2} | all-to-all | bytes 4194304 | tf_op jit(solution)/shard_map/all_to_all | solution.py:173
  316.7 2.9 copy.154
  319.5 3.5 squeeze_reshape.3
  323.1 4.0 fusion.305
  332.1 1.9 add_bitcast_fusion.1
  337.2 1.8 fusion.30
  340.6 2.5 copy.166
  346.7 9.1 %add_bitcast_fusion = (f32[32,8,8,128]{3,1,2,0:T(8,128)S(1)}, f32[32,8,8,128]{3,1,2,0:T(8,128)S(1)}) fusion(f32[256,1024]{1,0:T(8,128)S(1)} %copy-done.1, f32[256,1024]{1,0:T(8,128)} %copy.162, f32[256,1024]{1,0:T(8,128)S(1)} %fusion.94, f32[]{:T(128)} %bitcast.10, f32[256]{0:T(256)S(1)} %get-tuple-element.35, f32[]{:T(128)} %bitcast.9, ...), kind=kLoop, calls=%fused_computation.90 | loop fusion | flops 6815744 | bytes 5254164
  356.9 54.2 %all_to_all.41 = f32[8,1,65536]{2,1,0:T(1,128)S(1)} all-to-all(f32[8,1,65536]{2,1,0:T(1,128)S(1)} %bitcast.271), channel_id=1, replica_groups=mesh['led'=8,'tile'=4] {'led'}, dimensions={0} | all-to-all | bytes 4194304 | tf_op jit(solution)/shard_map/all_to_all | solution.py:180
  412.7 24.7 %scatter_custom_fusion = f32[32768,256]{1,0:T(8,128)} fusion(s32[2048]{0:T(1024)S(1)} %bitcast.290, f32[]{:T(128)} %constant.178.clone.1, f32[256,8,2,128]{3,2,1,0:T(2,128)S(1)} %bitcast.268), kind=kCustom, calls=%fused_computation.8 | custom fusion | flops 524288 | bytes 35651588 | tf_op jit(solution)/shard_map/scatter-add | solution.py:184
  437.3 22.7 %broadcast_multiply_fusion = f32[32768,256]{1,0:T(8,128)} fusion(f32[32768,256]{1,0:T(8,128)} %scatter_custom_fusion), kind=kLoop, calls=%fused_computation.7 | loop fusion | flops 8388608 | bytes 67108864 | tf_op jit(solution)/shard_map/mul | solution.py:186
  460.1 40.8 %reshape.616 = f32[16,8,256,2,128]{4,3,2,1,0:T(2,128)} reshape(f32[32768,256]{1,0:T(8,128)} %broadcast_multiply_fusion) | data formatting | bytes 67108864 | tf_op jit(solution)/shard_map/mul | solution.py:186
  500.9 25.2 %copy.261 = f32[16,8,256,2,128]{4,2,3,1,0:T(8,128)} copy(f32[16,8,256,2,128]{4,3,2,1,0:T(2,128)} %reshape.616) | data formatting | bytes 67108864 | tf_op jit(solution)/shard_map/mul | solution.py:186
  526.0 28.7 %mul.874 = f32[16,8,1,1,65536]{4,1,0,3,2:T(8,128)} reshape(f32[16,8,2,256,128]{4,3,2,1,0:T(8,128)} %bitcast.253) | data formatting | bytes 67108864 | tf_op jit(solution)/shard_map/mul | solution.py:186
  554.7 41.1 %copy_subtract_fusion = f32[16,8,1,1,65536]{4,1,0,3,2:T(8,128)} fusion(f32[16,8,1,1,65536]{4,1,0,3,2:T(8,128)} %mul.874, f32[16,8,1,1,65536]{4,3,2,1,0:T(1,128)} %param.7), kind=kLoop, calls=%fused_computation.6 | loop fusion | flops 8388608 | bytes 100663296 | tf_op jit(solution)/shard_map/sub | solution.py:186
  595.7 38.1 %copy.177 = f32[16,8,1,1,65536]{4,3,2,1,0:T(1,128)} copy(f32[16,8,1,1,65536]{4,1,0,3,2:T(8,128)} %copy_subtract_fusion) | data formatting | bytes 67108864 | tf_op jit(solution)/shard_map/sub | solution.py:186
  (84 shorter events, 58.3 us)
Async XLA Ops:
  111.0 6.0 copy-start
  111.0 7.4 %copy-start.3 = (f32[5]{0:T(128)S(1)}, f32[5]{0:T(128)}, u32[]{:S(2)}) copy-start(f32[5]{0:T(128)} %param.13) | copy-start | bytes 64
  111.0 51.5 %all-to-all-start = ((f32[8,1,65536]{2,1,0:T(1,128)}), f32[8,1,65536]{2,1,0:T(1,128)}, u32[]{:S(2)}, u32[]{:S(2)}) async-start(f32[8,1,65536]{2,1,0:T(1,128)} %bitcast.16), calls=%async_computation | async-start | bytes 4194304 | tf_op jit(solution)/shard_map/all_to_all | solution.py:142
  225.7 4.8 copy-start.2
  225.7 29.1 %all-to-all-start.1 = ((f32[1,256,4,512]{1,3,0,2:T(8,128)}), f32[1,256,4,512]{1,3,0,2:T(8,128)}, u32[]{:S(2)}, u32[]{:S(2)}) async-start(f32[1,256,4,512]{1,3,0,2:T(8,128)} %bitcast.269), calls=%async_computation.1 | async-start | bytes 4194304 | tf_op jit(solution)/shard_map/all_to_all | solution.py:162
  344.7 1.9 copy-start.1
where the time goes:
time: 644 us; the launch traced here: 634 us
  local copies, waits for them, and re-layouts  274 us (43%)
  other arithmetic  112 us (17%)
  matrix products  86.8 us (13%)
  blocking collectives  80.8 us (13%)
  waiting for transfers between devices  65.8 us (10%)
  starting transfers between devices  10.8 us (2%)
    mul x3, local copies, waits for them, and re-layouts, shards(): updated = spectrum - STEP_SIZE * grad_sum.reshape(spectrum.shape)  94.6 us
    reshape x1, local copies, waits for them, and re-layouts, shards(): spectrum.reshape(GR, GC, 2, band_rows, unit_cols)  54.9 us
    all_to_all x1, blocking collectives, shards(): lax.all_to_all(outgoing_all, 'led', split_axis=0, concat_axis=0, tiled=True)  54.2 us
    dot_general x3, matrix products, times_table(): jnp.dot(operand, transform, precision=HIGHEST_MODE, preferred_element_typ...  46.5 us
    all_to_all x1, waiting for transfers between devices, shards(): lax.all_to_all(outgoing, 'led', split_axis=0, concat_axis=0, tiled=True)  41.8 us
    sub x1, other arithmetic, shards(): updated = spectrum - STEP_SIZE * grad_sum.reshape(spectrum.shape)  41.1 us
    sub x1, local copies, waits for them, and re-layouts, shards(): updated = spectrum - STEP_SIZE * grad_sum.reshape(spectrum.shape)  38.1 us
    all_to_all x1, blocking collectives, shards(): lax.all_to_all(inbound, 'tile', split_axis=2, concat_axis=1, tiled=True)  26.6 us
  transfers between devices with their start and end apart: 2, of which 2 were waited for; matrix products, arithmetic and copies ran while one was open for 1% of the time, Pallas kernels for 0%

commit v1 on v0

--- a/solution.py
+++ b/solution.py
@@ -1,8 +1,12 @@
+import functools
 import math
 
 import jax
 import jax.numpy as jnp
+import numpy as np
 from jax import lax
+from jax.experimental import pallas as pl
+from jax.experimental.pallas import tpu as pltpu
 from jax.sharding import PartitionSpec as P
 
 M = 1024
@@ -113,7 +117,7 @@
     return jnp.transpose(stacked, (2, 0, 1, 3)).reshape(led_count, 2 * row_count * unit_cols)
 
 
-def shards(spectrum, intensities, led_of_slot, row_offset, col_offset, tile_mask, aberration):
+def general_shards(spectrum, intensities, led_of_slot, row_offset, col_offset, tile_mask, aberration):
     tile_count = lax.axis_size("tile")
     led_count = lax.axis_size("led")
     band_rows = M // tile_count
@@ -187,10 +191,510 @@
     return updated
 
 
+QUARTER = M // 4
+HALF_LANES = 64
+LANES = 128
+SUB = 128
+CHUNKS = 2
+ANY = pl.ANY
+F32 = jnp.float32
+BF16 = jnp.bfloat16
+
+
+def split_table(values):
+    high = values.astype(np.float32).astype(jnp.bfloat16)
+    low = (values - high.astype(np.float64)).astype(np.float32).astype(jnp.bfloat16)
+    return high, low
+
+
+def quarter_tables():
+    grid_b = np.arange(QUARTER)[:, None]
+    grid_k = np.arange(QUARTER)[None, :]
+    swapped = grid_k ^ HALF_LANES
+    row_fwd, row_bwd, col_fwd, col_bwd = [], [], [], []
+    for step in range(4):
+        lanes = swapped if step % 2 else grid_k
+        angle = 2.0 * math.pi * (grid_b * (step + 4 * lanes) % M) / M
+        cos, sin = np.cos(angle) / 32.0, np.sin(angle) / 32.0
+        for stacked, out in (
+            (np.concatenate([cos, sin], 0), row_fwd),
+            (np.concatenate([cos.T, -sin.T], 0), row_bwd),
+        ):
+            high, low = split_table(stacked)
+            out.append(np.concatenate([high, high, low], 0))
+        angle = 2.0 * math.pi * (grid_b * (step + 4 * grid_k) % M) / M
+        cos, sin = np.cos(angle) / 32.0, np.sin(angle) / 32.0
+        for stacked, out in (
+            (np.concatenate([cos.T, sin.T], 1), col_fwd),
+            (np.concatenate([cos, -sin], 1), col_bwd),
+        ):
+            high, low = split_table(stacked)
+            out.append(np.concatenate([high, high, low], 1))
+    return [np.stack(t) for t in (row_fwd, row_bwd, col_fwd, col_bwd)]
+
+
+def halves(x):
+    high = x.astype(BF16)
+    low = (x - high.astype(F32)).astype(BF16)
+    return high, low
+
+
+def right_product(re, im, table):
+    re_high, re_low = halves(re)
+    im_high, im_low = halves(im)
+    top = jnp.concatenate([re_high, -im_high, re_low, -im_low, re_high, -im_high], axis=1)
+    bottom = jnp.concatenate([im_high, re_high, im_low, re_low, im_high, re_high], axis=1)
+    return (
+        jnp.dot(top, table, preferred_element_type=F32),
+        jnp.dot(bottom, table, preferred_element_type=F32),
+    )
+
+
+def left_product(re, im, table):
+    re_high, re_low = halves(re)
+    im_high, im_low = halves(im)
+    left = jnp.concatenate([re_high, -im_high, re_low, -im_low, re_high, -im_high], axis=0)
+    right = jnp.concatenate([im_high, re_high, im_low, re_low, im_high, re_high], axis=0)
+    return (
+        jnp.dot(table, left, preferred_element_type=F32),
+        jnp.dot(table, right, preferred_element_type=F32),
+    )
+
+
+def butterfly(parts, sign):
+    (r0, i0), (r1, i1), (r2, i2), (r3, i3) = parts
+    sr, si, dr, di = r0 + r2, i0 + i2, r0 - r2, i0 - i2
+    tr, ti, er, ei = r1 + r3, i1 + i3, r1 - r3, i1 - i3
+    if sign > 0:
+        return ((sr + tr, si + ti), (dr - ei, di + er), (sr - tr, si - ti), (dr + ei, di - er))
+    return ((sr + tr, si + ti), (dr + ei, di - er), (sr - tr, si - ti), (dr - ei, di + er))
+
+
+def cos_sin(angle):
+    turns = jnp.floor(angle * (2.0 / math.pi) + 0.5)
+    rest = ((angle - turns * 1.5703125) - turns * 4.837512969970703125e-4) - turns * 7.549789948768648e-8
+    square = rest * rest
+    sine = rest + rest * square * (
+        -1.6666654611e-1 + square * (8.3321608736e-3 - square * 1.9515295891e-4)
+    )
+    cosine = 1.0 - 0.5 * square + square * square * (
+        4.166664568298827e-2 + square * (-1.388731625493765e-3 + square * 2.443315711809948e-5)
+    )
+    quarter = turns.astype(jnp.int32) & 3
+    odd = (quarter & 1) == 1
+    cos_out = jnp.where(odd, sine, cosine)
+    sin_out = jnp.where(odd, cosine, sine)
+    cos_out = jnp.where((quarter == 1) | (quarter == 2), -cos_out, cos_out)
+    sin_out = jnp.where(quarter >= 2, -sin_out, sin_out)
+    return cos_out, sin_out
+
+
+def piece_row(slot, row_first, col_first, band, lead, row_off, col_off):
+    led = lead[slot]
+    row_start = row_off[led] * TILE
+    col_start = col_off[led] * TILE
+    row_group = (row_start + ((row_first - row_start) & (M - 1))) // M
+    col_group = (col_start + ((col_first - col_start) & (M - 1))) // M
+    return (row_group * GC + col_group) * (2 * band)
+
+
+def start_all(copies):
+    for copy in copies:
+        copy.start()
+
+
+def wait_all(copies):
+    for copy in copies:
+        copy.wait()
+
+
+def gather_kernel(sizes, chunk, lead, row_off, col_off, spectrum, *refs):
+    leds, tiles, band, rows = sizes
+    outs, sems = refs[:-1], refs[-1]
+    me, tile = lax.axis_index("led"), lax.axis_index("tile")
+    copies = []
+    for shift in range(leds):
+        slot = lax.rem(me + shift, leds)
+        base = piece_row(slot, tile * band + chunk * rows, me * LANES, band, lead, row_off, col_off)
+        for part in range(2):
+            first = pl.multiple_of(base + part * band + chunk * rows, 8)
+            copies.append(
+                pltpu.make_async_copy(
+                    spectrum.at[pl.ds(first, rows)], outs[shift].at[part], sems.at[shift, part]
+                )
+            )
+    start_all(copies)
+    wait_all(copies)
+
+
+def prepare_kernel(sizes, lead, row_off, col_off, mask, aberration, intensities, pupil, images, turned):
+    leds, tiles, band, rows = sizes
+    me, tile = lax.axis_index("led"), lax.axis_index("tile")
+    led = lead[me]
+    line = lax.broadcasted_iota(jnp.int32, (band, band), 0)
+    place = lax.broadcasted_iota(jnp.int32, (band, band), 1)
+    residue = 2 * (place // LANES) + (((place // HALF_LANES) & 1) ^ (tile & 1))
+    wanted = residue + 4 * (place & (HALF_LANES - 1))
+    chosen = (line == wanted).astype(BF16)
+    for block in range(M // QUARTER):
+        columns = lax.dot_general(
+            intensities[:, block * QUARTER : (block + 1) * QUARTER],
+            chosen,
+            (((0,), (0,)), ((), ())),
+            preferred_element_type=F32,
+        )
+        for side in range(band // LANES):
+            turned[side, block * QUARTER : (block + 1) * QUARTER, :] = columns[
+                :, side * LANES : (side + 1) * LANES
+            ]
+    for part in range(4):
+        for side in range(band // LANES):
+            images[part * QUARTER : (part + 1) * QUARTER, side * LANES : (side + 1) * LANES] = turned[
+                side, pl.ds(part, QUARTER, 4), :
+            ]
+    half = M // 2
+    run_p = lax.broadcasted_iota(jnp.int32, (TILE, TILE), 0)
+    run_q = lax.broadcasted_iota(jnp.int32, (TILE, TILE), 1)
+    tile_rows = band // TILE
+    for i in range(tile_rows):
+        row_tile = (tile * tile_rows + i - row_off[led]) & (M // TILE - 1)
+        coord_p = (run_p + (row_tile * TILE - half)).astype(F32) / half
+        for j in range(M // TILE):
+            col_tile = (j - col_off[led]) & (M // TILE - 1)
+            coord_q = (run_q + (col_tile * TILE - half)).astype(F32) / half
+            gate = mask[led, row_tile, col_tile].astype(F32)
+            cosine, sine = cos_sin(aberration_phase(aberration, coord_p, coord_q))
+            where = (slice(i * TILE, (i + 1) * TILE), slice(j * TILE, (j + 1) * TILE))
+            pupil[(0,) + where] = gate * cosine
+            pupil[(1,) + where] = gate * sine
+
+
+def forward_kernel(sizes, chunk, table, pupil, *refs):
+    leds, tiles, band, rows = sizes
+    pieces, refs = refs[:leds], refs[leds:]
+    outs, refs = refs[:tiles], refs[tiles:]
+    table_v, pupil_v, window, result, sems, sems_out = refs
+    me, tile = lax.axis_index("led"), lax.axis_index("tile")
+    copies = []
+    for shift in range(leds):
+        first = pl.multiple_of(lax.rem(me - shift + leds, leds) * LANES, LANES)
+        copies.append(
+            pltpu.make_async_copy(pieces[shift], window.at[:, :, pl.ds(first, LANES)], sems.at[shift])
+        )
+    copies.append(
+        pltpu.make_async_copy(pupil.at[:, chunk * rows : (chunk + 1) * rows], pupil_v, sems.at[leds])
+    )
+    copies.append(pltpu.make_async_copy(table, table_v, sems.at[leds + 1]))
+    start_all(copies)
+    wait_all(copies)
+    parts = []
+    for a in range(4):
+        cells = slice(a * QUARTER, (a + 1) * QUARTER)
+        gate_re, gate_im = pupil_v[0, :, cells], pupil_v[1, :, cells]
+        cell_re, cell_im = window[0, :, cells], window[1, :, cells]
+        parts.append((gate_re * cell_re - gate_im * cell_im, gate_re * cell_im + gate_im * cell_re))
+    mixed = butterfly(parts, 1)
+    lines = [right_product(re, im, table_v[k]) for k, (re, im) in enumerate(mixed)]
+    lane = lax.broadcasted_iota(jnp.int32, (rows, LANES), 1)
+    for other in range(tiles):
+        block = slice((other // 2) * LANES, (other // 2 + 1) * LANES)
+        for part in range(2):
+            for pair in range(2):
+                first, second = lines[2 * pair][part][:, block], lines[2 * pair + 1][part][:, block]
+                if other % 2:
+                    first, second = second, first
+                result[other, part, :, pair * LANES : (pair + 1) * LANES] = jnp.where(
+                    lane < HALF_LANES, first, second
+                )
+    copies = [
+        pltpu.make_async_copy(result.at[tile ^ shift], outs[shift], sems_out.at[shift])
+        for shift in range(tiles)
+    ]
+    start_all(copies)
+    wait_all(copies)
+
+
+def middle_kernel(sizes, table, table_back, images, *refs):
+    leds, tiles, band, rows = sizes
+    chunks = band // rows
+    blocks, refs = refs[: chunks * tiles], refs[chunks * tiles :]
+    outs, refs = refs[: chunks * tiles], refs[chunks * tiles :]
+    table_v, back_v, images_v, field, residual, sems, sems_out = refs
+    tile = lax.axis_index("tile")
+    copies = []
+    for chunk in range(chunks):
+        for shift in range(tiles):
+            where = chunk * tiles + shift
+            copies.append(
+                pltpu.make_async_copy(
+                    blocks[where],
+                    field.at[tile ^ shift, :, chunk * rows : (chunk + 1) * rows],
+                    sems.at[where],
+                )
+            )
+    count = chunks * tiles
+    copies.append(pltpu.make_async_copy(table, table_v, sems.at[count]))
+    copies.append(pltpu.make_async_copy(images, images_v, sems.at[count + 1]))
+    copies.append(pltpu.make_async_copy(table_back, back_v, sems.at[count + 2]))
+    start_all(copies)
+    wait_all(copies)
+    mixed = butterfly([(field[a, 0], field[a, 1]) for a in range(4)], 1)
+    for k, (re, im) in enumerate(mixed):
+        wave_re, wave_im = left_product(re, im, table_v[k])
+        measured = images_v[k * QUARTER : (k + 1) * QUARTER, :]
+        excess = wave_re * wave_re + wave_im * wave_im - measured
+        back_re, back_im = left_product(excess * wave_re, excess * wave_im, back_v[k])
+        residual[k, 0] = back_re
+        residual[k, 1] = back_im
+    mixed = butterfly([(residual[k, 0], residual[k, 1]) for k in range(4)], -1)
+    for a, (re, im) in enumerate(mixed):
+        field[a, 0] = re
+        field[a, 1] = im
+    copies = []
+    for chunk in range(chunks):
+        for shift in range(tiles):
+            where = chunk * tiles + shift
+            copies.append(
+                pltpu.make_async_copy(
+                    field.at[tile ^ shift, :, chunk * rows : (chunk + 1) * rows],
+                    outs[where],
+                    sems_out.at[where],
+                )
+            )
+    start_all(copies)
+    wait_all(copies)
+
+
+def backward_kernel(sizes, chunk, table, pupil, *refs):
+    leds, tiles, band, rows = sizes
+    blocks, refs = refs[:tiles], refs[tiles:]
+    outs, refs = refs[:leds], refs[leds:]
+    table_v, pupil_v, lines, result, sems, sems_out = refs
+    me, tile = lax.axis_index("led"), lax.axis_index("tile")
+    copies = [
+        pltpu.make_async_copy(blocks[shift], lines.at[tile ^ shift], sems.at[shift])
+        for shift in range(tiles)
+    ]
+    copies.append(
+        pltpu.make_async_copy(pupil.at[:, chunk * rows : (chunk + 1) * rows], pupil_v, sems.at[tiles])
+    )
+    copies.append(pltpu.make_async_copy(table, table_v, sems.at[tiles + 1]))
+    start_all(copies)
+    wait_all(copies)
+    lane = lax.broadcasted_iota(jnp.int32, (rows, LANES), 1)
+    parts = []
+    for k in range(4):
+        cells = slice((k // 2) * LANES, (k // 2 + 1) * LANES)
+        both = []
+        for part in range(2):
+            joined = []
+            for pair in range(tiles // 2):
+                first, second = lines[2 * pair, part, :, cells], lines[2 * pair + 1, part, :, cells]
+                if k % 2:
+                    first, second = second, first
+                joined.append(jnp.where(lane < HALF_LANES, first, second))
+            both.append(jnp.concatenate(joined, axis=1))
+        parts.append(right_product(both[0], both[1], table_v[k]))
+    for a, (re, im) in enumerate(butterfly(parts, -1)):
+        cells = slice(a * QUARTER, (a + 1) * QUARTER)
+        gate_re, gate_im = pupil_v[0, :, cells], pupil_v[1, :, cells]
+        result[0, :, cells] = gate_re * re + gate_im * im
+        result[1, :, cells] = gate_re * im - gate_im * re
+    copies = []
+    for shift in range(leds):
+        first = pl.multiple_of(lax.rem(me + shift, leds) * LANES, LANES)
+        copies.append(
+            pltpu.make_async_copy(
+                result.at[:, :, pl.ds(first, LANES)], outs[shift], sems_out.at[shift]
+            )
+        )
+    start_all(copies)
+    wait_all(copies)
+
+
+def update_kernel(sizes, chunk, lead, row_off, col_off, spectrum, buffer, *refs):
+    leds, tiles, band, rows = sizes
+    pieces, refs = refs[:leds], refs[leds:]
+    updated, grads, cells, sems, sems_in, sems_out = refs
+    me, tile = lax.axis_index("led"), lax.axis_index("tile")
+    bases = [
+        piece_row(slot, tile * band + chunk * rows, me * LANES, band, lead, row_off, col_off)
+        for slot in range(leds)
+    ]
+    copies = []
+    for shift in range(leds):
+        slot = lax.rem(me - shift + leds, leds)
+        copies.append(pltpu.make_async_copy(pieces[shift], grads.at[slot], sems.at[shift]))
+    for slot in range(leds):
+        for part in range(2):
+            first = pl.multiple_of(bases[slot] + part * band + chunk * rows, 8)
+            copies.append(
+                pltpu.make_async_copy(
+                    spectrum.at[pl.ds(first, rows)], cells.at[slot, part], sems_in.at[slot, part]
+                )
+            )
+    start_all(copies)
+    wait_all(copies)
+    firsts = []
+    for slot in range(leds):
+        is_first = jnp.bool_(True)
+        for earlier in range(slot):
+            is_first = jnp.logical_and(is_first, bases[earlier] != bases[slot])
+        firsts.append(is_first)
+        for later in range(slot + 1, leds):
+
+            @pl.when(jnp.logical_and(is_first, bases[later] == bases[slot]))
+            def _():
+                grads[slot] = grads[slot] + grads[later]
+
+        cells[slot] = cells[slot] - STEP_SIZE * grads[slot]
+    for waiting in (False, True):
+        for slot in range(leds):
+
+            @pl.when(firsts[slot])
+            def _():
+                for part in range(2):
+                    first = pl.multiple_of(bases[slot] + part * band + chunk * rows, 8)
+                    copy = pltpu.make_async_copy(
+                        cells.at[slot, part], updated.at[pl.ds(first, rows)], sems_out.at[slot, part]
+                    )
+                    if waiting:
+                        copy.wait()
+                    else:
+                        copy.start()
+
+
+COPY_PARTS = 16
+
+
+def copy_kernel(spectrum, copied, sems):
+    lines = spectrum.shape[0] // COPY_PARTS
+    copies = [
+        pltpu.make_async_copy(
+            spectrum.at[pl.ds(n * lines, lines)], copied.at[pl.ds(n * lines, lines)], sems.at[n]
+        )
+        for n in range(COPY_PARTS)
+    ]
+    start_all(copies)
+    wait_all(copies)
+
+
+def call(kernel, name, ins, outs, scratch, flops=0, moved=0, aliases=None, vmem=16):
+    return pl.pallas_call(
+        kernel,
+        name=name,
+        out_shape=outs,
+        in_specs=[pl.BlockSpec(memory_space=place) for place in ins],
+        out_specs=jax.tree.map(lambda _: pl.BlockSpec(memory_space=ANY), outs),
+        scratch_shapes=scratch,
+        input_output_aliases=aliases or {},
+        cost_estimate=pl.CostEstimate(flops=flops, bytes_accessed=moved, transcendentals=0),
+        compiler_params=pltpu.CompilerParams(vmem_limit_bytes=vmem * 2**20),
+    )
+
+
+def unit_shards(spectrum, intensities, led_of_slot, row_offset, col_offset, tile_mask, aberration):
+    tiles = lax.axis_size("tile")
+    leds = lax.axis_size("led")
+    band = M // tiles
+    rows = band // CHUNKS
+    sizes = (leds, tiles, band, rows)
+    row_fwd, row_bwd, col_fwd, col_bwd = (jnp.asarray(t) for t in quarter_tables())
+    flat = spectrum.reshape(-1, LANES)
+    smem, vmem = pltpu.SMEM, pltpu.VMEM
+    dma = pltpu.SemaphoreType.DMA
+    f32 = lambda *shape: jax.ShapeDtypeStruct(shape, F32)
+    part = functools.partial
+
+    def over_led(arrays):
+        moved = [arrays[0]]
+        for shift in range(1, leds):
+            moved.append(
+                lax.ppermute(arrays[shift], "led", [(i, (i + shift) % leds) for i in range(leds)])
+            )
+        return moved
+
+    def over_tile(arrays):
+        moved = [arrays[0]]
+        for shift in range(1, tiles):
+            moved.append(lax.ppermute(arrays[shift], "tile", [(i, i ^ shift) for i in range(tiles)]))
+        return moved
+
+    piece = f32(2, rows, LANES)
+    taken = [
+        call(
+            part(gather_kernel, sizes, chunk), f"gather_{chunk}", [smem] * 3 + [ANY], [piece] * leds,
+            [dma((leds, 2))], moved=4 * leds * piece.size * 2,
+        )(led_of_slot, row_offset, col_offset, flat)
+        for chunk in range(CHUNKS)
+    ]
+    arrived = [over_led(arrays) for arrays in taken]
+    pupil, images = pl.pallas_call(
+        part(prepare_kernel, sizes),
+        name="prepare",
+        out_shape=[f32(2, band, M), f32(M, band)],
+        in_specs=[pl.BlockSpec(memory_space=smem)] * 5 + [pl.BlockSpec(memory_space=vmem)],
+        out_specs=[pl.BlockSpec(memory_space=vmem)] * 2,
+        scratch_shapes=[pltpu.VMEM((band // LANES, M, LANES), F32)],
+        compiler_params=pltpu.CompilerParams(vmem_limit_bytes=24 * 2**20),
+        cost_estimate=pl.CostEstimate(flops=2 * 10**9, bytes_accessed=4 * 10**6, transcendentals=0),
+    )(led_of_slot, row_offset, col_offset, tile_mask, aberration, intensities[0])
+    copied = call(
+        copy_kernel, "copy_spectrum", [ANY], f32(*flat.shape), [dma((COPY_PARTS,))], moved=8 * flat.size
+    )(flat)
+    block = f32(2, rows, band)
+    table_shape = (4, 6 * QUARTER, QUARTER)
+    received = []
+    for chunk in range(CHUNKS):
+        lines = call(
+            part(forward_kernel, sizes, chunk), f"forward_{chunk}", [ANY] * (2 + leds), [block] * tiles,
+            [
+                pltpu.VMEM(table_shape, BF16), pltpu.VMEM((2, rows, M), F32),
+                pltpu.VMEM((2, rows, M), F32), pltpu.VMEM((tiles, 2, rows, band), F32),
+                dma((leds + 2,)), dma((tiles,)),
+            ],
+            flops=24 * rows * M * QUARTER, moved=2**23, vmem=40,
+        )(row_fwd, pupil, *arrived[chunk])
+        received += over_tile(lines)
+    count = CHUNKS * tiles
+    returned = call(
+        part(middle_kernel, sizes), "middle", [ANY] * (3 + count), [block] * count,
+        [
+            pltpu.VMEM((4, QUARTER, 6 * QUARTER), BF16), pltpu.VMEM((4, QUARTER, 6 * QUARTER), BF16),
+            pltpu.VMEM((M, band), F32), pltpu.VMEM((4, 2, QUARTER, band), F32),
+            pltpu.VMEM((4, 2, QUARTER, band), F32), dma((count + 3,)), dma((count,)),
+        ],
+        flops=48 * band * M * QUARTER, moved=2**24, vmem=48,
+    )(col_fwd, col_bwd, images, *received)
+    updated = copied
+    for chunk in range(CHUNKS):
+        lines = over_tile(returned[chunk * tiles : (chunk + 1) * tiles])
+        pieces = call(
+            part(backward_kernel, sizes, chunk), f"backward_{chunk}", [ANY] * (2 + tiles), [piece] * leds,
+            [
+                pltpu.VMEM(table_shape, BF16), pltpu.VMEM((2, rows, M), F32),
+                pltpu.VMEM((tiles, 2, rows, band), F32), pltpu.VMEM((2, rows, M), F32),
+                dma((tiles + 2,)), dma((leds,)),
+            ],
+            flops=24 * rows * M * QUARTER, moved=2**23, vmem=40,
+        )(row_bwd, pupil, *lines)
+        updated = call(
+            part(update_kernel, sizes, chunk), f"update_{chunk}", [smem] * 3 + [ANY] * (2 + leds),
+            f32(*flat.shape),
+            [
+                pltpu.VMEM((leds, 2, rows, LANES), F32), pltpu.VMEM((leds, 2, rows, LANES), F32),
+                dma((leds,)), dma((leds, 2)), dma((leds, 2)),
+            ],
+            moved=2**22, aliases={4: 0},
+        )(led_of_slot, row_offset, col_offset, flat, updated, *over_led(pieces))
+    return updated.reshape(spectrum.shape)
+
+
 def solution(mesh):
     placed = (P(None, None, "tile", "led", None), P("led", "tile", None), P(), P(), P(), P(), P())
+    whole_units = mesh.shape["tile"] == 4 and M // mesh.shape["led"] == LANES
     return jax.shard_map(
-        shards,
+        unit_shards if whole_units else general_shards,
         mesh=mesh,
         in_specs=placed,
         out_specs=P(None, None, "tile", "led", None),

time: 644 us -> 189 us (0.29); the launches traced: 634 us -> 186 us
  local copies, waits for them, and re-layouts: 274 us -> 23.1 us
  other arithmetic: 112 us -> 0 us
  matrix products: 86.8 us -> 0 us
  blocking collectives: 80.8 us -> 0 us
  starting transfers between devices: 10.8 us -> 58.2 us
  Pallas kernels: 0 us -> 44.8 us
  waiting for transfers between devices: 65.8 us -> 59.1 us
    mul x3 -> x0, local copies, waits for them, and re-layouts: 94.6 us -> none  [shards(): updated = spectrum - STEP_SIZE * grad_sum.reshape(spectrum.shape)]
    dot_general x27 -> x0, matrix products: 86.8 us -> none  [the longest x3 46.5 us: times_table(): jnp.dot(operand, transform, precision=HIGHEST_MODE, preferred_element_typ...]
    all_to_all x2 -> x0, blocking collectives: 80.8 us -> none  [the longest x1 54.2 us: shards(): lax.all_to_all(outgoing_all, 'led', split_axis=0, concat_axis=0, tiled=True)]
    all_to_all x2 -> x0, waiting for transfers between devices: 65.8 us -> none  [the longest x1 41.8 us: shards(): lax.all_to_all(outgoing, 'led', split_axis=0, concat_axis=0, tiled=True)]
    reshape x4 -> x0, local copies, waits for them, and re-layouts: 61.7 us -> none  [the longest x1 54.9 us: shards(): spectrum.reshape(GR, GC, 2, band_rows, unit_cols)]
    ppermute x0 -> x40, waiting for transfers between devices: none -> 59.1 us  [the longest x28 36.2 us: over_led(): lax.ppermute(arrays[shift], 'led', [(i, (i + shift) % leds) for i in rang...]
    ppermute x0 -> x40, starting transfers between devices: none -> 58.2 us  [the longest x28 45.4 us: over_led(): lax.ppermute(arrays[shift], 'led', [(i, (i + shift) % leds) for i in rang...]
    pallas_call x0 -> x11, Pallas kernels: none -> 44.8 us  [the longest x1 11 us: unit_shards(): call(copy_kernel, 'copy_spectrum', [ANY], f32(*flat.shape), [dma((COPY_PA...]
  transfers between devices with their start and end apart: 2 -> 40, of which waited for: 2 -> 11; matrix products, arithmetic and copies ran while one was open for 1% -> 0% of each run, Pallas kernels for 0% -> 16%
where the time goes in v1:
time: 189 us; the launch traced here: 186 us
  waiting for transfers between devices  59.1 us (31%)
  starting transfers between devices  58.2 us (31%)
  Pallas kernels  44.8 us (24%)
  local copies, waits for them, and re-layouts  23.1 us (12%)
    ppermute x28, starting transfers between devices, over_led(): lax.ppermute(arrays[shift], 'led', [(i, (i + shift) % leds) for i in rang...  45.4 us
    ppermute x28, waiting for transfers between devices, over_led(): lax.ppermute(arrays[shift], 'led', [(i, (i + shift) % leds) for i in rang...  36.2 us
    unnamed x26, local copies, waits for them, and re-layouts  23.1 us
    ppermute x12, waiting for transfers between devices, over_tile(): lax.ppermute(arrays[shift], 'tile', [(i, i ^ shift) for i in range(tiles)])  23 us
    ppermute x12, starting transfers between devices, over_tile(): lax.ppermute(arrays[shift], 'tile', [(i, i ^ shift) for i in range(tiles)])  12.8 us
    pallas_call x1, Pallas kernels, unit_shards(): call(copy_kernel, 'copy_spectrum', [ANY], f32(*flat.shape), [dma((COPY_PA...  11 us
    pallas_call x2, Pallas kernels, unit_shards(): call(part(update_kernel, sizes, chunk), f'update_{chunk}', [smem] * 3 + [...  10.3 us
    pallas_call x1, Pallas kernels, unit_shards(): call(part(middle_kernel, sizes), 'middle', [ANY] * (3 + count), [block] *...  7.79 us
  transfers between devices with their start and end apart: 40, of which 11 were waited for; matrix products, arithmetic and copies ran while one was open for 0% of the time, Pallas kernels for 16%

profile of v1, /device:TPU:11, one launch (start us, length us, event | category | flops | bytes accessed | tf_op | source)
XLA Modules:
  0.0 185.7 jit_solution(17706605073294381430)
XLA Ops:
  0.0 10.5 %copy-done = f32[16,8,1,1,65536]{4,3,2,1,0:T(1,128)S(1)} copy-done((f32[16,8,1,1,65536]{4,3,2,1,0:T(1,128)S(1)}, f32[16,8,1,1,65536]{4,3,2,1,0:T(1,128)}, u32[]{:S(2)}) %copy-start) | copy-done | bytes 33554456
  12.5 2.4 %gather_0.1 = (f32[2,128,128]{2,1,0:T(8,128)S(1)}, f32[2,128,128]{2,1,0:T(8,128)S(1)}, f32[2,128,128]{2,1,0:T(8,128)S(1)}, f32[2,128,128]{2,1,0:T(8,128)S(1)}, f...) custom-call(s32[8]{0:T(128)S(1)} %copy-done.4, ...), custom_call_target="tpu_custom_call" | custom-call | bytes 2097152 | tf_op jit(solution)/shard_map/gather_0/pallas_call | solution.py:625
  14.9 1.9 %collective-permute-start = (f32[2,128,128]{2,1,0:T(8,128)S(1)}, f32[2,128,128]{2,1,0:T(8,128)S(1)}, u32[]{:S(2)}, u32[]{:S(2)}) collective-permute-start(f32[2,128,128]{2,1,0:T(8,128)S(1)} %get-tuple-element.58), channel_id=1, source_target_pairs={{0,4},{4,8},{8,12},{12,16},{16,20},{20,24},{24,28},{28,0},{1,5},{5... | collective-permute-start | bytes 393224 | tf_op jit(solution)/shard_map/ppermute | solution.py:613
  19.6 1.6 collective-permute-start.4
  21.2 2.4 %gather_1.1 = (f32[2,128,128]{2,1,0:T(8,128)S(1)}, f32[2,128,128]{2,1,0:T(8,128)S(1)}, f32[2,128,128]{2,1,0:T(8,128)S(1)}, f32[2,128,128]{2,1,0:T(8,128)S(1)}, f...) custom-call(s32[8]{0:T(128)S(1)} %copy-done.4, ...), custom_call_target="tpu_custom_call" | custom-call | bytes 2097152 | tf_op jit(solution)/shard_map/gather_1/pallas_call | solution.py:625
  25.1 7.1 %collective-permute-done.2.refs_3_ = f32[2,128,128]{2,1,0:T(8,128)S(1)} collective-permute-done((f32[2,128,128]{2,1,0:T(8,128)S(1)}, f32[2,128,128]{2,1,0:T(8,128)S(1)}, u32[]{:S(2)}, u32[]{:S(2)}) %collective-permute-start.2) | collective-permute-done | bytes 131104 | tf_op jit(solution)/shard_map/ppermute | solution.py:613
  32.2 3.4 %collective-permute-start.12 = (f32[2,128,128]{2,1,0:T(8,128)S(1)}, f32[2,128,128]{2,1,0:T(8,128)S(1)}, u32[]{:S(2)}, u32[]{:S(2)}) collective-permute-start(f32[2,128,128]{2,1,0:T(8,128)S(1)} %get-tuple-element.72), channel_id=1, source_target_pairs={{0,12},{4,16},{8,20},{12,24},{16,28},{20,0},{24,4},{28,8},{1,13},{... | collective-permute-start | bytes 393224 | tf_op jit(solution)/shard_map/ppermute | solution.py:613
  36.3 7.4 %collective-permute-start.5 = (f32[2,128,128]{2,1,0:T(8,128)S(1)}, f32[2,128,128]{2,1,0:T(8,128)S(1)}, u32[]{:S(2)}, u32[]{:S(2)}) collective-permute-start(f32[2,128,128]{2,1,0:T(8,128)S(1)} %get-tuple-element.63), channel_id=1, source_target_pairs={{0,24},{4,28},{8,0},{12,4},{16,8},{20,12},{24,16},{28,20},{1,25},{... | collective-permute-start | bytes 393224 | tf_op jit(solution)/shard_map/ppermute | solution.py:613
  43.7 2.3 %collective-permute-start.6 = (f32[2,128,128]{2,1,0:T(8,128)S(1)}, f32[2,128,128]{2,1,0:T(8,128)S(1)}, u32[]{:S(2)}, u32[]{:S(2)}) collective-permute-start(f32[2,128,128]{2,1,0:T(8,128)S(1)} %get-tuple-element.64), channel_id=1, source_target_pairs={{0,28},{4,0},{8,4},{12,8},{16,12},{20,16},{24,20},{28,24},{1,29},{... | collective-permute-start | bytes 393224 | tf_op jit(solution)/shard_map/ppermute | solution.py:613
  46.1 3.6 %prepare.1 = (f32[2,256,1024]{2,1,0:T(8,128)S(1)}, f32[1024,256]{1,0:T(8,128)S(1)}) custom-call(s32[8]{0:T(128)S(1)} %copy-done.5, s32[8]{0:T(128)S(1)} %copy-done.7, s32[8]{0:T(128)S(1)} %copy-done.9, s32[8,8,8]{2,1,0:T(8,128)S(1)} %copy-done.11, f32[5]{0:T(128)S(1)} %copy-done.12, bf16[256,1024]{1,0:T(8,128)(2,1)S(1)} %bitcast.8), custom_call_target="tpu_custom_call" | custom-call | flops 2000000000 | bytes 4000000 | tf_op jit(solution)/shard_map/prepare/pallas_call | solution.py:632
  49.7 1.9 forward_0.1
  52.9 2.6 %collective-permute-start.15 = (f32[2,128,128]{2,1,0:T(8,128)S(1)}, f32[2,128,128]{2,1,0:T(8,128)S(1)}, u32[]{:S(2)}, u32[]{:S(2)}) collective-permute-start(f32[2,128,128]{2,1,0:T(8,128)S(1)} %get-tuple-element.75), channel_id=1, source_target_pairs={{0,24},{4,28},{8,0},{12,4},{16,8},{20,12},{24,16},{28,20},{1,25},{... | collective-permute-start | bytes 393224 | tf_op jit(solution)/shard_map/ppermute | solution.py:613
  55.5 9.9 %collective-permute-done.13.refs_4_ = f32[2,128,128]{2,1,0:T(8,128)S(1)} collective-permute-done((f32[2,128,128]{2,1,0:T(8,128)S(1)}, f32[2,128,128]{2,1,0:T(8,128)S(1)}, u32[]{:S(2)}, u32[]{:S(2)}) %collective-permute-start.13) | collective-permute-done | bytes 131104 | tf_op jit(solution)/shard_map/ppermute | solution.py:613
  67.9 1.8 forward_1.1
  72.6 5.9 %collective-permute-done.8.refs_2_ = f32[2,128,256]{2,1,0:T(8,128)S(1)} collective-permute-done((f32[2,128,256]{2,1,0:T(8,128)S(1)}, f32[2,128,256]{2,1,0:T(8,128)S(1)}, u32[]{:S(2)}, u32[]{:S(2)}) %collective-permute-start.8) | collective-permute-done | bytes 262176 | tf_op jit(solution)/shard_map/ppermute | solution.py:620
  78.4 11.2 %collective-permute-done.18.refs_6_ = f32[2,128,256]{2,1,0:T(8,128)S(1)} collective-permute-done((f32[2,128,256]{2,1,0:T(8,128)S(1)}, f32[2,128,256]{2,1,0:T(8,128)S(1)}, u32[]{:S(2)}, u32[]{:S(2)}) %collective-permute-start.18) | collective-permute-done | bytes 262176 | tf_op jit(solution)/shard_map/ppermute | solution.py:620
  89.7 7.8 %middle.1 = (f32[2,128,256]{2,1,0:T(8,128)S(1)}, f32[2,128,256]{2,1,0:T(8,128)S(1)}, f32[2,128,256]{2,1,0:T(8,128)S(1)}, f32[2,128,256]{2,1,0:T(8,128)S(1)}, f32...) custom-call(bf16[4,256,1536]{2,1,0:T(8,128)(2,1)} %constant.10.clone, ...), custom_call_target="tpu_custom_call" | custom-call | flops 3221225472 | bytes 16777216 | tf_op jit(solution)/shard_map/middle/pallas_call | solution.py:660
  104.1 2.1 %collective-permute-start.32 = (f32[2,128,256]{2,1,0:T(8,128)S(1)}, f32[2,128,256]{2,1,0:T(8,128)S(1)}, u32[]{:S(2)}, u32[]{:S(2)}) collective-permute-start(f32[2,128,256]{2,1,0:T(8,128)S(1)} %get-tuple-element.96), channel_id=1, source_target_pairs={{0,3},{1,2},{2,1},{3,0},{4,7},{5,6},{6,5},{7,4},{8,11},{9,10},{10,... | collective-permute-start | bytes 786440 | tf_op jit(solution)/shard_map/ppermute | solution.py:620
  106.3 4.4 %collective-permute-done.22.refs_3_ = f32[2,128,256]{2,1,0:T(8,128)S(1)} collective-permute-done((f32[2,128,256]{2,1,0:T(8,128)S(1)}, f32[2,128,256]{2,1,0:T(8,128)S(1)}, u32[]{:S(2)}, u32[]{:S(2)}) %collective-permute-start.22) | collective-permute-done | bytes 262176 | tf_op jit(solution)/shard_map/ppermute | solution.py:620
  110.7 1.8 backward_0.1
  112.6 7.8 %collective-permute-start.24 = (f32[2,128,128]{2,1,0:T(8,128)S(1)}, f32[2,128,128]{2,1,0:T(8,128)S(1)}, u32[]{:S(2)}, u32[]{:S(2)}) collective-permute-start(f32[2,128,128]{2,1,0:T(8,128)S(1)} %get-tuple-element.87), channel_id=1, source_target_pairs={{0,8},{4,12},{8,16},{12,20},{16,24},{20,28},{24,0},{28,4},{1,9},{5... | collective-permute-start | bytes 393224 | tf_op jit(solution)/shard_map/ppermute | solution.py:613
  120.4 1.9 %collective-permute-start.25 = (f32[2,128,128]{2,1,0:T(8,128)S(1)}, f32[2,128,128]{2,1,0:T(8,128)S(1)}, u32[]{:S(2)}, u32[]{:S(2)}) collective-permute-start(f32[2,128,128]{2,1,0:T(8,128)S(1)} %get-tuple-element.88), channel_id=1, source_target_pairs={{0,12},{4,16},{8,20},{12,24},{16,28},{20,0},{24,4},{28,8},{1,13},{... | collective-permute-start | bytes 393224 | tf_op jit(solution)/shard_map/ppermute | solution.py:613
  122.6 1.8 backward_1.1
  124.4 6.0 %collective-permute-start.28 = (f32[2,128,128]{2,1,0:T(8,128)S(1)}, f32[2,128,128]{2,1,0:T(8,128)S(1)}, u32[]{:S(2)}, u32[]{:S(2)}) collective-permute-start(f32[2,128,128]{2,1,0:T(8,128)S(1)} %get-tuple-element.91), channel_id=1, source_target_pairs={{0,24},{4,28},{8,0},{12,4},{16,8},{20,12},{24,16},{28,20},{1,25},{... | collective-permute-start | bytes 393224 | tf_op jit(solution)/shard_map/ppermute | solution.py:613
  130.5 5.9 %collective-permute-done.25.refs_3_ = f32[2,128,128]{2,1,0:T(8,128)S(1)} collective-permute-done((f32[2,128,128]{2,1,0:T(8,128)S(1)}, f32[2,128,128]{2,1,0:T(8,128)S(1)}, u32[]{:S(2)}, u32[]{:S(2)}) %collective-permute-start.25) | collective-permute-done | bytes 131104 | tf_op jit(solution)/shard_map/ppermute | solution.py:613
  136.4 3.4 %collective-permute-done.26.refs_4_ = f32[2,128,128]{2,1,0:T(8,128)S(1)} collective-permute-done((f32[2,128,128]{2,1,0:T(8,128)S(1)}, f32[2,128,128]{2,1,0:T(8,128)S(1)}, u32[]{:S(2)}, u32[]{:S(2)}) %collective-permute-start.26) | collective-permute-done | bytes 131104 | tf_op jit(solution)/shard_map/ppermute | solution.py:613
  141.9 8.8 %collective-permute-done.28.refs_6_ = f32[2,128,128]{2,1,0:T(8,128)S(1)} collective-permute-done((f32[2,128,128]{2,1,0:T(8,128)S(1)}, f32[2,128,128]{2,1,0:T(8,128)S(1)}, u32[]{:S(2)}, u32[]{:S(2)}) %collective-permute-start.28) | collective-permute-done | bytes 131104 | tf_op jit(solution)/shard_map/ppermute | solution.py:613
  151.4 2.2 %collective-permute-start.39 = (f32[2,128,128]{2,1,0:T(8,128)S(1)}, f32[2,128,128]{2,1,0:T(8,128)S(1)}, u32[]{:S(2)}, u32[]{:S(2)}) collective-permute-start(f32[2,128,128]{2,1,0:T(8,128)S(1)} %get-tuple-element.104), channel_id=1, source_target_pairs={{0,28},{4,0},{8,4},{12,8},{16,12},{20,16},{24,20},{28,24},{1,29},{... | collective-permute-start | bytes 393224 | tf_op jit(solution)/shard_map/ppermute | solution.py:613
  153.5 10.5 %copy-done.1 = f32[16,8,1,1,65536]{4,3,2,1,0:T(1,128)S(1)} copy-done((f32[16,8,1,1,65536]{4,3,2,1,0:T(1,128)S(1)}, f32[16,8,1,1,65536]{4,3,2,1,0:T(1,128)}, u32[]{:S(2)}) %copy-start.1) | copy-done | bytes 33554456
  164.1 11.0 %copy_spectrum.1.buffer = f32[65536,128]{1,0:T(8,128)} custom-call(f32[65536,128]{1,0:T(8,128)S(1)} %bitcast.5), custom_call_target="tpu_custom_call" | custom-call | bytes 67108864 | tf_op jit(solution)/shard_map/copy_spectrum/pallas_call | solution.py:642
  175.1 5.1 %update_0.1.buffer = f32[65536,128]{1,0:T(8,128)} custom-call(s32[8]{0:T(128)S(1)} %copy-done.5, s32[8]{0:T(128)S(1)} %copy-done.7, s32[8]{0:T(128)S(1)} %copy-done.9, f32[65536,128]{1,0:T(8,128)S(1)} %bitcast.6, f32[65536,128]{1,0:T(8,128)} %copy_spectrum.1.buffer, f32[2,128,128]{2,1,0:T(8,128)S(1)} %get-tuple-element.85.refs_0_, ...), custom_call_target="tpu_custom_call", output_to_operand_aliasing={{}: (4, {})} | custom-call | bytes 4194304 | tf_op jit(solution)/shard_map/update_0/pallas_call | solution.py:681
  180.3 5.2 %update_1.1 = f32[65536,128]{1,0:T(8,128)} custom-call(s32[8]{0:T(128)S(1)} %copy-done.5, s32[8]{0:T(128)S(1)} %copy-done.7, s32[8]{0:T(128)S(1)} %copy-done.9, f32[65536,128]{1,0:T(8,128)S(1)} %bitcast.7, f32[65536,128]{1,0:T(8,128)} %update_0.1.buffer, f32[2,128,128]{2,1,0:T(8,128)S(1)} %get-tuple-element.97.refs_0_, ...), custom_call_target="tpu_custom_call", output_to_operand_aliasing={{}: (4, {})} | custom-call | bytes 4194304 | tf_op jit(solution)/shard_map/update_1/pallas_call | solution.py:681
  (85 shorter events, 23.4 us)
Async XLA Ops:
  18.2 14.1 %collective-permute-start.2 = (f32[2,128,128]{2,1,0:T(8,128)S(1)}, f32[2,128,128]{2,1,0:T(8,128)S(1)}, u32[]{:S(2)}, u32[]{:S(2)}) collective-permute-start(f32[2,128,128]{2,1,0:T(8,128)S(1)} %get-tuple-element.60), channel_id=1, source_target_pairs={{0,12},{4,16},{8,20},{12,24},{16,28},{20,0},{24,4},{28,8},{1,13},{... | collective-permute-start | bytes 393224 | tf_op jit(solution)/shard_map/ppermute | solution.py:613
  18.2 18.1 %collective-permute-start.3 = (f32[2,128,128]{2,1,0:T(8,128)S(1)}, f32[2,128,128]{2,1,0:T(8,128)S(1)}, u32[]{:S(2)}, u32[]{:S(2)}) collective-permute-start(f32[2,128,128]{2,1,0:T(8,128)S(1)} %get-tuple-element.61), channel_id=1, source_target_pairs={{0,16},{4,20},{8,24},{12,28},{16,0},{20,4},{24,8},{28,12},{1,17},{... | collective-permute-start | bytes 393224 | tf_op jit(solution)/shard_map/ppermute | solution.py:613
  19.6 24.1 %collective-permute-start.4 = (f32[2,128,128]{2,1,0:T(8,128)S(1)}, f32[2,128,128]{2,1,0:T(8,128)S(1)}, u32[]{:S(2)}, u32[]{:S(2)}) collective-permute-start(f32[2,128,128]{2,1,0:T(8,128)S(1)} %get-tuple-element.62), channel_id=1, source_target_pairs={{0,20},{4,24},{8,28},{12,0},{16,4},{20,8},{24,12},{28,16},{1,21},{... | collective-permute-start | bytes 393224 | tf_op jit(solution)/shard_map/ppermute | solution.py:613
  23.7 28.9 %collective-permute-start.10 = (f32[2,128,128]{2,1,0:T(8,128)S(1)}, f32[2,128,128]{2,1,0:T(8,128)S(1)}, u32[]{:S(2)}, u32[]{:S(2)}) collective-permute-start(f32[2,128,128]{2,1,0:T(8,128)S(1)} %get-tuple-element.70), channel_id=1, source_target_pairs={{0,4},{4,8},{8,12},{12,16},{16,20},{20,24},{24,28},{28,0},{1,5},{5... | collective-permute-start | bytes 393224 | tf_op jit(solution)/shard_map/ppermute | solution.py:613
  24.0 28.9 %collective-permute-start.11 = (f32[2,128,128]{2,1,0:T(8,128)S(1)}, f32[2,128,128]{2,1,0:T(8,128)S(1)}, u32[]{:S(2)}, u32[]{:S(2)}) collective-permute-start(f32[2,128,128]{2,1,0:T(8,128)S(1)} %get-tuple-element.71), channel_id=1, source_target_pairs={{0,8},{4,12},{8,16},{12,20},{16,24},{20,28},{24,0},{28,4},{1,9},{5... | collective-permute-start | bytes 393224 | tf_op jit(solution)/shard_map/ppermute | solution.py:613
  32.2 23.2 %collective-permute-start.12 = (f32[2,128,128]{2,1,0:T(8,128)S(1)}, f32[2,128,128]{2,1,0:T(8,128)S(1)}, u32[]{:S(2)}, u32[]{:S(2)}) collective-permute-start(f32[2,128,128]{2,1,0:T(8,128)S(1)} %get-tuple-element.72), channel_id=1, source_target_pairs={{0,12},{4,16},{8,20},{12,24},{16,28},{20,0},{24,4},{28,8},{1,13},{... | collective-permute-start | bytes 393224 | tf_op jit(solution)/shard_map/ppermute | solution.py:613
  36.3 13.4 %collective-permute-start.5 = (f32[2,128,128]{2,1,0:T(8,128)S(1)}, f32[2,128,128]{2,1,0:T(8,128)S(1)}, u32[]{:S(2)}, u32[]{:S(2)}) collective-permute-start(f32[2,128,128]{2,1,0:T(8,128)S(1)} %get-tuple-element.63), channel_id=1, source_target_pairs={{0,24},{4,28},{8,0},{12,4},{16,8},{20,12},{24,16},{28,20},{1,25},{... | collective-permute-start | bytes 393224 | tf_op jit(solution)/shard_map/ppermute | solution.py:613
  51.6 21.0 %collective-permute-start.7 = (f32[2,128,256]{2,1,0:T(8,128)S(1)}, f32[2,128,256]{2,1,0:T(8,128)S(1)}, u32[]{:S(2)}, u32[]{:S(2)}) collective-permute-start(f32[2,128,256]{2,1,0:T(8,128)S(1)} %get-tuple-element.66), channel_id=1, source_target_pairs={{0,1},{1,0},{2,3},{3,2},{4,5},{5,4},{6,7},{7,6},{8,9},{9,8},{10,11... | collective-permute-start | bytes 786440 | tf_op jit(solution)/shard_map/ppermute | solution.py:620
  51.6 13.7 %collective-permute-start.13 = (f32[2,128,128]{2,1,0:T(8,128)S(1)}, f32[2,128,128]{2,1,0:T(8,128)S(1)}, u32[]{:S(2)}, u32[]{:S(2)}) collective-permute-start(f32[2,128,128]{2,1,0:T(8,128)S(1)} %get-tuple-element.73), channel_id=1, source_target_pairs={{0,16},{4,20},{8,24},{12,28},{16,0},{20,4},{24,8},{28,12},{1,17},{... | collective-permute-start | bytes 393224 | tf_op jit(solution)/shard_map/ppermute | solution.py:613
  52.5 14.2 %collective-permute-start.14 = (f32[2,128,128]{2,1,0:T(8,128)S(1)}, f32[2,128,128]{2,1,0:T(8,128)S(1)}, u32[]{:S(2)}, u32[]{:S(2)}) collective-permute-start(f32[2,128,128]{2,1,0:T(8,128)S(1)} %get-tuple-element.74), channel_id=1, source_target_pairs={{0,20},{4,24},{8,28},{12,0},{16,4},{20,8},{24,12},{28,16},{1,21},{... | collective-permute-start | bytes 393224 | tf_op jit(solution)/shard_map/ppermute | solution.py:613
  52.9 15.0 %collective-permute-start.15 = (f32[2,128,128]{2,1,0:T(8,128)S(1)}, f32[2,128,128]{2,1,0:T(8,128)S(1)}, u32[]{:S(2)}, u32[]{:S(2)}) collective-permute-start(f32[2,128,128]{2,1,0:T(8,128)S(1)} %get-tuple-element.75), channel_id=1, source_target_pairs={{0,24},{4,28},{8,0},{12,4},{16,8},{20,12},{24,16},{28,20},{1,25},{... | collective-permute-start | bytes 393224 | tf_op jit(solution)/shard_map/ppermute | solution.py:613
  55.5 12.4 %collective-permute-start.16 = (f32[2,128,128]{2,1,0:T(8,128)S(1)}, f32[2,128,128]{2,1,0:T(8,128)S(1)}, u32[]{:S(2)}, u32[]{:S(2)}) collective-permute-start(f32[2,128,128]{2,1,0:T(8,128)S(1)} %get-tuple-element.76), channel_id=1, source_target_pairs={{0,28},{4,0},{8,4},{12,8},{16,12},{20,16},{24,20},{28,24},{1,29},{... | collective-permute-start | bytes 393224 | tf_op jit(solution)/shard_map/ppermute | solution.py:613
  65.3 13.1 %collective-permute-start.8 = (f32[2,128,256]{2,1,0:T(8,128)S(1)}, f32[2,128,256]{2,1,0:T(8,128)S(1)}, u32[]{:S(2)}, u32[]{:S(2)}) collective-permute-start(f32[2,128,256]{2,1,0:T(8,128)S(1)} %get-tuple-element.67), channel_id=1, source_target_pairs={{0,2},{1,3},{2,0},{3,1},{4,6},{5,7},{6,4},{7,5},{8,10},{9,11},{10,... | collective-permute-start | bytes 786440 | tf_op jit(solution)/shard_map/ppermute | solution.py:620
  66.7 11.7 %collective-permute-start.9 = (f32[2,128,256]{2,1,0:T(8,128)S(1)}, f32[2,128,256]{2,1,0:T(8,128)S(1)}, u32[]{:S(2)}, u32[]{:S(2)}) collective-permute-start(f32[2,128,256]{2,1,0:T(8,128)S(1)} %get-tuple-element.68), channel_id=1, source_target_pairs={{0,3},{1,2},{2,1},{3,0},{4,7},{5,6},{6,5},{7,4},{8,11},{9,10},{10,... | collective-permute-start | bytes 786440 | tf_op jit(solution)/shard_map/ppermute | solution.py:620
  71.3 18.4 %collective-permute-start.18 = (f32[2,128,256]{2,1,0:T(8,128)S(1)}, f32[2,128,256]{2,1,0:T(8,128)S(1)}, u32[]{:S(2)}, u32[]{:S(2)}) collective-permute-start(f32[2,128,256]{2,1,0:T(8,128)S(1)} %get-tuple-element.79), channel_id=1, source_target_pairs={{0,2},{1,3},{2,0},{3,1},{4,6},{5,7},{6,4},{7,5},{8,10},{9,11},{10,... | collective-permute-start | bytes 786440 | tf_op jit(solution)/shard_map/ppermute | solution.py:620
  72.6 17.1 %collective-permute-start.19 = (f32[2,128,256]{2,1,0:T(8,128)S(1)}, f32[2,128,256]{2,1,0:T(8,128)S(1)}, u32[]{:S(2)}, u32[]{:S(2)}) collective-permute-start(f32[2,128,256]{2,1,0:T(8,128)S(1)} %get-tuple-element.80), channel_id=1, source_target_pairs={{0,3},{1,2},{2,1},{3,0},{4,7},{5,6},{6,5},{7,4},{8,11},{9,10},{10,... | collective-permute-start | bytes 786440 | tf_op jit(solution)/shard_map/ppermute | solution.py:620
  100.2 20.2 %collective-permute-start.30 = (f32[2,128,256]{2,1,0:T(8,128)S(1)}, f32[2,128,256]{2,1,0:T(8,128)S(1)}, u32[]{:S(2)}, u32[]{:S(2)}) collective-permute-start(f32[2,128,256]{2,1,0:T(8,128)S(1)} %get-tuple-element.94), channel_id=1, source_target_pairs={{0,1},{1,0},{2,3},{3,2},{4,5},{5,4},{6,7},{7,6},{8,9},{9,8},{10,11... | collective-permute-start | bytes 786440 | tf_op jit(solution)/shard_map/ppermute | solution.py:620
  101.5 20.8 %collective-permute-start.31 = (f32[2,128,256]{2,1,0:T(8,128)S(1)}, f32[2,128,256]{2,1,0:T(8,128)S(1)}, u32[]{:S(2)}, u32[]{:S(2)}) collective-permute-start(f32[2,128,256]{2,1,0:T(8,128)S(1)} %get-tuple-element.95), channel_id=1, source_target_pairs={{0,2},{1,3},{2,0},{3,1},{4,6},{5,7},{6,4},{7,5},{8,10},{9,11},{10,... | collective-permute-start | bytes 786440 | tf_op jit(solution)/shard_map/ppermute | solution.py:620
  104.1 18.2 %collective-permute-start.32 = (f32[2,128,256]{2,1,0:T(8,128)S(1)}, f32[2,128,256]{2,1,0:T(8,128)S(1)}, u32[]{:S(2)}, u32[]{:S(2)}) collective-permute-start(f32[2,128,256]{2,1,0:T(8,128)S(1)} %get-tuple-element.96), channel_id=1, source_target_pairs={{0,3},{1,2},{2,1},{3,0},{4,7},{5,6},{6,5},{7,4},{8,11},{9,10},{10,... | collective-permute-start | bytes 786440 | tf_op jit(solution)/shard_map/ppermute | solution.py:620
  112.5 11.9 %collective-permute-start.23 = (f32[2,128,128]{2,1,0:T(8,128)S(1)}, f32[2,128,128]{2,1,0:T(8,128)S(1)}, u32[]{:S(2)}, u32[]{:S(2)}) collective-permute-start(f32[2,128,128]{2,1,0:T(8,128)S(1)} %get-tuple-element.86), channel_id=1, source_target_pairs={{0,4},{4,8},{8,12},{12,16},{16,20},{20,24},{24,28},{28,0},{1,5},{5... | collective-permute-start | bytes 393224 | tf_op jit(solution)/shard_map/ppermute | solution.py:613
  112.6 17.9 %collective-permute-start.24 = (f32[2,128,128]{2,1,0:T(8,128)S(1)}, f32[2,128,128]{2,1,0:T(8,128)S(1)}, u32[]{:S(2)}, u32[]{:S(2)}) collective-permute-start(f32[2,128,128]{2,1,0:T(8,128)S(1)} %get-tuple-element.87), channel_id=1, source_target_pairs={{0,8},{4,12},{8,16},{12,20},{16,24},{20,28},{24,0},{28,4},{1,9},{5... | collective-permute-start | bytes 393224 | tf_op jit(solution)/shard_map/ppermute | solution.py:613
  120.4 16.0 %collective-permute-start.25 = (f32[2,128,128]{2,1,0:T(8,128)S(1)}, f32[2,128,128]{2,1,0:T(8,128)S(1)}, u32[]{:S(2)}, u32[]{:S(2)}) collective-permute-start(f32[2,128,128]{2,1,0:T(8,128)S(1)} %get-tuple-element.88), channel_id=1, source_target_pairs={{0,12},{4,16},{8,20},{12,24},{16,28},{20,0},{24,4},{28,8},{1,13},{... | collective-permute-start | bytes 393224 | tf_op jit(solution)/shard_map/ppermute | solution.py:613
  122.3 17.5 %collective-permute-start.26 = (f32[2,128,128]{2,1,0:T(8,128)S(1)}, f32[2,128,128]{2,1,0:T(8,128)S(1)}, u32[]{:S(2)}, u32[]{:S(2)}) collective-permute-start(f32[2,128,128]{2,1,0:T(8,128)S(1)} %get-tuple-element.89), channel_id=1, source_target_pairs={{0,16},{4,20},{8,24},{12,28},{16,0},{20,4},{24,8},{28,12},{1,17},{... | collective-permute-start | bytes 393224 | tf_op jit(solution)/shard_map/ppermute | solution.py:613
  122.3 18.2 %collective-permute-start.27 = (f32[2,128,128]{2,1,0:T(8,128)S(1)}, f32[2,128,128]{2,1,0:T(8,128)S(1)}, u32[]{:S(2)}, u32[]{:S(2)}) collective-permute-start(f32[2,128,128]{2,1,0:T(8,128)S(1)} %get-tuple-element.90), channel_id=1, source_target_pairs={{0,20},{4,24},{8,28},{12,0},{16,4},{20,8},{24,12},{28,16},{1,21},{... | collective-permute-start | bytes 393224 | tf_op jit(solution)/shard_map/ppermute | solution.py:613
  124.4 26.3 %collective-permute-start.28 = (f32[2,128,128]{2,1,0:T(8,128)S(1)}, f32[2,128,128]{2,1,0:T(8,128)S(1)}, u32[]{:S(2)}, u32[]{:S(2)}) collective-permute-start(f32[2,128,128]{2,1,0:T(8,128)S(1)} %get-tuple-element.91), channel_id=1, source_target_pairs={{0,24},{4,28},{8,0},{12,4},{16,8},{20,12},{24,16},{28,20},{1,25},{... | collective-permute-start | bytes 393224 | tf_op jit(solution)/shard_map/ppermute | solution.py:613
  130.5 20.6 %collective-permute-start.29 = (f32[2,128,128]{2,1,0:T(8,128)S(1)}, f32[2,128,128]{2,1,0:T(8,128)S(1)}, u32[]{:S(2)}, u32[]{:S(2)}) collective-permute-start(f32[2,128,128]{2,1,0:T(8,128)S(1)} %get-tuple-element.92), channel_id=1, source_target_pairs={{0,28},{4,0},{8,4},{12,8},{16,12},{20,16},{24,20},{28,24},{1,29},{... | collective-permute-start | bytes 393224 | tf_op jit(solution)/shard_map/ppermute | solution.py:613
  136.4 14.7 %collective-permute-start.33 = (f32[2,128,128]{2,1,0:T(8,128)S(1)}, f32[2,128,128]{2,1,0:T(8,128)S(1)}, u32[]{:S(2)}, u32[]{:S(2)}) collective-permute-start(f32[2,128,128]{2,1,0:T(8,128)S(1)} %get-tuple-element.98), channel_id=1, source_target_pairs={{0,4},{4,8},{8,12},{12,16},{16,20},{20,24},{24,28},{28,0},{1,5},{5... | collective-permute-start | bytes 393224 | tf_op jit(solution)/shard_map/ppermute | solution.py:613
  140.5 39.7 %collective-permute-start.35 = (f32[2,128,128]{2,1,0:T(8,128)S(1)}, f32[2,128,128]{2,1,0:T(8,128)S(1)}, u32[]{:S(2)}, u32[]{:S(2)}) collective-permute-start(f32[2,128,128]{2,1,0:T(8,128)S(1)} %get-tuple-element.100), channel_id=1, source_target_pairs={{0,12},{4,16},{8,20},{12,24},{16,28},{20,0},{24,4},{28,8},{1,13},{... | collective-permute-start | bytes 393224 | tf_op jit(solution)/shard_map/ppermute | solution.py:613
  150.7 29.6 %collective-permute-start.36 = (f32[2,128,128]{2,1,0:T(8,128)S(1)}, f32[2,128,128]{2,1,0:T(8,128)S(1)}, u32[]{:S(2)}, u32[]{:S(2)}) collective-permute-start(f32[2,128,128]{2,1,0:T(8,128)S(1)} %get-tuple-element.101), channel_id=1, source_target_pairs={{0,16},{4,20},{8,24},{12,28},{16,0},{20,4},{24,8},{28,12},{1,17},{... | collective-permute-start | bytes 393224 | tf_op jit(solution)/shard_map/ppermute | solution.py:613
  151.1 29.2 %collective-permute-start.37 = (f32[2,128,128]{2,1,0:T(8,128)S(1)}, f32[2,128,128]{2,1,0:T(8,128)S(1)}, u32[]{:S(2)}, u32[]{:S(2)}) collective-permute-start(f32[2,128,128]{2,1,0:T(8,128)S(1)} %get-tuple-element.102), channel_id=1, source_target_pairs={{0,20},{4,24},{8,28},{12,0},{16,4},{20,8},{24,12},{28,16},{1,21},{... | collective-permute-start | bytes 393224 | tf_op jit(solution)/shard_map/ppermute | solution.py:613
  151.1 29.2 %collective-permute-start.38 = (f32[2,128,128]{2,1,0:T(8,128)S(1)}, f32[2,128,128]{2,1,0:T(8,128)S(1)}, u32[]{:S(2)}, u32[]{:S(2)}) collective-permute-start(f32[2,128,128]{2,1,0:T(8,128)S(1)} %get-tuple-element.103), channel_id=1, source_target_pairs={{0,24},{4,28},{8,0},{12,4},{16,8},{20,12},{24,16},{28,20},{1,25},{... | collective-permute-start | bytes 393224 | tf_op jit(solution)/shard_map/ppermute | solution.py:613
  151.4 28.9 %collective-permute-start.39 = (f32[2,128,128]{2,1,0:T(8,128)S(1)}, f32[2,128,128]{2,1,0:T(8,128)S(1)}, u32[]{:S(2)}, u32[]{:S(2)}) collective-permute-start(f32[2,128,128]{2,1,0:T(8,128)S(1)} %get-tuple-element.104), channel_id=1, source_target_pairs={{0,28},{4,0},{8,4},{12,8},{16,12},{20,16},{24,20},{28,24},{1,29},{... | collective-permute-start | bytes 393224 | tf_op jit(solution)/shard_map/ppermute | solution.py:613
  (21 other events, 273.4 us)

commit v2 on v1

--- a/solution.py
+++ b/solution.py
@@ -195,8 +195,20 @@
 HALF_LANES = 64
 LANES = 128
 SUB = 128
-CHUNKS = 2
+FORWARD_CUTS = (4, 4)
+COPY_FIRST = False
+EARLY = (0,)
+COST = 1
+SECOND_AFTER = ()
+FORWARD_LED = (False, False)
+BACKWARD_LED = (True, False)
+FORWARD_TILE = (True, False)
+BACKWARD_TILE = (False, False)
+BACKWARD_CUTS = (4, 4)
+MIDDLE_VMEM = 20
+ROW_VMEM = 14
 ANY = pl.ANY
+HBM = pltpu.HBM
 F32 = jnp.float32
 BF16 = jnp.bfloat16
 
@@ -221,7 +233,7 @@
             (np.concatenate([cos.T, -sin.T], 0), row_bwd),
         ):
             high, low = split_table(stacked)
-            out.append(np.concatenate([high, high, low], 0))
+            out.append(np.concatenate([high, low], 0))
         angle = 2.0 * math.pi * (grid_b * (step + 4 * grid_k) % M) / M
         cos, sin = np.cos(angle) / 32.0, np.sin(angle) / 32.0
         for stacked, out in (
@@ -229,7 +241,7 @@
             (np.concatenate([cos, -sin], 1), col_bwd),
         ):
             high, low = split_table(stacked)
-            out.append(np.concatenate([high, high, low], 1))
+            out.append(np.concatenate([high, low], 1))
     return [np.stack(t) for t in (row_fwd, row_bwd, col_fwd, col_bwd)]
 
 
@@ -242,6 +254,7 @@
 def right_product(re, im, table):
     re_high, re_low = halves(re)
     im_high, im_low = halves(im)
+    table = jnp.concatenate([table[: 2 * QUARTER], table], axis=0)
     top = jnp.concatenate([re_high, -im_high, re_low, -im_low, re_high, -im_high], axis=1)
     bottom = jnp.concatenate([im_high, re_high, im_low, re_low, im_high, re_high], axis=1)
     return (
@@ -253,6 +266,7 @@
 def left_product(re, im, table):
     re_high, re_low = halves(re)
     im_high, im_low = halves(im)
+    table = jnp.concatenate([table[:, : 2 * QUARTER], table], axis=1)
     left = jnp.concatenate([re_high, -im_high, re_low, -im_low, re_high, -im_high], axis=0)
     right = jnp.concatenate([im_high, re_high, im_low, re_low, im_high, re_high], axis=0)
     return (
@@ -289,7 +303,26 @@
     return cos_out, sin_out
 
 
-def piece_row(slot, row_first, col_first, band, lead, row_off, col_off):
+def runs_of(band, cuts):
+    unit = band // sum(cuts)
+    runs, first = [], 0
+    for cut in cuts:
+        runs.append((first, cut * unit))
+        first += cut * unit
+    return runs
+
+
+def spans_of(run):
+    first, rows = run
+    spans, last = [], first + rows
+    while first < last:
+        end = min(last, (first // TILE + 1) * TILE)
+        spans.append((first, end - first))
+        first = end
+    return spans
+
+
+def block_base(slot, row_first, col_first, band, lead, row_off, col_off):
     led = lead[slot]
     row_start = row_off[led] * TILE
     col_start = col_off[led] * TILE
@@ -308,27 +341,45 @@
         copy.wait()
 
 
-def gather_kernel(sizes, chunk, lead, row_off, col_off, spectrum, *refs):
-    leds, tiles, band, rows = sizes
-    outs, sems = refs[:-1], refs[-1]
+def gather_kernel(sizes, run, packed, after, lead, row_off, col_off, spectrum, *refs):
+    leds, tiles, band = sizes
+    outs, (staged, sems_in, sems_out, scalars, sems_scalar) = refs[after:-5], refs[-5:]
     me, tile = lax.axis_index("led"), lax.axis_index("tile")
-    copies = []
-    for shift in range(leds):
-        slot = lax.rem(me + shift, leds)
-        base = piece_row(slot, tile * band + chunk * rows, me * LANES, band, lead, row_off, col_off)
-        for part in range(2):
-            first = pl.multiple_of(base + part * band + chunk * rows, 8)
-            copies.append(
-                pltpu.make_async_copy(
-                    spectrum.at[pl.ds(first, rows)], outs[shift].at[part], sems.at[shift, part]
-                )
-            )
+    copies = [
+        pltpu.make_async_copy(ref, scalars.at[n], sems_scalar.at[n])
+        for n, ref in enumerate((lead, row_off, col_off))
+    ]
     start_all(copies)
     wait_all(copies)
+    lead, row_off, col_off = scalars.at[0], scalars.at[1], scalars.at[2]
+    spans = spans_of(run)
+    arriving = []
+    for shift in range(leds):
+        slot = shift if packed else lax.rem(me + shift, leds)
+        for n, (first, rows) in enumerate(spans):
+            base = block_base(slot, tile * band + first, me * LANES, band, lead, row_off, col_off)
+            for part in range(2):
+                line = pl.multiple_of(base + part * band + first, 8)
+                arriving.append(
+                    pltpu.make_async_copy(
+                        spectrum.at[pl.ds(line, rows)],
+                        staged.at[shift, part, first - run[0] : first - run[0] + rows],
+                        sems_in.at[shift, n, part],
+                    )
+                )
+    start_all(arriving)
+    each = len(spans) * 2
+    leaving = []
+    for shift in range(leds):
+        wait_all(arriving[shift * each : (shift + 1) * each])
+        target = outs[0].at[shift] if packed else outs[shift]
+        leaving.append(pltpu.make_async_copy(staged.at[shift], target, sems_out.at[shift]))
+        leaving[-1].start()
+    wait_all(leaving)
 
 
 def prepare_kernel(sizes, lead, row_off, col_off, mask, aberration, intensities, pupil, images, turned):
-    leds, tiles, band, rows = sizes
+    leds, tiles, band = sizes
     me, tile = lax.axis_index("led"), lax.axis_index("tile")
     led = lead[me]
     line = lax.broadcasted_iota(jnp.int32, (band, band), 0)
@@ -369,20 +420,26 @@
             pupil[(1,) + where] = gate * sine
 
 
-def forward_kernel(sizes, chunk, table, pupil, *refs):
-    leds, tiles, band, rows = sizes
-    pieces, refs = refs[:leds], refs[leds:]
-    outs, refs = refs[:tiles], refs[tiles:]
+def forward_kernel(sizes, run, packed, piece_count, early, table, pupil, *refs):
+    leds, tiles, band = sizes
+    run_first, rows = run
+    pieces, refs = refs[:piece_count], refs[piece_count + early :]
+    count = 1 if packed else tiles
+    outs, refs = refs[:count], refs[count:]
     table_v, pupil_v, window, result, sems, sems_out = refs
     me, tile = lax.axis_index("led"), lax.axis_index("tile")
     copies = []
     for shift in range(leds):
-        first = pl.multiple_of(lax.rem(me - shift + leds, leds) * LANES, LANES)
+        if piece_count == 1:
+            piece, first = pieces[0].at[shift], shift * LANES
+        else:
+            piece = pieces[shift]
+            first = pl.multiple_of(lax.rem(me - shift + leds, leds) * LANES, LANES)
         copies.append(
-            pltpu.make_async_copy(pieces[shift], window.at[:, :, pl.ds(first, LANES)], sems.at[shift])
+            pltpu.make_async_copy(piece, window.at[:, :, pl.ds(first, LANES)], sems.at[shift])
         )
     copies.append(
-        pltpu.make_async_copy(pupil.at[:, chunk * rows : (chunk + 1) * rows], pupil_v, sems.at[leds])
+        pltpu.make_async_copy(pupil.at[:, run_first : run_first + rows], pupil_v, sems.at[leds])
     )
     copies.append(pltpu.make_async_copy(table, table_v, sems.at[leds + 1]))
     start_all(copies)
@@ -406,33 +463,34 @@
                 result[other, part, :, pair * LANES : (pair + 1) * LANES] = jnp.where(
                     lane < HALF_LANES, first, second
                 )
-    copies = [
-        pltpu.make_async_copy(result.at[tile ^ shift], outs[shift], sems_out.at[shift])
-        for shift in range(tiles)
-    ]
+    if packed:
+        copies = [pltpu.make_async_copy(result, outs[0], sems_out.at[0])]
+    else:
+        copies = [
+            pltpu.make_async_copy(result.at[tile ^ shift], outs[shift], sems_out.at[shift])
+            for shift in range(tiles)
+        ]
     start_all(copies)
     wait_all(copies)
 
 
-def middle_kernel(sizes, table, table_back, images, *refs):
-    leds, tiles, band, rows = sizes
-    chunks = band // rows
-    blocks, refs = refs[: chunks * tiles], refs[chunks * tiles :]
-    outs, refs = refs[: chunks * tiles], refs[chunks * tiles :]
-    table_v, back_v, images_v, field, residual, sems, sems_out = refs
+def tile_views(stack, run, packed, tile, tiles):
+    first, rows = run
+    cells = slice(first, first + rows)
+    if packed:
+        return [stack.at[:, :, cells]]
+    return [stack.at[tile ^ shift, :, cells] for shift in range(tiles)]
+
+
+def middle_kernel(sizes, runs_in, runs_out, table, table_back, images, copied, *refs):
+    leds, tiles, band = sizes
     tile = lax.axis_index("tile")
-    copies = []
-    for chunk in range(chunks):
-        for shift in range(tiles):
-            where = chunk * tiles + shift
-            copies.append(
-                pltpu.make_async_copy(
-                    blocks[where],
-                    field.at[tile ^ shift, :, chunk * rows : (chunk + 1) * rows],
-                    sems.at[where],
-                )
-            )
-    count = chunks * tiles
+    table_v, back_v, images_v, field, residual, sems, sems_out = refs[-7:]
+    views = [v for run, packed in runs_in for v in tile_views(field, run, packed, tile, tiles)]
+    leaving = [v for run, packed in runs_out for v in tile_views(field, run, packed, tile, tiles)]
+    blocks, outs = refs[: len(views)], refs[len(views) : -7]
+    count = len(views)
+    copies = [pltpu.make_async_copy(b, v, sems.at[n]) for n, (b, v) in enumerate(zip(blocks, views))]
     copies.append(pltpu.make_async_copy(table, table_v, sems.at[count]))
     copies.append(pltpu.make_async_copy(images, images_v, sems.at[count + 1]))
     copies.append(pltpu.make_async_copy(table_back, back_v, sems.at[count + 2]))
@@ -450,33 +508,24 @@
     for a, (re, im) in enumerate(mixed):
         field[a, 0] = re
         field[a, 1] = im
-    copies = []
-    for chunk in range(chunks):
-        for shift in range(tiles):
-            where = chunk * tiles + shift
-            copies.append(
-                pltpu.make_async_copy(
-                    field.at[tile ^ shift, :, chunk * rows : (chunk + 1) * rows],
-                    outs[where],
-                    sems_out.at[where],
-                )
-            )
+    copies = [pltpu.make_async_copy(v, o, sems_out.at[n]) for n, (v, o) in enumerate(zip(leaving, outs))]
     start_all(copies)
     wait_all(copies)
 
 
-def backward_kernel(sizes, chunk, table, pupil, *refs):
-    leds, tiles, band, rows = sizes
-    blocks, refs = refs[:tiles], refs[tiles:]
-    outs, refs = refs[:leds], refs[leds:]
+def backward_kernel(sizes, run, packed, led_packed, held, table, pupil, *refs):
+    leds, tiles, band = sizes
+    run_first, rows = run
+    count = 1 if packed else tiles
+    blocks, refs = refs[:count], refs[count + held :]
+    sent = 1 if led_packed else leds
+    outs, refs = refs[:sent], refs[sent + held :]
     table_v, pupil_v, lines, result, sems, sems_out = refs
     me, tile = lax.axis_index("led"), lax.axis_index("tile")
-    copies = [
-        pltpu.make_async_copy(blocks[shift], lines.at[tile ^ shift], sems.at[shift])
-        for shift in range(tiles)
-    ]
+    views = tile_views(lines, (0, rows), packed, tile, tiles)
+    copies = [pltpu.make_async_copy(b, v, sems.at[n]) for n, (b, v) in enumerate(zip(blocks, views))]
     copies.append(
-        pltpu.make_async_copy(pupil.at[:, chunk * rows : (chunk + 1) * rows], pupil_v, sems.at[tiles])
+        pltpu.make_async_copy(pupil.at[:, run_first : run_first + rows], pupil_v, sems.at[tiles])
     )
     copies.append(pltpu.make_async_copy(table, table_v, sems.at[tiles + 1]))
     start_all(copies)
@@ -502,111 +551,183 @@
         result[1, :, cells] = gate_re * im - gate_im * re
     copies = []
     for shift in range(leds):
-        first = pl.multiple_of(lax.rem(me + shift, leds) * LANES, LANES)
+        if led_packed:
+            first, target = shift * LANES, outs[0].at[shift]
+        else:
+            first = pl.multiple_of(lax.rem(me + shift, leds) * LANES, LANES)
+            target = outs[shift]
         copies.append(
-            pltpu.make_async_copy(
-                result.at[:, :, pl.ds(first, LANES)], outs[shift], sems_out.at[shift]
-            )
+            pltpu.make_async_copy(result.at[:, :, pl.ds(first, LANES)], target, sems_out.at[shift])
         )
     start_all(copies)
     wait_all(copies)
 
 
-def update_kernel(sizes, chunk, lead, row_off, col_off, spectrum, buffer, *refs):
-    leds, tiles, band, rows = sizes
-    pieces, refs = refs[:leds], refs[leds:]
-    updated, grads, cells, sems, sems_in, sems_out = refs
+def update_kernel(sizes, run, lead, row_off, col_off, spectrum, buffer, *refs):
+    leds, tiles, band = sizes
+    pieces = refs[:-6]
+    updated, grads, cells, sems, sems_in, sems_out = refs[-6:]
     me, tile = lax.axis_index("led"), lax.axis_index("tile")
+    run_first = run[0]
+    arriving = []
+    spans = spans_of(run)
     bases = [
-        piece_row(slot, tile * band + chunk * rows, me * LANES, band, lead, row_off, col_off)
+        [
+            block_base(slot, tile * band + first, me * LANES, band, lead, row_off, col_off)
+            for first, rows in spans
+        ]
         for slot in range(leds)
     ]
-    copies = []
-    for shift in range(leds):
-        slot = lax.rem(me - shift + leds, leds)
-        copies.append(pltpu.make_async_copy(pieces[shift], grads.at[slot], sems.at[shift]))
+
+    def lines_at(ref, slot, n, part):
+        first, rows = spans[n]
+        return ref.at[pl.ds(pl.multiple_of(bases[slot][n] + part * band + first, 8), rows)]
+
+    def cells_at(slot, n, part):
+        first, rows = spans[n]
+        return cells.at[slot, part, first - run_first : first - run_first + rows]
+
+    every = [(n, part) for n in range(len(spans)) for part in range(2)]
     for slot in range(leds):
-        for part in range(2):
-            first = pl.multiple_of(bases[slot] + part * band + chunk * rows, 8)
-            copies.append(
+        for n, part in every:
+            arriving.append(
                 pltpu.make_async_copy(
-                    spectrum.at[pl.ds(first, rows)], cells.at[slot, part], sems_in.at[slot, part]
+                    lines_at(spectrum, slot, n, part), cells_at(slot, n, part), sems_in.at[slot, n, part]
                 )
             )
-    start_all(copies)
-    wait_all(copies)
-    firsts = []
+    for shift in range(leds):
+        if len(pieces) == 1:
+            arriving.append(pltpu.make_async_copy(pieces[0].at[shift], grads.at[shift], sems.at[shift]))
+        else:
+            slot = lax.rem(me - shift + leds, leds)
+            arriving.append(pltpu.make_async_copy(pieces[shift], grads.at[slot], sems.at[shift]))
+    start_all(arriving)
+    shared = jnp.bool_(False)
+    is_first = []
     for slot in range(leds):
-        is_first = jnp.bool_(True)
+        is_first.append([jnp.bool_(True)] * len(spans))
         for earlier in range(slot):
-            is_first = jnp.logical_and(is_first, bases[earlier] != bases[slot])
-        firsts.append(is_first)
-        for later in range(slot + 1, leds):
-
-            @pl.when(jnp.logical_and(is_first, bases[later] == bases[slot]))
-            def _():
-                grads[slot] = grads[slot] + grads[later]
-
-        cells[slot] = cells[slot] - STEP_SIZE * grads[slot]
+            for n in range(len(spans)):
+                same = bases[earlier][n] == bases[slot][n]
+                shared = jnp.logical_or(shared, same)
+                is_first[slot][n] = jnp.logical_and(is_first[slot][n], jnp.logical_not(same))
+    wait_all(arriving)
+
+    @pl.when(shared)
+    def _():
+        for n, (first, rows) in enumerate(spans):
+            where = slice(first - run_first, first - run_first + rows)
+            for slot in range(leds):
+                for later in range(slot + 1, leds):
+
+                    @pl.when(jnp.logical_and(is_first[slot][n], bases[later][n] == bases[slot][n]))
+                    def _():
+                        grads[slot, :, where] = grads[slot, :, where] + grads[later, :, where]
+
     for waiting in (False, True):
         for slot in range(leds):
-
-            @pl.when(firsts[slot])
-            def _():
-                for part in range(2):
-                    first = pl.multiple_of(bases[slot] + part * band + chunk * rows, 8)
-                    copy = pltpu.make_async_copy(
-                        cells.at[slot, part], updated.at[pl.ds(first, rows)], sems_out.at[slot, part]
-                    )
-                    if waiting:
-                        copy.wait()
-                    else:
-                        copy.start()
-
-
-COPY_PARTS = 16
-
-
-def copy_kernel(spectrum, copied, sems):
-    lines = spectrum.shape[0] // COPY_PARTS
-    copies = [
-        pltpu.make_async_copy(
-            spectrum.at[pl.ds(n * lines, lines)], copied.at[pl.ds(n * lines, lines)], sems.at[n]
+            if not waiting:
+                cells[slot] = cells[slot] - STEP_SIZE * grads[slot]
+            for n in range(len(spans)):
+
+                @pl.when(is_first[slot][n])
+                def _():
+                    for part in range(2):
+                        copy = pltpu.make_async_copy(
+                            cells_at(slot, n, part),
+                            lines_at(updated, slot, n, part),
+                            sems_out.at[slot, n, part],
+                        )
+                        if waiting:
+                            copy.wait()
+                        else:
+                            copy.start()
+
+
+COPY_LINES = 2048
+COPY_SLOTS = 8
+
+
+def copy_kernel(first, lines, after, spectrum, *refs):
+    copied, staged, sems_in, sems_out = refs[-4:]
+    count = lines // COPY_LINES
+
+    def copy_in(n):
+        return pltpu.make_async_copy(
+            spectrum.at[pl.ds(first + n * COPY_LINES, COPY_LINES)],
+            staged.at[n % COPY_SLOTS],
+            sems_in.at[n % COPY_SLOTS],
         )
-        for n in range(COPY_PARTS)
-    ]
-    start_all(copies)
-    wait_all(copies)
-
-
-def call(kernel, name, ins, outs, scratch, flops=0, moved=0, aliases=None, vmem=16):
-    return pl.pallas_call(
+
+    def copy_out(n):
+        return pltpu.make_async_copy(
+            staged.at[n % COPY_SLOTS],
+            copied.at[pl.ds(first + n * COPY_LINES, COPY_LINES)],
+            sems_out.at[n % COPY_SLOTS],
+        )
+
+    lag = COPY_SLOTS // 2
+    for n in range(count + lag):
+        if n < count:
+            if n >= COPY_SLOTS:
+                copy_out(n - COPY_SLOTS).wait()
+            copy_in(n).start()
+        if n >= lag:
+            copy_in(n - lag).wait()
+            copy_out(n - lag).start()
+    for n in range(max(count - COPY_SLOTS, 0), count):
+        copy_out(n).wait()
+
+
+def call(kernel, name, ins, outs, scratch, flops=0, moved=0, aliases=None, vmem=36):
+    run = pl.pallas_call(
         kernel,
         name=name,
-        out_shape=outs,
+        out_shape=jax.tree.map(lambda o: HBM(o.shape, o.dtype), outs),
         in_specs=[pl.BlockSpec(memory_space=place) for place in ins],
-        out_specs=jax.tree.map(lambda _: pl.BlockSpec(memory_space=ANY), outs),
+        out_specs=jax.tree.map(lambda _: pl.BlockSpec(memory_space=HBM), outs),
         scratch_shapes=scratch,
         input_output_aliases=aliases or {},
-        cost_estimate=pl.CostEstimate(flops=flops, bytes_accessed=moved, transcendentals=0),
+        cost_estimate=pl.CostEstimate(flops=COST * flops, bytes_accessed=COST * moved, transcendentals=0),
         compiler_params=pltpu.CompilerParams(vmem_limit_bytes=vmem * 2**20),
     )
+
+    def pinned(*arrays):
+        return run(
+            *(
+                pltpu.with_memory_space_constraint(x, HBM) if place == HBM else x
+                for place, x in zip(ins, arrays)
+            )
+        )
+
+    return pinned
+
+
+def own_first(count):
+    return [ANY] if count == 1 else [HBM] + [ANY] * (count - 1)
 
 
 def unit_shards(spectrum, intensities, led_of_slot, row_offset, col_offset, tile_mask, aberration):
     tiles = lax.axis_size("tile")
     leds = lax.axis_size("led")
     band = M // tiles
-    rows = band // CHUNKS
-    sizes = (leds, tiles, band, rows)
+    sizes = (leds, tiles, band)
+    forward_runs = runs_of(band, FORWARD_CUTS)
+    backward_runs = runs_of(band, BACKWARD_CUTS)
+    forward_packed = FORWARD_TILE
+    backward_packed = BACKWARD_TILE
     row_fwd, row_bwd, col_fwd, col_bwd = (jnp.asarray(t) for t in quarter_tables())
     flat = spectrum.reshape(-1, LANES)
     smem, vmem = pltpu.SMEM, pltpu.VMEM
     dma = pltpu.SemaphoreType.DMA
-    f32 = lambda *shape: jax.ShapeDtypeStruct(shape, F32)
     part = functools.partial
 
-    def over_led(arrays):
+    def f32(*shape):
+        return jax.ShapeDtypeStruct(shape, F32)
+
+    def over_led(arrays, packed):
+        if packed:
+            return [lax.all_to_all(arrays[0], "led", split_axis=0, concat_axis=0, tiled=True)]
         moved = [arrays[0]]
         for shift in range(1, leds):
             moved.append(
@@ -614,21 +735,37 @@
             )
         return moved
 
-    def over_tile(arrays):
+    def over_tile(arrays, packed):
+        if packed:
+            return [lax.all_to_all(arrays[0], "tile", split_axis=0, concat_axis=0, tiled=True)]
         moved = [arrays[0]]
         for shift in range(1, tiles):
             moved.append(lax.ppermute(arrays[shift], "tile", [(i, i ^ shift) for i in range(tiles)]))
         return moved
 
-    piece = f32(2, rows, LANES)
-    taken = [
-        call(
-            part(gather_kernel, sizes, chunk), f"gather_{chunk}", [smem] * 3 + [ANY], [piece] * leds,
-            [dma((leds, 2))], moved=4 * leds * piece.size * 2,
-        )(led_of_slot, row_offset, col_offset, flat)
-        for chunk in range(CHUNKS)
-    ]
-    arrived = [over_led(arrays) for arrays in taken]
+    def pieces_of(run, packed):
+        if packed:
+            return [f32(leds, 2, run[1], LANES)]
+        return [f32(2, run[1], LANES)] * leds
+
+    def blocks_of(run, packed):
+        if packed:
+            return [f32(tiles, 2, run[1], band)]
+        return [f32(2, run[1], band)] * tiles
+
+    arrived = []
+    for number, (run, packed) in enumerate(zip(forward_runs, FORWARD_LED)):
+        after = [arrived[0][shift] for shift in SECOND_AFTER] if number else []
+        taken = call(
+            part(gather_kernel, sizes, run, packed, len(after)), f"gather_{number}",
+            [HBM] * 4 + [ANY] * len(after), pieces_of(run, packed),
+            [
+                pltpu.VMEM((leds, 2, run[1], LANES), F32), dma((leds, len(spans_of(run)), 2)), dma((leds,)),
+                pltpu.SMEM((3, leds), jnp.int32), dma((3,)),
+            ],
+            moved=2**22, vmem=8,
+        )(led_of_slot, row_offset, col_offset, flat, *after)
+        arrived.append(over_led(taken, packed))
     pupil, images = pl.pallas_call(
         part(prepare_kernel, sizes),
         name="prepare",
@@ -636,57 +773,85 @@
         in_specs=[pl.BlockSpec(memory_space=smem)] * 5 + [pl.BlockSpec(memory_space=vmem)],
         out_specs=[pl.BlockSpec(memory_space=vmem)] * 2,
         scratch_shapes=[pltpu.VMEM((band // LANES, M, LANES), F32)],
-        compiler_params=pltpu.CompilerParams(vmem_limit_bytes=24 * 2**20),
+        compiler_params=pltpu.CompilerParams(vmem_limit_bytes=16 * 2**20),
         cost_estimate=pl.CostEstimate(flops=2 * 10**9, bytes_accessed=4 * 10**6, transcendentals=0),
     )(led_of_slot, row_offset, col_offset, tile_mask, aberration, intensities[0])
-    copied = call(
-        copy_kernel, "copy_spectrum", [ANY], f32(*flat.shape), [dma((COPY_PARTS,))], moved=8 * flat.size
-    )(flat)
-    block = f32(2, rows, band)
-    table_shape = (4, 6 * QUARTER, QUARTER)
-    received = []
-    for chunk in range(CHUNKS):
+    def copy_half(number, after, so_far):
+        lines = flat.shape[0] // 2
+        return call(
+            part(copy_kernel, number * lines, lines), f"copy_{number}",
+            [HBM] * (2 + len(so_far)), f32(*flat.shape),
+            [pltpu.VMEM((COPY_SLOTS, COPY_LINES, LANES), F32), dma((COPY_SLOTS,)), dma((COPY_SLOTS,))],
+            moved=4 * flat.size, aliases={2: 0} if so_far else None, vmem=16,
+        )(after, flat, *so_far)
+
+    table_shape = (4, 4 * QUARTER, QUARTER)
+    received, copied = [], None
+    for number, (run, packed, pieces) in enumerate(zip(forward_runs, forward_packed, arrived)):
+        rows = run[1]
+        early = ([copied] if COPY_FIRST else lines[:1]) if number else []
+        if number == 0:
+            early = [arrived[1][shift] for shift in EARLY]
+        pieces_count = len(pieces)
         lines = call(
-            part(forward_kernel, sizes, chunk), f"forward_{chunk}", [ANY] * (2 + leds), [block] * tiles,
+            part(forward_kernel, sizes, run, packed, pieces_count, len(early)), f"forward_{run[0]}", [HBM, ANY] + own_first(pieces_count) + [HBM] * len(early),
+            blocks_of(run, packed),
             [
                 pltpu.VMEM(table_shape, BF16), pltpu.VMEM((2, rows, M), F32),
                 pltpu.VMEM((2, rows, M), F32), pltpu.VMEM((tiles, 2, rows, band), F32),
                 dma((leds + 2,)), dma((tiles,)),
             ],
-            flops=24 * rows * M * QUARTER, moved=2**23, vmem=40,
-        )(row_fwd, pupil, *arrived[chunk])
-        received += over_tile(lines)
-    count = CHUNKS * tiles
+            flops=24 * rows * M * QUARTER, moved=2**23, vmem=ROW_VMEM,
+        )(row_fwd, pupil, *pieces, *early)
+        received += over_tile(lines, packed)
+        if number == (0 if COPY_FIRST else 1):
+            copied = copy_half(0, lines[0], [])
+
+    arrays_in, arrays_out = len(received), sum(1 if p else tiles for p in backward_packed)
     returned = call(
-        part(middle_kernel, sizes), "middle", [ANY] * (3 + count), [block] * count,
+        part(middle_kernel, sizes, list(zip(forward_runs, forward_packed)), list(zip(backward_runs, backward_packed))),
+        "middle", [HBM] * 2 + [ANY, HBM] + [HBM] * arrays_in,
+        [b for run, packed in zip(backward_runs, backward_packed) for b in blocks_of(run, packed)],
         [
-            pltpu.VMEM((4, QUARTER, 6 * QUARTER), BF16), pltpu.VMEM((4, QUARTER, 6 * QUARTER), BF16),
+            pltpu.VMEM((4, QUARTER, 4 * QUARTER), BF16), pltpu.VMEM((4, QUARTER, 4 * QUARTER), BF16),
             pltpu.VMEM((M, band), F32), pltpu.VMEM((4, 2, QUARTER, band), F32),
-            pltpu.VMEM((4, 2, QUARTER, band), F32), dma((count + 3,)), dma((count,)),
+            pltpu.VMEM((4, 2, QUARTER, band), F32), dma((arrays_in + 3,)), dma((arrays_out,)),
         ],
-        flops=48 * band * M * QUARTER, moved=2**24, vmem=48,
-    )(col_fwd, col_bwd, images, *received)
-    updated = copied
-    for chunk in range(CHUNKS):
-        lines = over_tile(returned[chunk * tiles : (chunk + 1) * tiles])
-        pieces = call(
-            part(backward_kernel, sizes, chunk), f"backward_{chunk}", [ANY] * (2 + tiles), [piece] * leds,
+        flops=48 * band * M * QUARTER, moved=2**24, vmem=MIDDLE_VMEM,
+    )(col_fwd, col_bwd, images, copied, *received)
+    updated = copy_half(1, returned[0], [copied])
+    count = 1 if backward_packed[0] else tiles
+    returned, later = returned[:count], returned[count:]
+    for number, (run, packed, led_packed) in enumerate(zip(backward_runs, backward_packed, BACKWARD_LED)):
+        rows = run[1]
+        sent = 1 if led_packed else leds
+        lines = over_tile(returned if number == 0 else later, packed)
+        held, through = (list(later), [updated]) if number == 0 else ([], [])
+        count = len(lines)
+        results = call(
+            part(backward_kernel, sizes, run, packed, led_packed, len(held + through)), f"backward_{run[0]}",
+            [HBM, ANY] + own_first(count) + [ANY] * len(held) + [HBM] * len(through),
+            pieces_of(run, led_packed) + [f32(*h.shape) for h in held + through],
             [
                 pltpu.VMEM(table_shape, BF16), pltpu.VMEM((2, rows, M), F32),
                 pltpu.VMEM((tiles, 2, rows, band), F32), pltpu.VMEM((2, rows, M), F32),
                 dma((tiles + 2,)), dma((leds,)),
             ],
-            flops=24 * rows * M * QUARTER, moved=2**23, vmem=40,
-        )(row_bwd, pupil, *lines)
+            flops=24 * rows * M * QUARTER, moved=2**23, vmem=ROW_VMEM,
+            aliases={2 + count + n: sent + n for n in range(len(held + through))},
+        )(row_bwd, pupil, *lines, *held, *through)
+        pieces, later = over_led(results[:sent], led_packed), results[sent : sent + len(held)]
+        updated = results[-1] if through else updated
+        spans = len(spans_of(run))
         updated = call(
-            part(update_kernel, sizes, chunk), f"update_{chunk}", [smem] * 3 + [ANY] * (2 + leds),
+            part(update_kernel, sizes, run), f"update_{run[0]}", [smem] * 3 + [HBM] * 2 + own_first(sent),
             f32(*flat.shape),
             [
                 pltpu.VMEM((leds, 2, rows, LANES), F32), pltpu.VMEM((leds, 2, rows, LANES), F32),
-                dma((leds,)), dma((leds, 2)), dma((leds, 2)),
+                dma((leds,)), dma((leds, spans, 2)), dma((leds, spans, 2)),
             ],
-            moved=2**22, aliases={4: 0},
-        )(led_of_slot, row_offset, col_offset, flat, updated, *over_led(pieces))
+            moved=2**22, aliases={4: 0}, vmem=16,
+        )(led_of_slot, row_offset, col_offset, flat, updated, *pieces)
     return updated.reshape(spectrum.shape)
 
 

time: 189 us -> 167 us (0.88); the launches traced: 186 us -> 167 us
  local copies, waits for them, and re-layouts: 23.1 us -> 0.69 us
  Pallas kernels: 44.8 us -> 66.5 us
  starting transfers between devices: 58.2 us -> 38.1 us
    ppermute x28 -> x21, starting transfers between devices: 45.4 us -> 21.4 us  [over_led(): lax.ppermute(arrays[shift], 'led', [(i, (i + shift) % leds) for i in rang...]
    unnamed x26 -> x18, local copies, waits for them, and re-layouts: 23.1 us -> 0.69 us
    pallas_call x10 -> x11, Pallas kernels: 41.3 us -> 62.9 us  [pinned(): run(*(pltpu.with_memory_space_constraint(x, HBM) if place == HBM else x f...]
    ppermute x28 -> x21, waiting for transfers between devices: 36.2 us -> 49.3 us  [over_led(): lax.ppermute(arrays[shift], 'led', [(i, (i + shift) % leds) for i in rang...]
    ppermute x12 -> x9, waiting for transfers between devices: 23 us -> 11.6 us  [over_tile(): lax.ppermute(arrays[shift], 'tile', [(i, i ^ shift) for i in range(tiles)])]
    all_to_all x0 -> x2, starting transfers between devices: none -> 8.65 us  [the longest x1 4.39 us: over_led(): lax.all_to_all(arrays[0], 'led', split_axis=0, concat_axis=0, tiled=True)]
    ppermute x12 -> x9, starting transfers between devices: 12.8 us -> 8.08 us  [over_tile(): lax.ppermute(arrays[shift], 'tile', [(i, i ^ shift) for i in range(tiles)])]
  transfers between devices with their start and end apart: 40 -> 32, of which waited for: 11 -> 16; matrix products, arithmetic and copies ran while one was open for 0% -> 0% of each run, Pallas kernels for 16% -> 26%
where the time goes in v2:
time: 167 us
  Pallas kernels  66.5 us (40%)
  waiting for transfers between devices  60.9 us (36%)
  starting transfers between devices  38.1 us (23%)
    pallas_call x11, Pallas kernels, pinned(): run(*(pltpu.with_memory_space_constraint(x, HBM) if place == HBM else x f...  62.9 us
    ppermute x21, waiting for transfers between devices, over_led(): lax.ppermute(arrays[shift], 'led', [(i, (i + shift) % leds) for i in rang...  49.3 us
    ppermute x21, starting transfers between devices, over_led(): lax.ppermute(arrays[shift], 'led', [(i, (i + shift) % leds) for i in rang...  21.4 us
    ppermute x9, waiting for transfers between devices, over_tile(): lax.ppermute(arrays[shift], 'tile', [(i, i ^ shift) for i in range(tiles)])  11.6 us
    ppermute x9, starting transfers between devices, over_tile(): lax.ppermute(arrays[shift], 'tile', [(i, i ^ shift) for i in range(tiles)])  8.08 us
    all_to_all x1, starting transfers between devices, over_led(): lax.all_to_all(arrays[0], 'led', split_axis=0, concat_axis=0, tiled=True)  4.39 us
    all_to_all x1, starting transfers between devices, over_tile(): lax.all_to_all(arrays[0], 'tile', split_axis=0, concat_axis=0, tiled=True)  4.26 us
    pallas_call x1, Pallas kernels, unit_shards(): pl.pallas_call(part(prepare_kernel, sizes), name='prepare', out_shape=[f3...  3.59 us
  transfers between devices with their start and end apart: 32, of which 16 were waited for; matrix products, arithmetic and copies ran while one was open for 0% of the time, Pallas kernels for 26%

profile of v2, /device:TPU:11, one launch (start us, length us, event | category | flops | bytes accessed | tf_op | source)
XLA Modules:
  0.0 166.7 jit_solution(8711609400702744646)
XLA Ops:
  0.0 3.0 %gather_0.1 = (f32[2,128,128]{2,1,0:T(8,128)}, f32[2,128,128]{2,1,0:T(8,128)}, f32[2,128,128]{2,1,0:T(8,128)}, f32[2,128,128]{2,1,0:T(8,128)}, f32[2,128,128]{2,...) custom-call(s32[8]{0:T(128)} %lead.9, s32[8]{0:T(128)} %row_off.9, ...), custom_call_target="tpu_custom_call" | custom-call | bytes 4194304 | tf_op jit(solution)/shard_map/gather_0/pallas_call | solution.py:696
  3.1 1.9 %collective-permute-start.7 = (f32[2,128,128]{2,1,0:T(8,128)}, f32[2,128,128]{2,1,0:T(8,128)S(1)}, u32[]{:S(2)}, u32[]{:S(2)}) collective-permute-start(f32[2,128,128]{2,1,0:T(8,128)} %get-tuple-element.60), channel_id=1, source_target_pairs={{0,4},{4,8},{8,12},{12,16},{16,20},{20,24},{24,28},{28,0},{1,5},{5... | collective-permute-start | bytes 393224 | tf_op jit(solution)/shard_map/ppermute | solution.py:734
  6.3 1.4 collective-permute-start.10
  7.7 1.6 collective-permute-start.11
  9.3 2.8 %gather_1.1 = (f32[2,128,128]{2,1,0:T(8,128)}, f32[2,128,128]{2,1,0:T(8,128)}, f32[2,128,128]{2,1,0:T(8,128)}, f32[2,128,128]{2,1,0:T(8,128)}, f32[2,128,128]{2,...) custom-call(s32[8]{0:T(128)} %lead.9, s32[8]{0:T(128)} %row_off.9, ...), custom_call_target="tpu_custom_call" | custom-call | bytes 4194304 | tf_op jit(solution)/shard_map/gather_1/pallas_call | solution.py:696
  13.8 3.6 %prepare.1 = (f32[2,256,1024]{2,1,0:T(8,128)S(1)}, f32[1024,256]{1,0:T(8,128)S(1)}) custom-call(s32[8]{0:T(128)S(1)} %copy-done, s32[8]{0:T(128)S(1)} %copy-done.1, s32[8]{0:T(128)S(1)} %copy-done.2, s32[8,8,8]{2,1,0:T(8,128)S(1)} %copy-done.4, f32[5]{0:T(128)S(1)} %copy-done.5, bf16[256,1024]{1,0:T(8,128)(2,1)S(1)} %bitcast.3), custom_call_target="tpu_custom_call" | custom-call | flops 2000000000 | bytes 4000000 | tf_op jit(solution)/shard_map/prepare/pallas_call | solution.py:769
  17.4 7.5 %collective-permute-done.9.refs_3_ = f32[2,128,128]{2,1,0:T(8,128)S(1)} collective-permute-done((f32[2,128,128]{2,1,0:T(8,128)}, f32[2,128,128]{2,1,0:T(8,128)S(1)}, u32[]{:S(2)}, u32[]{:S(2)}) %collective-permute-start.9) | collective-permute-done | bytes 131104 | tf_op jit(solution)/shard_map/ppermute | solution.py:734
  24.9 2.8 %collective-permute-done.10.refs_4_ = f32[2,128,128]{2,1,0:T(8,128)S(1)} collective-permute-done((f32[2,128,128]{2,1,0:T(8,128)}, f32[2,128,128]{2,1,0:T(8,128)S(1)}, u32[]{:S(2)}, u32[]{:S(2)}) %collective-permute-start.10) | collective-permute-done | bytes 131104 | tf_op jit(solution)/shard_map/ppermute | solution.py:734
  27.7 1.8 %collective-permute-done.12.refs_6_ = f32[2,128,128]{2,1,0:T(8,128)S(1)} collective-permute-done((f32[2,128,128]{2,1,0:T(8,128)S(1)}, f32[2,128,128]{2,1,0:T(8,128)S(1)}, u32[]{:S(2)}, u32[]{:S(2)}) %collective-permute-start.12) | collective-permute-done | bytes 131104 | tf_op jit(solution)/shard_map/ppermute | solution.py:734
  29.6 4.1 %forward_0.1.refs_8_ = f32[4,2,128,256]{3,2,1,0:T(8,128)} custom-call(bf16[4,1024,256]{2,1,0:T(8,128)(2,1)} %constant.8.clone.table, f32[2,256,1024]{2,1,0:T(8,128)S(1)} %get-tuple-element.49.pupil, f32[2,128,128]{2,1,0:T(8,128)} %get-tuple-element.59.refs_0_, f32[2,128,128]{2,1,0:T(8,128)S(1)} %collective-permute-done.7.refs_1_, ...), custom_call_target="tpu_custom_call" | custom-call | flops 805306368 | bytes 8388608 | tf_op jit(solution)/shard_map/forward_0/pallas_call | solution.py:696
  33.8 4.3 %all-to-all-start = ((f32[4,2,128,256]{3,2,1,0:T(8,128)}), f32[4,2,128,256]{3,2,1,0:T(8,128)}, u32[]{:S(2)}, u32[]{:S(2)}) async-start(f32[4,2,128,256]{3,2,1,0:T(8,128)} %forward_0.1.refs_8_), calls=%async_computation | async-start | bytes 2097152 | tf_op jit(solution)/shard_map/all_to_all | solution.py:740
  38.5 1.5 collective-permute-start.2
  41.0 2.0 %collective-permute-start.4 = (f32[2,128,128]{2,1,0:T(8,128)}, f32[2,128,128]{2,1,0:T(8,128)S(1)}, u32[]{:S(2)}, u32[]{:S(2)}) collective-permute-start(f32[2,128,128]{2,1,0:T(8,128)} %get-tuple-element.56), channel_id=1, source_target_pairs={{0,20},{4,24},{8,28},{12,0},{16,4},{20,8},{24,12},{28,16},{1,21},{... | collective-permute-start | bytes 393224 | tf_op jit(solution)/shard_map/ppermute | solution.py:734
  45.2 12.7 %collective-permute-done.2.refs_3_ = f32[2,128,128]{2,1,0:T(8,128)S(1)} collective-permute-done((f32[2,128,128]{2,1,0:T(8,128)}, f32[2,128,128]{2,1,0:T(8,128)S(1)}, u32[]{:S(2)}, u32[]{:S(2)}) %collective-permute-start.2) | collective-permute-done | bytes 131104 | tf_op jit(solution)/shard_map/ppermute | solution.py:734
  57.9 2.8 %collective-permute-done.3.refs_4_ = f32[2,128,128]{2,1,0:T(8,128)S(1)} collective-permute-done((f32[2,128,128]{2,1,0:T(8,128)}, f32[2,128,128]{2,1,0:T(8,128)S(1)}, u32[]{:S(2)}, u32[]{:S(2)}) %collective-permute-start.3) | collective-permute-done | bytes 131104 | tf_op jit(solution)/shard_map/ppermute | solution.py:734
  60.7 2.4 %collective-permute-done.5.refs_6_ = f32[2,128,128]{2,1,0:T(8,128)S(1)} collective-permute-done((f32[2,128,128]{2,1,0:T(8,128)}, f32[2,128,128]{2,1,0:T(8,128)S(1)}, u32[]{:S(2)}, u32[]{:S(2)}) %collective-permute-start.5) | collective-permute-done | bytes 131104 | tf_op jit(solution)/shard_map/ppermute | solution.py:734
  63.2 4.1 %forward_128.1 = (f32[2,128,256]{2,1,0:T(8,128)}, f32[2,128,256]{2,1,0:T(8,128)}, f32[2,128,256]{2,1,0:T(8,128)}, f32[2,128,256]{2,1,0:T(8,128)}) custom-call(bf16[4,1024,256]{2,1,0:T(8,128)(2,1)} %constant.8.clone.table, f32[2,256,1024]{2,1,0:T(8,128)S(1)} %get-tuple-element.49.pupil, f32[2,128,128]{2,1,0:T(8,128)} %get-tuple-element.51.refs_8_.refs_0_, ...), custom_call_target="tpu_custom_call" | custom-call | flops 805306368 | bytes 8388608 | tf_op jit(solution)/shard_map/forward_128/pallas_call | solution.py:696
  70.1 12.4 %copy_0.1.copied.refs_0_ = f32[65536,128]{1,0:T(8,128)} custom-call(f32[2,128,256]{2,1,0:T(8,128)} %get-tuple-element.67.after.refs_1_, f32[65536,128]{1,0:T(8,128)} %bitcast.6), custom_call_target="tpu_custom_call" | custom-call | bytes 33554432 | tf_op jit(solution)/shard_map/copy_0/pallas_call | solution.py:696
  83.2 8.7 %middle.1 = (f32[2,128,256]{2,1,0:T(8,128)}, f32[2,128,256]{2,1,0:T(8,128)}, f32[2,128,256]{2,1,0:T(8,128)}, f32[2,128,256]{2,1,0:T(8,128)}, f32[2,128,256]{2,1,...) custom-call(bf16[4,256,1024]{2,1,0:T(8,128)(2,1)} %constant.10.clone.table, ...), custom_call_target="tpu_custom_call" | custom-call | flops 3221225472 | bytes 16777216 | tf_op jit(solution)/shard_map/middle/pallas_call | solution.py:696
  94.7 12.4 %copy_1.1.refs_8_ = f32[65536,128]{1,0:T(8,128)} custom-call(f32[2,128,256]{2,1,0:T(8,128)} %get-tuple-element.71.after.refs_0_, f32[65536,128]{1,0:T(8,128)} %bitcast.7, f32[65536,128]{1,0:T(8,128)} %copy_0.1.copied.refs_0_), custom_call_target="tpu_custom_call", output_to_operand_aliasing={{}: (2, {})} | custom-call | bytes 33554432 | tf_op jit(solution)/shard_map/copy_1/pallas_call | solution.py:696
  107.1 4.0 %backward_0.1 = (f32[8,2,128,128]{3,2,1,0:T(8,128)}, f32[2,128,256]{2,1,0:T(8,128)}, f32[2,128,256]{2,1,0:T(8,128)}, f32[2,128,256]{2,1,0:T(8,128)}, f32[2,128,256]{2,1,0:T(8,128)}, /*index=5*/f32[65536,128]{1,0:T(8,128)}) custom-call(bf16[4,1024,256]{2,1,0:T(8,128)(2,1)} %constant.9.clone., ...), custom_call_target="tpu_custom_call", output_to_operand_aliasing={{1}: (6, {}), {2}: (7, {}), {3}: (8, {}), {4}: (9, {}), {5}... | custom-call | flops 805306368 | bytes 8388608 | tf_op jit(solution)/shard_map/backward_0/pallas_call | solution.py:696
  111.1 4.4 %all-to-all-start.1 = ((f32[8,2,128,128]{3,2,1,0:T(8,128)}), f32[8,2,128,128]{3,2,1,0:T(8,128)S(1)}, u32[]{:S(2)}, u32[]{:S(2)}) async-start(f32[8,2,128,128]{3,2,1,0:T(8,128)} %get-tuple-element.80), calls=%async_computation.1 | async-start | bytes 2097152 | tf_op jit(solution)/shard_map/all_to_all | solution.py:730
  118.2 5.1 %collective-permute-done.20.refs_1_ = f32[2,128,256]{2,1,0:T(8,128)S(1)} collective-permute-done((f32[2,128,256]{2,1,0:T(8,128)}, f32[2,128,256]{2,1,0:T(8,128)S(1)}, u32[]{:S(2)}, u32[]{:S(2)}) %collective-permute-start.20) | collective-permute-done | bytes 262176 | tf_op jit(solution)/shard_map/ppermute | solution.py:743
  123.3 6.5 %collective-permute-done.22.refs_3_ = f32[2,128,256]{2,1,0:T(8,128)S(1)} collective-permute-done((f32[2,128,256]{2,1,0:T(8,128)}, f32[2,128,256]{2,1,0:T(8,128)S(1)}, u32[]{:S(2)}, u32[]{:S(2)}) %collective-permute-start.22) | collective-permute-done | bytes 262176 | tf_op jit(solution)/shard_map/ppermute | solution.py:743
  129.8 4.0 %backward_128.1 = (f32[2,128,128]{2,1,0:T(8,128)}, f32[2,128,128]{2,1,0:T(8,128)}, f32[2,128,128]{2,1,0:T(8,128)}, f32[2,128,128]{2,1,0:T(8,128)}, f32[2,128,128...) custom-call(bf16[4,1024,256]{2,1,0:T(8,128)(2,1)} %constant.9.clone.table, ...), custom_call_target="tpu_custom_call" | custom-call | flops 805306368 | bytes 8388608 | tf_op jit(solution)/shard_map/backward_128/pallas_call | solution.py:696
  133.8 2.3 %collective-permute-start.23 = (f32[2,128,128]{2,1,0:T(8,128)}, f32[2,128,128]{2,1,0:T(8,128)S(1)}, u32[]{:S(2)}, u32[]{:S(2)}) collective-permute-start(f32[2,128,128]{2,1,0:T(8,128)} %get-tuple-element.86), channel_id=1, source_target_pairs={{0,4},{4,8},{8,12},{12,16},{16,20},{20,24},{24,28},{28,0},{1,5},{5... | collective-permute-start | bytes 393224 | tf_op jit(solution)/shard_map/ppermute | solution.py:734
  137.4 1.4 collective-permute-start.26
  138.8 1.7 %collective-permute-start.27 = (f32[2,128,128]{2,1,0:T(8,128)}, f32[2,128,128]{2,1,0:T(8,128)S(1)}, u32[]{:S(2)}, u32[]{:S(2)}) collective-permute-start(f32[2,128,128]{2,1,0:T(8,128)} %get-tuple-element.90), channel_id=1, source_target_pairs={{0,20},{4,24},{8,28},{12,0},{16,4},{20,8},{24,12},{28,16},{1,21},{... | collective-permute-start | bytes 393224 | tf_op jit(solution)/shard_map/ppermute | solution.py:734
  141.5 13.9 %collective-permute-done.24.refs_2_ = f32[2,128,128]{2,1,0:T(8,128)S(1)} collective-permute-done((f32[2,128,128]{2,1,0:T(8,128)}, f32[2,128,128]{2,1,0:T(8,128)S(1)}, u32[]{:S(2)}, u32[]{:S(2)}) %collective-permute-start.24) | collective-permute-done | bytes 131104 | tf_op jit(solution)/shard_map/ppermute | solution.py:734
  155.4 3.5 %update_0.1.buffer = f32[65536,128]{1,0:T(8,128)} custom-call(s32[8]{0:T(128)S(1)} %copy-done, s32[8]{0:T(128)S(1)} %copy-done.1, s32[8]{0:T(128)S(1)} %copy-done.2, f32[65536,128]{1,0:T(8,128)} %bitcast.8, f32[65536,128]{1,0:T(8,128)} %get-tuple-element.79.buffer, f32[8,2,128,128]{3,2,1,0:T(8,128)S(1)} %all-to-all-done.1.refs_0_), custom_call_target="tpu_custom_call", output_to_operand_aliasing={{}: (4, {})} | custom-call | bytes 4194304 | tf_op jit(solution)/shard_map/update_0/pallas_call | solution.py:696
  159.0 2.1 %collective-permute-done.26.refs_4_ = f32[2,128,128]{2,1,0:T(8,128)S(1)} collective-permute-done((f32[2,128,128]{2,1,0:T(8,128)}, f32[2,128,128]{2,1,0:T(8,128)S(1)}, u32[]{:S(2)}, u32[]{:S(2)}) %collective-permute-start.26) | collective-permute-done | bytes 131104 | tf_op jit(solution)/shard_map/ppermute | solution.py:734
  162.8 3.7 %update_128.1 = f32[65536,128]{1,0:T(8,128)} custom-call(s32[8]{0:T(128)S(1)} %copy-done, s32[8]{0:T(128)S(1)} %copy-done.1, s32[8]{0:T(128)S(1)} %copy-done.2, f32[65536,128]{1,0:T(8,128)} %bitcast.9, f32[65536,128]{1,0:T(8,128)} %update_0.1.buffer, f32[2,128,128]{2,1,0:T(8,128)} %get-tuple-element.85.refs_0_, ...), custom_call_target="tpu_custom_call", output_to_operand_aliasing={{}: (4, {})} | custom-call | bytes 4194304 | tf_op jit(solution)/shard_map/update_128/pallas_call | solution.py:696
  (62 shorter events, 19.7 us)
Async XLA Ops:
  3.1 9.0 %collective-permute-start.7 = (f32[2,128,128]{2,1,0:T(8,128)}, f32[2,128,128]{2,1,0:T(8,128)S(1)}, u32[]{:S(2)}, u32[]{:S(2)}) collective-permute-start(f32[2,128,128]{2,1,0:T(8,128)} %get-tuple-element.60), channel_id=1, source_target_pairs={{0,4},{4,8},{8,12},{12,16},{16,20},{20,24},{24,28},{28,0},{1,5},{5... | collective-permute-start | bytes 393224 | tf_op jit(solution)/shard_map/ppermute | solution.py:734
  5.0 8.4 %collective-permute-start.8 = (f32[2,128,128]{2,1,0:T(8,128)}, f32[2,128,128]{2,1,0:T(8,128)S(1)}, u32[]{:S(2)}, u32[]{:S(2)}) collective-permute-start(f32[2,128,128]{2,1,0:T(8,128)} %get-tuple-element.61), channel_id=1, source_target_pairs={{0,8},{4,12},{8,16},{12,20},{16,24},{20,28},{24,0},{28,4},{1,9},{5... | collective-permute-start | bytes 393224 | tf_op jit(solution)/shard_map/ppermute | solution.py:734
  6.3 18.6 %collective-permute-start.9 = (f32[2,128,128]{2,1,0:T(8,128)}, f32[2,128,128]{2,1,0:T(8,128)S(1)}, u32[]{:S(2)}, u32[]{:S(2)}) collective-permute-start(f32[2,128,128]{2,1,0:T(8,128)} %get-tuple-element.62), channel_id=1, source_target_pairs={{0,12},{4,16},{8,20},{12,24},{16,28},{20,0},{24,4},{28,8},{1,13},{... | collective-permute-start | bytes 393224 | tf_op jit(solution)/shard_map/ppermute | solution.py:734
  6.3 21.4 %collective-permute-start.10 = (f32[2,128,128]{2,1,0:T(8,128)}, f32[2,128,128]{2,1,0:T(8,128)S(1)}, u32[]{:S(2)}, u32[]{:S(2)}) collective-permute-start(f32[2,128,128]{2,1,0:T(8,128)} %get-tuple-element.63), channel_id=1, source_target_pairs={{0,16},{4,20},{8,24},{12,28},{16,0},{20,4},{24,8},{28,12},{1,17},{... | collective-permute-start | bytes 393224 | tf_op jit(solution)/shard_map/ppermute | solution.py:734
  7.7 20.0 %collective-permute-start.11 = (f32[2,128,128]{2,1,0:T(8,128)}, f32[2,128,128]{2,1,0:T(8,128)S(1)}, u32[]{:S(2)}, u32[]{:S(2)}) collective-permute-start(f32[2,128,128]{2,1,0:T(8,128)} %get-tuple-element.64), channel_id=1, source_target_pairs={{0,20},{4,24},{8,28},{12,0},{16,4},{20,8},{24,12},{28,16},{1,21},{... | collective-permute-start | bytes 393224 | tf_op jit(solution)/shard_map/ppermute | solution.py:734
  12.1 17.4 %collective-permute-start.12 = (f32[2,128,128]{2,1,0:T(8,128)S(1)}, f32[2,128,128]{2,1,0:T(8,128)S(1)}, u32[]{:S(2)}, u32[]{:S(2)}) collective-permute-start(f32[2,128,128]{2,1,0:T(8,128)S(1)} %copy-done.8), channel_id=1, source_target_pairs={{0,24},{4,28},{8,0},{12,4},{16,8},{20,12},{24,16},{28,20},{1,25},{... | collective-permute-start | bytes 393224 | tf_op jit(solution)/shard_map/ppermute | solution.py:734
  13.4 16.3 %collective-permute-start.13 = (f32[2,128,128]{2,1,0:T(8,128)S(1)}, f32[2,128,128]{2,1,0:T(8,128)S(1)}, u32[]{:S(2)}, u32[]{:S(2)}) collective-permute-start(f32[2,128,128]{2,1,0:T(8,128)S(1)} %copy-done.7), channel_id=1, source_target_pairs={{0,28},{4,0},{8,4},{12,8},{16,12},{20,16},{24,20},{28,24},{1,29},{... | collective-permute-start | bytes 393224 | tf_op jit(solution)/shard_map/ppermute | solution.py:734
  33.8 48.8 %all-to-all-start = ((f32[4,2,128,256]{3,2,1,0:T(8,128)}), f32[4,2,128,256]{3,2,1,0:T(8,128)}, u32[]{:S(2)}, u32[]{:S(2)}) async-start(f32[4,2,128,256]{3,2,1,0:T(8,128)} %forward_0.1.refs_8_), calls=%async_computation | async-start | bytes 2097152 | tf_op jit(solution)/shard_map/all_to_all | solution.py:740
  38.0 5.0 %collective-permute-start = (f32[2,128,128]{2,1,0:T(8,128)}, f32[2,128,128]{2,1,0:T(8,128)S(1)}, u32[]{:S(2)}, u32[]{:S(2)}) collective-permute-start(f32[2,128,128]{2,1,0:T(8,128)} %get-tuple-element.52), channel_id=1, source_target_pairs={{0,4},{4,8},{8,12},{12,16},{16,20},{20,24},{24,28},{28,0},{1,5},{5... | collective-permute-start | bytes 393224 | tf_op jit(solution)/shard_map/ppermute | solution.py:734
  38.1 6.3 %collective-permute-start.1 = (f32[2,128,128]{2,1,0:T(8,128)}, f32[2,128,128]{2,1,0:T(8,128)S(1)}, u32[]{:S(2)}, u32[]{:S(2)}) collective-permute-start(f32[2,128,128]{2,1,0:T(8,128)} %get-tuple-element.53), channel_id=1, source_target_pairs={{0,8},{4,12},{8,16},{12,20},{16,24},{20,28},{24,0},{28,4},{1,9},{5... | collective-permute-start | bytes 393224 | tf_op jit(solution)/shard_map/ppermute | solution.py:734
  38.5 19.4 %collective-permute-start.2 = (f32[2,128,128]{2,1,0:T(8,128)}, f32[2,128,128]{2,1,0:T(8,128)S(1)}, u32[]{:S(2)}, u32[]{:S(2)}) collective-permute-start(f32[2,128,128]{2,1,0:T(8,128)} %get-tuple-element.54), channel_id=1, source_target_pairs={{0,12},{4,16},{8,20},{12,24},{16,28},{20,0},{24,4},{28,8},{1,13},{... | collective-permute-start | bytes 393224 | tf_op jit(solution)/shard_map/ppermute | solution.py:734
  40.0 20.7 %collective-permute-start.3 = (f32[2,128,128]{2,1,0:T(8,128)}, f32[2,128,128]{2,1,0:T(8,128)S(1)}, u32[]{:S(2)}, u32[]{:S(2)}) collective-permute-start(f32[2,128,128]{2,1,0:T(8,128)} %get-tuple-element.55), channel_id=1, source_target_pairs={{0,16},{4,20},{8,24},{12,28},{16,0},{20,4},{24,8},{28,12},{1,17},{... | collective-permute-start | bytes 393224 | tf_op jit(solution)/shard_map/ppermute | solution.py:734
  41.0 19.7 %collective-permute-start.4 = (f32[2,128,128]{2,1,0:T(8,128)}, f32[2,128,128]{2,1,0:T(8,128)S(1)}, u32[]{:S(2)}, u32[]{:S(2)}) collective-permute-start(f32[2,128,128]{2,1,0:T(8,128)} %get-tuple-element.56), channel_id=1, source_target_pairs={{0,20},{4,24},{8,28},{12,0},{16,4},{20,8},{24,12},{28,16},{1,21},{... | collective-permute-start | bytes 393224 | tf_op jit(solution)/shard_map/ppermute | solution.py:734
  43.0 20.1 %collective-permute-start.5 = (f32[2,128,128]{2,1,0:T(8,128)}, f32[2,128,128]{2,1,0:T(8,128)S(1)}, u32[]{:S(2)}, u32[]{:S(2)}) collective-permute-start(f32[2,128,128]{2,1,0:T(8,128)} %get-tuple-element.57), channel_id=1, source_target_pairs={{0,24},{4,28},{8,0},{12,4},{16,8},{20,12},{24,16},{28,20},{1,25},{... | collective-permute-start | bytes 393224 | tf_op jit(solution)/shard_map/ppermute | solution.py:734
  44.4 18.8 %collective-permute-start.6 = (f32[2,128,128]{2,1,0:T(8,128)}, f32[2,128,128]{2,1,0:T(8,128)S(1)}, u32[]{:S(2)}, u32[]{:S(2)}) collective-permute-start(f32[2,128,128]{2,1,0:T(8,128)} %get-tuple-element.58), channel_id=1, source_target_pairs={{0,28},{4,0},{8,4},{12,8},{16,12},{20,16},{24,20},{28,24},{1,29},{... | collective-permute-start | bytes 393224 | tf_op jit(solution)/shard_map/ppermute | solution.py:734
  67.3 15.2 %collective-permute-start.14 = (f32[2,128,256]{2,1,0:T(8,128)}, f32[2,128,256]{2,1,0:T(8,128)S(1)}, u32[]{:S(2)}, u32[]{:S(2)}) collective-permute-start(f32[2,128,256]{2,1,0:T(8,128)} %get-tuple-element.68), channel_id=1, source_target_pairs={{0,1},{1,0},{2,3},{3,2},{4,5},{5,4},{6,7},{7,6},{8,9},{9,8},{10,11... | collective-permute-start | bytes 786440 | tf_op jit(solution)/shard_map/ppermute | solution.py:743
  67.5 15.0 %collective-permute-start.15 = (f32[2,128,256]{2,1,0:T(8,128)}, f32[2,128,256]{2,1,0:T(8,128)}, u32[]{:S(2)}, u32[]{:S(2)}) collective-permute-start(f32[2,128,256]{2,1,0:T(8,128)} %get-tuple-element.69), channel_id=1, source_target_pairs={{0,2},{1,3},{2,0},{3,1},{4,6},{5,7},{6,4},{7,5},{8,10},{9,11},{10,... | collective-permute-start | bytes 786440 | tf_op jit(solution)/shard_map/ppermute | solution.py:743
  68.9 13.7 %collective-permute-start.16 = (f32[2,128,256]{2,1,0:T(8,128)}, f32[2,128,256]{2,1,0:T(8,128)}, u32[]{:S(2)}, u32[]{:S(2)}) collective-permute-start(f32[2,128,256]{2,1,0:T(8,128)} %get-tuple-element.70), channel_id=1, source_target_pairs={{0,3},{1,2},{2,1},{3,0},{4,7},{5,6},{6,5},{7,4},{8,11},{9,10},{10,... | collective-permute-start | bytes 786440 | tf_op jit(solution)/shard_map/ppermute | solution.py:743
  91.9 15.2 %collective-permute-start.17 = (f32[2,128,256]{2,1,0:T(8,128)}, f32[2,128,256]{2,1,0:T(8,128)S(1)}, u32[]{:S(2)}, u32[]{:S(2)}) collective-permute-start(f32[2,128,256]{2,1,0:T(8,128)} %get-tuple-element.72), channel_id=1, source_target_pairs={{0,1},{1,0},{2,3},{3,2},{4,5},{5,4},{6,7},{7,6},{8,9},{9,8},{10,11... | collective-permute-start | bytes 786440 | tf_op jit(solution)/shard_map/ppermute | solution.py:743
  92.1 15.0 %collective-permute-start.18 = (f32[2,128,256]{2,1,0:T(8,128)}, f32[2,128,256]{2,1,0:T(8,128)S(1)}, u32[]{:S(2)}, u32[]{:S(2)}) collective-permute-start(f32[2,128,256]{2,1,0:T(8,128)} %get-tuple-element.73), channel_id=1, source_target_pairs={{0,2},{1,3},{2,0},{3,1},{4,6},{5,7},{6,4},{7,5},{8,10},{9,11},{10,... | collective-permute-start | bytes 786440 | tf_op jit(solution)/shard_map/ppermute | solution.py:743
  93.5 13.7 %collective-permute-start.19 = (f32[2,128,256]{2,1,0:T(8,128)}, f32[2,128,256]{2,1,0:T(8,128)S(1)}, u32[]{:S(2)}, u32[]{:S(2)}) collective-permute-start(f32[2,128,256]{2,1,0:T(8,128)} %get-tuple-element.74), channel_id=1, source_target_pairs={{0,3},{1,2},{2,1},{3,0},{4,7},{5,6},{6,5},{7,4},{8,11},{9,10},{10,... | collective-permute-start | bytes 786440 | tf_op jit(solution)/shard_map/ppermute | solution.py:743
  111.1 44.3 %all-to-all-start.1 = ((f32[8,2,128,128]{3,2,1,0:T(8,128)}), f32[8,2,128,128]{3,2,1,0:T(8,128)S(1)}, u32[]{:S(2)}, u32[]{:S(2)}) async-start(f32[8,2,128,128]{3,2,1,0:T(8,128)} %get-tuple-element.80), calls=%async_computation.1 | async-start | bytes 2097152 | tf_op jit(solution)/shard_map/all_to_all | solution.py:730
  115.5 7.7 %collective-permute-start.20 = (f32[2,128,256]{2,1,0:T(8,128)}, f32[2,128,256]{2,1,0:T(8,128)S(1)}, u32[]{:S(2)}, u32[]{:S(2)}) collective-permute-start(f32[2,128,256]{2,1,0:T(8,128)} %get-tuple-element.82), channel_id=1, source_target_pairs={{0,1},{1,0},{2,3},{3,2},{4,5},{5,4},{6,7},{7,6},{8,9},{9,8},{10,11... | collective-permute-start | bytes 786440 | tf_op jit(solution)/shard_map/ppermute | solution.py:743
  115.7 7.6 %collective-permute-start.21 = (f32[2,128,256]{2,1,0:T(8,128)}, f32[2,128,256]{2,1,0:T(8,128)S(1)}, u32[]{:S(2)}, u32[]{:S(2)}) collective-permute-start(f32[2,128,256]{2,1,0:T(8,128)} %get-tuple-element.83), channel_id=1, source_target_pairs={{0,2},{1,3},{2,0},{3,1},{4,6},{5,7},{6,4},{7,5},{8,10},{9,11},{10,... | collective-permute-start | bytes 786440 | tf_op jit(solution)/shard_map/ppermute | solution.py:743
  117.0 12.8 %collective-permute-start.22 = (f32[2,128,256]{2,1,0:T(8,128)}, f32[2,128,256]{2,1,0:T(8,128)S(1)}, u32[]{:S(2)}, u32[]{:S(2)}) collective-permute-start(f32[2,128,256]{2,1,0:T(8,128)} %get-tuple-element.84), channel_id=1, source_target_pairs={{0,3},{1,2},{2,1},{3,0},{4,7},{5,6},{6,5},{7,4},{8,11},{9,10},{10,... | collective-permute-start | bytes 786440 | tf_op jit(solution)/shard_map/ppermute | solution.py:743
  133.8 7.6 %collective-permute-start.23 = (f32[2,128,128]{2,1,0:T(8,128)}, f32[2,128,128]{2,1,0:T(8,128)S(1)}, u32[]{:S(2)}, u32[]{:S(2)}) collective-permute-start(f32[2,128,128]{2,1,0:T(8,128)} %get-tuple-element.86), channel_id=1, source_target_pairs={{0,4},{4,8},{8,12},{12,16},{16,20},{20,24},{24,28},{28,0},{1,5},{5... | collective-permute-start | bytes 393224 | tf_op jit(solution)/shard_map/ppermute | solution.py:734
  136.1 19.3 %collective-permute-start.24 = (f32[2,128,128]{2,1,0:T(8,128)}, f32[2,128,128]{2,1,0:T(8,128)S(1)}, u32[]{:S(2)}, u32[]{:S(2)}) collective-permute-start(f32[2,128,128]{2,1,0:T(8,128)} %get-tuple-element.87), channel_id=1, source_target_pairs={{0,8},{4,12},{8,16},{12,20},{16,24},{20,28},{24,0},{28,4},{1,9},{5... | collective-permute-start | bytes 393224 | tf_op jit(solution)/shard_map/ppermute | solution.py:734
  137.3 21.7 %collective-permute-start.25 = (f32[2,128,128]{2,1,0:T(8,128)}, f32[2,128,128]{2,1,0:T(8,128)S(1)}, u32[]{:S(2)}, u32[]{:S(2)}) collective-permute-start(f32[2,128,128]{2,1,0:T(8,128)} %get-tuple-element.88), channel_id=1, source_target_pairs={{0,12},{4,16},{8,20},{12,24},{16,28},{20,0},{24,4},{28,8},{1,13},{... | collective-permute-start | bytes 393224 | tf_op jit(solution)/shard_map/ppermute | solution.py:734
  137.4 23.6 %collective-permute-start.26 = (f32[2,128,128]{2,1,0:T(8,128)}, f32[2,128,128]{2,1,0:T(8,128)S(1)}, u32[]{:S(2)}, u32[]{:S(2)}) collective-permute-start(f32[2,128,128]{2,1,0:T(8,128)} %get-tuple-element.89), channel_id=1, source_target_pairs={{0,16},{4,20},{8,24},{12,28},{16,0},{20,4},{24,8},{28,12},{1,17},{... | collective-permute-start | bytes 393224 | tf_op jit(solution)/shard_map/ppermute | solution.py:734
  138.8 22.3 %collective-permute-start.27 = (f32[2,128,128]{2,1,0:T(8,128)}, f32[2,128,128]{2,1,0:T(8,128)S(1)}, u32[]{:S(2)}, u32[]{:S(2)}) collective-permute-start(f32[2,128,128]{2,1,0:T(8,128)} %get-tuple-element.90), channel_id=1, source_target_pairs={{0,20},{4,24},{8,28},{12,0},{16,4},{20,8},{24,12},{28,16},{1,21},{... | collective-permute-start | bytes 393224 | tf_op jit(solution)/shard_map/ppermute | solution.py:734
  141.4 20.9 %collective-permute-start.28 = (f32[2,128,128]{2,1,0:T(8,128)}, f32[2,128,128]{2,1,0:T(8,128)S(1)}, u32[]{:S(2)}, u32[]{:S(2)}) collective-permute-start(f32[2,128,128]{2,1,0:T(8,128)} %get-tuple-element.91), channel_id=1, source_target_pairs={{0,24},{4,28},{8,0},{12,4},{16,8},{20,12},{24,16},{28,20},{1,25},{... | collective-permute-start | bytes 393224 | tf_op jit(solution)/shard_map/ppermute | solution.py:734
  155.4 7.4 %collective-permute-start.29 = (f32[2,128,128]{2,1,0:T(8,128)}, f32[2,128,128]{2,1,0:T(8,128)S(1)}, u32[]{:S(2)}, u32[]{:S(2)}) collective-permute-start(f32[2,128,128]{2,1,0:T(8,128)} %get-tuple-element.92), channel_id=1, source_target_pairs={{0,28},{4,0},{8,4},{12,8},{16,12},{20,16},{24,20},{28,24},{1,29},{... | collective-permute-start | bytes 393224 | tf_op jit(solution)/shard_map/ppermute | solution.py:734
  (9 other events, 102.9 us)

commit v3 on v2

--- a/solution.py
+++ b/solution.py
@@ -195,11 +195,7 @@
 HALF_LANES = 64
 LANES = 128
 SUB = 128
-FORWARD_CUTS = (4, 4)
-COPY_FIRST = False
-EARLY = (0,)
-COST = 1
-SECOND_AFTER = ()
+FORWARD_CUTS = (5, 3)
 FORWARD_LED = (False, False)
 BACKWARD_LED = (True, False)
 FORWARD_TILE = (True, False)
@@ -209,6 +205,9 @@
 ROW_VMEM = 14
 ANY = pl.ANY
 HBM = pltpu.HBM
+TABLES = HBM
+COPY_AFTER = 2
+FREE_MIDDLE = FREE_BACKWARD = True
 F32 = jnp.float32
 BF16 = jnp.bfloat16
 
@@ -341,9 +340,9 @@
         copy.wait()
 
 
-def gather_kernel(sizes, run, packed, after, lead, row_off, col_off, spectrum, *refs):
+def gather_kernel(sizes, run, packed, lead, row_off, col_off, spectrum, *refs):
     leds, tiles, band = sizes
-    outs, (staged, sems_in, sems_out, scalars, sems_scalar) = refs[after:-5], refs[-5:]
+    outs, (staged, sems_in, sems_out, scalars, sems_scalar) = refs[:-5], refs[-5:]
     me, tile = lax.axis_index("led"), lax.axis_index("tile")
     copies = [
         pltpu.make_async_copy(ref, scalars.at[n], sems_scalar.at[n])
@@ -441,8 +440,8 @@
     copies.append(
         pltpu.make_async_copy(pupil.at[:, run_first : run_first + rows], pupil_v, sems.at[leds])
     )
-    copies.append(pltpu.make_async_copy(table, table_v, sems.at[leds + 1]))
-    start_all(copies)
+    tables = [pltpu.make_async_copy(table.at[k], table_v.at[k], sems.at[leds + 1 + k]) for k in range(4)]
+    start_all(copies + tables)
     wait_all(copies)
     parts = []
     for a in range(4):
@@ -451,27 +450,33 @@
         cell_re, cell_im = window[0, :, cells], window[1, :, cells]
         parts.append((gate_re * cell_re - gate_im * cell_im, gate_re * cell_im + gate_im * cell_re))
     mixed = butterfly(parts, 1)
-    lines = [right_product(re, im, table_v[k]) for k, (re, im) in enumerate(mixed)]
     lane = lax.broadcasted_iota(jnp.int32, (rows, LANES), 1)
-    for other in range(tiles):
-        block = slice((other // 2) * LANES, (other // 2 + 1) * LANES)
-        for part in range(2):
-            for pair in range(2):
-                first, second = lines[2 * pair][part][:, block], lines[2 * pair + 1][part][:, block]
+    lines, leaving = [], []
+    for k in range(4):
+        tables[k].wait()
+        lines.append(right_product(*mixed[k], table_v[k]))
+        if k % 2 == 0:
+            continue
+        places = slice((k // 2) * LANES, (k // 2 + 1) * LANES)
+        for other in range(tiles):
+            block = slice((other // 2) * LANES, (other // 2 + 1) * LANES)
+            for part in range(2):
+                first, second = lines[k - 1][part][:, block], lines[k][part][:, block]
                 if other % 2:
                     first, second = second, first
-                result[other, part, :, pair * LANES : (pair + 1) * LANES] = jnp.where(
-                    lane < HALF_LANES, first, second
+                result[other, part, :, places] = jnp.where(lane < HALF_LANES, first, second)
+        for shift in range(tiles):
+            if packed:
+                source, target = result.at[shift], outs[0].at[shift]
+            else:
+                source, target = result.at[tile ^ shift], outs[shift]
+            leaving.append(
+                pltpu.make_async_copy(
+                    source.at[:, :, places], target.at[:, :, places], sems_out.at[shift, k // 2]
                 )
-    if packed:
-        copies = [pltpu.make_async_copy(result, outs[0], sems_out.at[0])]
-    else:
-        copies = [
-            pltpu.make_async_copy(result.at[tile ^ shift], outs[shift], sems_out.at[shift])
-            for shift in range(tiles)
-        ]
-    start_all(copies)
-    wait_all(copies)
+            )
+            leaving[-1].start()
+    wait_all(leaving)
 
 
 def tile_views(stack, run, packed, tile, tiles):
@@ -491,13 +496,25 @@
     blocks, outs = refs[: len(views)], refs[len(views) : -7]
     count = len(views)
     copies = [pltpu.make_async_copy(b, v, sems.at[n]) for n, (b, v) in enumerate(zip(blocks, views))]
-    copies.append(pltpu.make_async_copy(table, table_v, sems.at[count]))
-    copies.append(pltpu.make_async_copy(images, images_v, sems.at[count + 1]))
-    copies.append(pltpu.make_async_copy(table_back, back_v, sems.at[count + 2]))
+    later = [
+        [
+            pltpu.make_async_copy(table.at[k], table_v.at[k], sems.at[count + k]),
+            pltpu.make_async_copy(
+                images.at[k * QUARTER : (k + 1) * QUARTER],
+                images_v.at[k * QUARTER : (k + 1) * QUARTER],
+                sems.at[count + 4 + k],
+            ),
+            pltpu.make_async_copy(table_back.at[k], back_v.at[k], sems.at[count + 8 + k]),
+        ]
+        for k in range(4)
+    ]
     start_all(copies)
+    for group in later:
+        start_all(group)
     wait_all(copies)
     mixed = butterfly([(field[a, 0], field[a, 1]) for a in range(4)], 1)
     for k, (re, im) in enumerate(mixed):
+        wait_all(later[k])
         wave_re, wave_im = left_product(re, im, table_v[k])
         measured = images_v[k * QUARTER : (k + 1) * QUARTER, :]
         excess = wave_re * wave_re + wave_im * wave_im - measured
@@ -524,11 +541,9 @@
     me, tile = lax.axis_index("led"), lax.axis_index("tile")
     views = tile_views(lines, (0, rows), packed, tile, tiles)
     copies = [pltpu.make_async_copy(b, v, sems.at[n]) for n, (b, v) in enumerate(zip(blocks, views))]
-    copies.append(
-        pltpu.make_async_copy(pupil.at[:, run_first : run_first + rows], pupil_v, sems.at[tiles])
-    )
-    copies.append(pltpu.make_async_copy(table, table_v, sems.at[tiles + 1]))
-    start_all(copies)
+    gate = pltpu.make_async_copy(pupil.at[:, run_first : run_first + rows], pupil_v, sems.at[tiles])
+    tables = [pltpu.make_async_copy(table.at[k], table_v.at[k], sems.at[tiles + 1 + k]) for k in range(4)]
+    start_all(copies + tables + [gate])
     wait_all(copies)
     lane = lax.broadcasted_iota(jnp.int32, (rows, LANES), 1)
     parts = []
@@ -543,23 +558,32 @@
                     first, second = second, first
                 joined.append(jnp.where(lane < HALF_LANES, first, second))
             both.append(jnp.concatenate(joined, axis=1))
+        tables[k].wait()
         parts.append(right_product(both[0], both[1], table_v[k]))
+    gate.wait()
+    copies = []
     for a, (re, im) in enumerate(butterfly(parts, -1)):
         cells = slice(a * QUARTER, (a + 1) * QUARTER)
         gate_re, gate_im = pupil_v[0, :, cells], pupil_v[1, :, cells]
         result[0, :, cells] = gate_re * re + gate_im * im
         result[1, :, cells] = gate_re * im - gate_im * re
-    copies = []
-    for shift in range(leds):
         if led_packed:
-            first, target = shift * LANES, outs[0].at[shift]
-        else:
+            for led in range(2 * a, 2 * a + 2):
+                copies.append(
+                    pltpu.make_async_copy(
+                        result.at[:, :, led * LANES : (led + 1) * LANES], outs[0].at[led], sems_out.at[led]
+                    )
+                )
+                copies[-1].start()
+    if not led_packed:
+        for shift in range(leds):
             first = pl.multiple_of(lax.rem(me + shift, leds) * LANES, LANES)
-            target = outs[shift]
-        copies.append(
-            pltpu.make_async_copy(result.at[:, :, pl.ds(first, LANES)], target, sems_out.at[shift])
-        )
-    start_all(copies)
+            copies.append(
+                pltpu.make_async_copy(
+                    result.at[:, :, pl.ds(first, LANES)], outs[shift], sems_out.at[shift]
+                )
+            )
+        start_all(copies)
     wait_all(copies)
 
 
@@ -595,13 +619,15 @@
                     lines_at(spectrum, slot, n, part), cells_at(slot, n, part), sems_in.at[slot, n, part]
                 )
             )
-    for shift in range(leds):
+    grads_arriving = []
+    for slot in range(leds):
         if len(pieces) == 1:
-            arriving.append(pltpu.make_async_copy(pieces[0].at[shift], grads.at[shift], sems.at[shift]))
+            piece, place = pieces[0].at[slot], slot
         else:
-            slot = lax.rem(me - shift + leds, leds)
-            arriving.append(pltpu.make_async_copy(pieces[shift], grads.at[slot], sems.at[shift]))
+            piece, place = pieces[slot], lax.rem(me - slot + leds, leds)
+        grads_arriving.append(pltpu.make_async_copy(piece, grads.at[place], sems.at[place]))
     start_all(arriving)
+    start_all(grads_arriving)
     shared = jnp.bool_(False)
     is_first = []
     for slot in range(leds):
@@ -611,10 +637,12 @@
                 same = bases[earlier][n] == bases[slot][n]
                 shared = jnp.logical_or(shared, same)
                 is_first[slot][n] = jnp.logical_and(is_first[slot][n], jnp.logical_not(same))
-    wait_all(arriving)
+    each = len(every)
 
     @pl.when(shared)
     def _():
+        wait_all(arriving)
+        wait_all(grads_arriving)
         for n, (first, rows) in enumerate(spans):
             where = slice(first - run_first, first - run_first + rows)
             for slot in range(leds):
@@ -627,6 +655,13 @@
     for waiting in (False, True):
         for slot in range(leds):
             if not waiting:
+
+                @pl.when(jnp.logical_not(shared))
+                def _():
+                    wait_all(arriving[slot * each : (slot + 1) * each])
+                    source = pieces[0].at[slot] if len(pieces) == 1 else pieces[0]
+                    pltpu.make_async_copy(source, grads.at[slot], sems.at[slot]).wait()
+
                 cells[slot] = cells[slot] - STEP_SIZE * grads[slot]
             for n in range(len(spans)):
 
@@ -679,16 +714,16 @@
         copy_out(n).wait()
 
 
-def call(kernel, name, ins, outs, scratch, flops=0, moved=0, aliases=None, vmem=36):
+def call(kernel, name, ins, outs, scratch, flops=0, moved=0, aliases=None, vmem=36, free=False):
     run = pl.pallas_call(
         kernel,
         name=name,
-        out_shape=jax.tree.map(lambda o: HBM(o.shape, o.dtype), outs),
+        out_shape=outs if free else jax.tree.map(lambda o: HBM(o.shape, o.dtype), outs),
         in_specs=[pl.BlockSpec(memory_space=place) for place in ins],
-        out_specs=jax.tree.map(lambda _: pl.BlockSpec(memory_space=HBM), outs),
+        out_specs=jax.tree.map(lambda _: pl.BlockSpec(memory_space=ANY if free else HBM), outs),
         scratch_shapes=scratch,
         input_output_aliases=aliases or {},
-        cost_estimate=pl.CostEstimate(flops=COST * flops, bytes_accessed=COST * moved, transcendentals=0),
+        cost_estimate=pl.CostEstimate(flops=flops, bytes_accessed=moved, transcendentals=0),
         compiler_params=pltpu.CompilerParams(vmem_limit_bytes=vmem * 2**20),
     )
 
@@ -703,8 +738,8 @@
     return pinned
 
 
-def own_first(count):
-    return [ANY] if count == 1 else [HBM] + [ANY] * (count - 1)
+def own_first(count, free=False):
+    return [ANY] * count if count == 1 or free else [HBM] + [ANY] * (count - 1)
 
 
 def unit_shards(spectrum, intensities, led_of_slot, row_offset, col_offset, tile_mask, aberration):
@@ -755,16 +790,15 @@
 
     arrived = []
     for number, (run, packed) in enumerate(zip(forward_runs, FORWARD_LED)):
-        after = [arrived[0][shift] for shift in SECOND_AFTER] if number else []
         taken = call(
-            part(gather_kernel, sizes, run, packed, len(after)), f"gather_{number}",
-            [HBM] * 4 + [ANY] * len(after), pieces_of(run, packed),
+            part(gather_kernel, sizes, run, packed), f"gather_{number}",
+            [HBM] * 4, pieces_of(run, packed),
             [
                 pltpu.VMEM((leds, 2, run[1], LANES), F32), dma((leds, len(spans_of(run)), 2)), dma((leds,)),
                 pltpu.SMEM((3, leds), jnp.int32), dma((3,)),
             ],
             moved=2**22, vmem=8,
-        )(led_of_slot, row_offset, col_offset, flat, *after)
+        )(led_of_slot, row_offset, col_offset, flat)
         arrived.append(over_led(taken, packed))
     pupil, images = pl.pallas_call(
         part(prepare_kernel, sizes),
@@ -776,50 +810,49 @@
         compiler_params=pltpu.CompilerParams(vmem_limit_bytes=16 * 2**20),
         cost_estimate=pl.CostEstimate(flops=2 * 10**9, bytes_accessed=4 * 10**6, transcendentals=0),
     )(led_of_slot, row_offset, col_offset, tile_mask, aberration, intensities[0])
-    def copy_half(number, after, so_far):
-        lines = flat.shape[0] // 2
+    def copy_part(number, after, so_far, place=HBM, also=()):
+        lines = flat.shape[0] // 4
         return call(
             part(copy_kernel, number * lines, lines), f"copy_{number}",
-            [HBM] * (2 + len(so_far)), f32(*flat.shape),
+            [place] + [HBM] * (1 + len(so_far) + len(also)), f32(*flat.shape),
             [pltpu.VMEM((COPY_SLOTS, COPY_LINES, LANES), F32), dma((COPY_SLOTS,)), dma((COPY_SLOTS,))],
-            moved=4 * flat.size, aliases={2: 0} if so_far else None, vmem=16,
-        )(after, flat, *so_far)
+            moved=2 * flat.size, aliases={2: 0} if so_far else None, vmem=16,
+        )(after, flat, *so_far, *also)
 
     table_shape = (4, 4 * QUARTER, QUARTER)
     received, copied = [], None
     for number, (run, packed, pieces) in enumerate(zip(forward_runs, forward_packed, arrived)):
         rows = run[1]
-        early = ([copied] if COPY_FIRST else lines[:1]) if number else []
-        if number == 0:
-            early = [arrived[1][shift] for shift in EARLY]
+        so_far = [copied] if number else []
+        copied = copy_part(number, lines[0] if number else arrived[0][COPY_AFTER], so_far, HBM if number else ANY, () if number else arrived[1][:1])
+        early = [copied]
         pieces_count = len(pieces)
         lines = call(
-            part(forward_kernel, sizes, run, packed, pieces_count, len(early)), f"forward_{run[0]}", [HBM, ANY] + own_first(pieces_count) + [HBM] * len(early),
+            part(forward_kernel, sizes, run, packed, pieces_count, len(early)), f"forward_{run[0]}", [TABLES, ANY] + own_first(pieces_count) + [HBM] * len(early),
             blocks_of(run, packed),
             [
                 pltpu.VMEM(table_shape, BF16), pltpu.VMEM((2, rows, M), F32),
                 pltpu.VMEM((2, rows, M), F32), pltpu.VMEM((tiles, 2, rows, band), F32),
-                dma((leds + 2,)), dma((tiles,)),
+                dma((leds + 5,)), dma((tiles, 2)),
             ],
             flops=24 * rows * M * QUARTER, moved=2**23, vmem=ROW_VMEM,
         )(row_fwd, pupil, *pieces, *early)
         received += over_tile(lines, packed)
-        if number == (0 if COPY_FIRST else 1):
-            copied = copy_half(0, lines[0], [])
-
+
+    copied = copy_part(2, lines[0], [copied])
     arrays_in, arrays_out = len(received), sum(1 if p else tiles for p in backward_packed)
     returned = call(
         part(middle_kernel, sizes, list(zip(forward_runs, forward_packed)), list(zip(backward_runs, backward_packed))),
-        "middle", [HBM] * 2 + [ANY, HBM] + [HBM] * arrays_in,
+        "middle", [TABLES] * 2 + [ANY, HBM] + [HBM] * arrays_in,
         [b for run, packed in zip(backward_runs, backward_packed) for b in blocks_of(run, packed)],
         [
             pltpu.VMEM((4, QUARTER, 4 * QUARTER), BF16), pltpu.VMEM((4, QUARTER, 4 * QUARTER), BF16),
             pltpu.VMEM((M, band), F32), pltpu.VMEM((4, 2, QUARTER, band), F32),
-            pltpu.VMEM((4, 2, QUARTER, band), F32), dma((arrays_in + 3,)), dma((arrays_out,)),
+            pltpu.VMEM((4, 2, QUARTER, band), F32), dma((arrays_in + 12,)), dma((arrays_out,)),
         ],
-        flops=48 * band * M * QUARTER, moved=2**24, vmem=MIDDLE_VMEM,
+        flops=48 * band * M * QUARTER, moved=2**24, vmem=MIDDLE_VMEM, free=FREE_MIDDLE,
     )(col_fwd, col_bwd, images, copied, *received)
-    updated = copy_half(1, returned[0], [copied])
+    updated = copy_part(3, returned[0], [copied], ANY if FREE_MIDDLE else HBM)
     count = 1 if backward_packed[0] else tiles
     returned, later = returned[:count], returned[count:]
     for number, (run, packed, led_packed) in enumerate(zip(backward_runs, backward_packed, BACKWARD_LED)):
@@ -830,21 +863,21 @@
         count = len(lines)
         results = call(
             part(backward_kernel, sizes, run, packed, led_packed, len(held + through)), f"backward_{run[0]}",
-            [HBM, ANY] + own_first(count) + [ANY] * len(held) + [HBM] * len(through),
+            [TABLES, ANY] + own_first(count, FREE_MIDDLE) + [ANY] * len(held) + [HBM] * len(through),
             pieces_of(run, led_packed) + [f32(*h.shape) for h in held + through],
             [
                 pltpu.VMEM(table_shape, BF16), pltpu.VMEM((2, rows, M), F32),
                 pltpu.VMEM((tiles, 2, rows, band), F32), pltpu.VMEM((2, rows, M), F32),
-                dma((tiles + 2,)), dma((leds,)),
+                dma((tiles + 5,)), dma((leds,)),
             ],
-            flops=24 * rows * M * QUARTER, moved=2**23, vmem=ROW_VMEM,
+            flops=24 * rows * M * QUARTER, moved=2**23, vmem=ROW_VMEM, free=FREE_BACKWARD and not (led_packed or through),
             aliases={2 + count + n: sent + n for n in range(len(held + through))},
         )(row_bwd, pupil, *lines, *held, *through)
         pieces, later = over_led(results[:sent], led_packed), results[sent : sent + len(held)]
         updated = results[-1] if through else updated
         spans = len(spans_of(run))
         updated = call(
-            part(update_kernel, sizes, run), f"update_{run[0]}", [smem] * 3 + [HBM] * 2 + own_first(sent),
+            part(update_kernel, sizes, run), f"update_{run[0]}", [smem] * 3 + [HBM] * 2 + own_first(sent, FREE_BACKWARD and not led_packed),
             f32(*flat.shape),
             [
                 pltpu.VMEM((leds, 2, rows, LANES), F32), pltpu.VMEM((leds, 2, rows, LANES), F32),

time: 167 us -> 163 us (0.976)
  waiting for transfers between devices: 60.9 us -> 53.5 us
  starting transfers between devices: 38.1 us -> 39.8 us
    ppermute x21, waiting for transfers between devices: 49.3 us -> 34.2 us  [over_led(): lax.ppermute(arrays[shift], 'led', [(i, (i + shift) % leds) for i in rang...]
    ppermute x9, waiting for transfers between devices: 11.6 us -> 19.3 us  [over_tile(): lax.ppermute(arrays[shift], 'tile', [(i, i ^ shift) for i in range(tiles)])]
    pallas_call x11 -> x13, Pallas kernels: 62.9 us -> 62.9 us  [pinned(): run(*(pltpu.with_memory_space_constraint(x, HBM) if place == HBM else x f...]
  transfers between devices with their start and end apart: 32 -> 32, of which waited for: 16 -> 18; matrix products, arithmetic and copies ran while one was open for 0% -> 0% of each run, Pallas kernels for 26% -> 27%
where the time goes in v3:
time: 163 us; the launch traced here: 161 us
  Pallas kernels  66.5 us (41%)
  waiting for transfers between devices  53.5 us (33%)
  starting transfers between devices  39.8 us (24%)
    pallas_call x13, Pallas kernels, pinned(): run(*(pltpu.with_memory_space_constraint(x, HBM) if place == HBM else x f...  62.9 us
    ppermute x21, waiting for transfers between devices, over_led(): lax.ppermute(arrays[shift], 'led', [(i, (i + shift) % leds) for i in rang...  34.2 us
    ppermute x21, starting transfers between devices, over_led(): lax.ppermute(arrays[shift], 'led', [(i, (i + shift) % leds) for i in rang...  22.5 us
    ppermute x9, waiting for transfers between devices, over_tile(): lax.ppermute(arrays[shift], 'tile', [(i, i ^ shift) for i in range(tiles)])  19.3 us
    ppermute x9, starting transfers between devices, over_tile(): lax.ppermute(arrays[shift], 'tile', [(i, i ^ shift) for i in range(tiles)])  8.09 us
    all_to_all x1, starting transfers between devices, over_led(): lax.all_to_all(arrays[0], 'led', split_axis=0, concat_axis=0, tiled=True)  4.92 us
    all_to_all x1, starting transfers between devices, over_tile(): lax.all_to_all(arrays[0], 'tile', split_axis=0, concat_axis=0, tiled=True)  4.3 us
    pallas_call x1, Pallas kernels, unit_shards(): pl.pallas_call(part(prepare_kernel, sizes), name='prepare', out_shape=[f3...  3.59 us
  transfers between devices with their start and end apart: 32, of which 18 were waited for; matrix products, arithmetic and copies ran while one was open for 0% of the time, Pallas kernels for 27%

profile of v3, /device:TPU:11, one launch (start us, length us, event | category | flops | bytes accessed | tf_op | source)
XLA Modules:
  0.0 161.4 jit_solution(15710067317282412044)
XLA Ops:
  0.0 3.3 %gather_0.1 = (f32[2,160,128]{2,1,0:T(8,128)}, f32[2,160,128]{2,1,0:T(8,128)}, f32[2,160,128]{2,1,0:T(8,128)}, f32[2,160,128]{2,1,0:T(8,128)}, f32[2,160,128]{2,...) custom-call(s32[8]{0:T(128)} %lead.9, s32[8]{0:T(128)} %row_off.9, ...), custom_call_target="tpu_custom_call" | custom-call | bytes 4194304 | tf_op jit(solution)/shard_map/gather_0/pallas_call | solution.py:731
  3.3 2.1 %collective-permute-start.7 = (f32[2,160,128]{2,1,0:T(8,128)}, f32[2,160,128]{2,1,0:T(8,128)S(1)}, u32[]{:S(2)}, u32[]{:S(2)}) collective-permute-start(f32[2,160,128]{2,1,0:T(8,128)} %get-tuple-element.60), channel_id=1, source_target_pairs={{0,4},{4,8},{8,12},{12,16},{16,20},{20,24},{24,28},{28,0},{1,5},{5... | collective-permute-start | bytes 491528 | tf_op jit(solution)/shard_map/ppermute | solution.py:769
  9.5 2.7 %gather_1.1 = (f32[2,96,128]{2,1,0:T(8,128)}, f32[2,96,128]{2,1,0:T(8,128)}, f32[2,96,128]{2,1,0:T(8,128)}, f32[2,96,128]{2,1,0:T(8,128)}, f32[2,96,128]{2,1,0:T...) custom-call(s32[8]{0:T(128)} %lead.9, s32[8]{0:T(128)} %row_off.9, s32[8]{0:T(128)} %col_off.9, ...), custom_call_target="tpu_custom_call" | custom-call | bytes 4194304 | tf_op jit(solution)/shard_map/gather_1/pallas_call | solution.py:731
  14.0 3.6 %prepare.1 = (f32[2,256,1024]{2,1,0:T(8,128)S(1)}, f32[1024,256]{1,0:T(8,128)S(1)}) custom-call(s32[8]{0:T(128)S(1)} %copy-done.5, s32[8]{0:T(128)S(1)} %copy-done.7, s32[8]{0:T(128)S(1)} %copy-done.9, s32[8,8,8]{2,1,0:T(8,128)S(1)} %copy-done.12, f32[5]{0:T(128)S(1)} %copy-done.13, bf16[256,1024]{1,0:T(8,128)(2,1)S(1)} %bitcast.3), custom_call_target="tpu_custom_call" | custom-call | flops 2000000000 | bytes 4000000 | tf_op jit(solution)/shard_map/prepare/pallas_call | solution.py:803
  17.6 6.6 %copy_0.1.refs_8_.refs_0_ = f32[65536,128]{1,0:T(8,128)} custom-call(f32[2,160,128]{2,1,0:T(8,128)S(1)} %collective-permute-done.8.after.refs_2_, f32[65536,128]{1,0:T(8,128)} %bitcast.6, f32[2,96,128]{2,1,0:T(8,128)} %get-tuple-element.51.refs_0_), custom_call_target="tpu_custom_call" | custom-call | bytes 16777216 | tf_op jit(solution)/shard_map/copy_0/pallas_call | solution.py:731
  24.2 6.0 %collective-permute-done.9.refs_3_ = f32[2,160,128]{2,1,0:T(8,128)S(1)} collective-permute-done((f32[2,160,128]{2,1,0:T(8,128)}, f32[2,160,128]{2,1,0:T(8,128)S(1)}, u32[]{:S(2)}, u32[]{:S(2)}) %collective-permute-start.9) | collective-permute-done | bytes 163872 | tf_op jit(solution)/shard_map/ppermute | solution.py:769
  30.2 3.5 %collective-permute-done.10.refs_4_ = f32[2,160,128]{2,1,0:T(8,128)S(1)} collective-permute-done((f32[2,160,128]{2,1,0:T(8,128)}, f32[2,160,128]{2,1,0:T(8,128)S(1)}, u32[]{:S(2)}, u32[]{:S(2)}) %collective-permute-start.10) | collective-permute-done | bytes 163872 | tf_op jit(solution)/shard_map/ppermute | solution.py:769
  33.7 1.7 %collective-permute-done.12.refs_6_ = f32[2,160,128]{2,1,0:T(8,128)S(1)} collective-permute-done((f32[2,160,128]{2,1,0:T(8,128)S(1)}, f32[2,160,128]{2,1,0:T(8,128)S(1)}, u32[]{:S(2)}, u32[]{:S(2)}) %collective-permute-start.12) | collective-permute-done | bytes 163872 | tf_op jit(solution)/shard_map/ppermute | solution.py:769
  35.5 4.4 %forward_0.1.after = f32[4,2,160,256]{3,2,1,0:T(8,128)} custom-call(bf16[4,1024,256]{2,1,0:T(8,128)(2,1)} %constant.8.clone.table, f32[2,256,1024]{2,1,0:T(8,128)S(1)} %get-tuple-element.49.pupil, f32[2,160,128]{2,1,0:T(8,128)} %get-tuple-element.59.refs_0_, f32[2,160,128]{2,1,0:T(8,128)S(1)} %collective-permute-done.7.refs_1_, ...), custom_call_target="tpu_custom_call" | custom-call | flops 1006632960 | bytes 8388608 | tf_op jit(solution)/shard_map/forward_0/pallas_call | solution.py:731
  39.9 4.3 %all-to-all-start = ((f32[4,2,160,256]{3,2,1,0:T(8,128)}), f32[4,2,160,256]{3,2,1,0:T(8,128)}, u32[]{:S(2)}, u32[]{:S(2)}) async-start(f32[4,2,160,256]{3,2,1,0:T(8,128)} %forward_0.1.after), calls=%async_computation | async-start | bytes 2621440 | tf_op jit(solution)/shard_map/all_to_all | solution.py:775
  44.3 2.0 %collective-permute-start.2 = (f32[2,96,128]{2,1,0:T(8,128)}, f32[2,96,128]{2,1,0:T(8,128)S(1)}, u32[]{:S(2)}, u32[]{:S(2)}) collective-permute-start(f32[2,96,128]{2,1,0:T(8,128)} %get-tuple-element.54), channel_id=1, source_target_pairs={{0,12},{4,16},{8,20},{12,24},{16,28},{20,0},{24,4},{28,8},{1,13},{... | collective-permute-start | bytes 294920 | tf_op jit(solution)/shard_map/ppermute | solution.py:769
  47.4 2.0 %collective-permute-start.4 = (f32[2,96,128]{2,1,0:T(8,128)S(1)}, f32[2,96,128]{2,1,0:T(8,128)S(1)}, u32[]{:S(2)}, u32[]{:S(2)}) collective-permute-start(f32[2,96,128]{2,1,0:T(8,128)S(1)} %copy-done.20), channel_id=1, source_target_pairs={{0,20},{4,24},{8,28},{12,0},{16,4},{20,8},{24,12},{28,16},{1,21},{... | collective-permute-start | bytes 294920 | tf_op jit(solution)/shard_map/ppermute | solution.py:769
  51.1 6.6 %copy_1.1.refs_8_.refs_0_ = f32[65536,128]{1,0:T(8,128)} custom-call(f32[4,2,160,256]{3,2,1,0:T(8,128)} %forward_0.1.after, f32[65536,128]{1,0:T(8,128)} %bitcast.7, f32[65536,128]{1,0:T(8,128)} %copy_0.1.refs_8_.refs_0_), custom_call_target="tpu_custom_call", output_to_operand_aliasing={{}: (2, {})} | custom-call | bytes 16777216 | tf_op jit(solution)/shard_map/copy_1/pallas_call | solution.py:731
  59.0 2.1 %collective-permute-done.3.refs_4_ = f32[2,96,128]{2,1,0:T(8,128)S(1)} collective-permute-done((f32[2,96,128]{2,1,0:T(8,128)S(1)}, f32[2,96,128]{2,1,0:T(8,128)S(1)}, u32[]{:S(2)}, u32[]{:S(2)}) %collective-permute-start.3) | collective-permute-done | bytes 98336 | tf_op jit(solution)/shard_map/ppermute | solution.py:769
  61.2 2.7 %collective-permute-done.5.refs_6_ = f32[2,96,128]{2,1,0:T(8,128)S(1)} collective-permute-done((f32[2,96,128]{2,1,0:T(8,128)S(1)}, f32[2,96,128]{2,1,0:T(8,128)S(1)}, u32[]{:S(2)}, u32[]{:S(2)}) %collective-permute-start.5) | collective-permute-done | bytes 98336 | tf_op jit(solution)/shard_map/ppermute | solution.py:769
  64.0 3.8 %forward_160.1 = (f32[2,96,256]{2,1,0:T(8,128)}, f32[2,96,256]{2,1,0:T(8,128)}, f32[2,96,256]{2,1,0:T(8,128)}, f32[2,96,256]{2,1,0:T(8,128)}) custom-call(bf16[4,1024,256]{2,1,0:T(8,128)(2,1)} %constant.8.clone.table, f32[2,256,1024]{2,1,0:T(8,128)S(1)} %get-tuple-element.49.pupil, f32[2,96,128]{2,1,0:T(8,128)} %get-tuple-element.51.refs_0_, ...), custom_call_target="tpu_custom_call" | custom-call | flops 603979776 | bytes 8388608 | tf_op jit(solution)/shard_map/forward_160/pallas_call | solution.py:731
  70.4 6.6 %copy_2.1.copied.refs_0_ = f32[65536,128]{1,0:T(8,128)} custom-call(f32[2,96,256]{2,1,0:T(8,128)} %get-tuple-element.67.after.refs_1_, f32[65536,128]{1,0:T(8,128)} %bitcast.8, f32[65536,128]{1,0:T(8,128)} %copy_1.1.refs_8_.refs_0_), custom_call_target="tpu_custom_call", output_to_operand_aliasing={{}: (2, {})} | custom-call | bytes 16777216 | tf_op jit(solution)/shard_map/copy_2/pallas_call | solution.py:731
  78.9 7.0 %middle.1 = (f32[2,128,256]{2,1,0:T(8,128)S(1)}, f32[2,128,256]{2,1,0:T(8,128)S(1)}, f32[2,128,256]{2,1,0:T(8,128)S(1)}, f32[2,128,256]{2,1,0:T(8,128)S(1)}, f32...) custom-call(bf16[4,256,1024]{2,1,0:T(8,128)(2,1)} %constant.10.clone, ...), custom_call_target="tpu_custom_call" | custom-call | flops 3221225472 | bytes 16777216 | tf_op jit(solution)/shard_map/middle/pallas_call | solution.py:731
  88.7 6.6 %copy_3.1.refs_8_ = f32[65536,128]{1,0:T(8,128)} custom-call(f32[2,128,256]{2,1,0:T(8,128)S(1)} %get-tuple-element.71.after.refs_0_, f32[65536,128]{1,0:T(8,128)} %bitcast.9, f32[65536,128]{1,0:T(8,128)} %copy_2.1.copied.refs_0_), custom_call_target="tpu_custom_call", output_to_operand_aliasing={{}: (2, {})} | custom-call | bytes 16777216 | tf_op jit(solution)/shard_map/copy_3/pallas_call | solution.py:731
  95.4 4.1 %collective-permute-done.18.refs_2_ = f32[2,128,256]{2,1,0:T(8,128)S(1)} collective-permute-done((f32[2,128,256]{2,1,0:T(8,128)S(1)}, f32[2,128,256]{2,1,0:T(8,128)S(1)}, u32[]{:S(2)}, u32[]{:S(2)}) %collective-permute-start.18) | collective-permute-done | bytes 262176 | tf_op jit(solution)/shard_map/ppermute | solution.py:778
  99.4 1.7 %collective-permute-done.19.refs_3_ = f32[2,128,256]{2,1,0:T(8,128)S(1)} collective-permute-done((f32[2,128,256]{2,1,0:T(8,128)S(1)}, f32[2,128,256]{2,1,0:T(8,128)S(1)}, u32[]{:S(2)}, u32[]{:S(2)}) %collective-permute-start.19) | collective-permute-done | bytes 262176 | tf_op jit(solution)/shard_map/ppermute | solution.py:778
  101.1 4.0 %backward_0.1 = (f32[8,2,128,128]{3,2,1,0:T(8,128)}, f32[2,128,256]{2,1,0:T(8,128)}, f32[2,128,256]{2,1,0:T(8,128)}, f32[2,128,256]{2,1,0:T(8,128)}, f32[2,128,256]{2,1,0:T(8,128)}, /*index=5*/f32[65536,128]{1,0:T(8,128)}) custom-call(bf16[4,1024,256]{2,1,0:T(8,128)(2,1)} %constant.9.clone., ...), custom_call_target="tpu_custom_call", output_to_operand_aliasing={{1}: (6, {}), {2}: (7, {}), {3}: (8, {}), {4}: (9, {}), {5}... | custom-call | flops 805306368 | bytes 8388608 | tf_op jit(solution)/shard_map/backward_0/pallas_call | solution.py:731
  105.2 4.9 %all-to-all-start.1 = ((f32[8,2,128,128]{3,2,1,0:T(8,128)}), f32[8,2,128,128]{3,2,1,0:T(8,128)S(1)}, u32[]{:S(2)}, u32[]{:S(2)}) async-start(f32[8,2,128,128]{3,2,1,0:T(8,128)} %get-tuple-element.80), calls=%async_computation.1 | async-start | bytes 2097152 | tf_op jit(solution)/shard_map/all_to_all | solution.py:765
  112.7 5.1 %collective-permute-done.20.refs_1_ = f32[2,128,256]{2,1,0:T(8,128)S(1)} collective-permute-done((f32[2,128,256]{2,1,0:T(8,128)}, f32[2,128,256]{2,1,0:T(8,128)S(1)}, u32[]{:S(2)}, u32[]{:S(2)}) %collective-permute-start.20) | collective-permute-done | bytes 262176 | tf_op jit(solution)/shard_map/ppermute | solution.py:778
  118.4 5.9 %collective-permute-done.22.refs_3_ = f32[2,128,256]{2,1,0:T(8,128)S(1)} collective-permute-done((f32[2,128,256]{2,1,0:T(8,128)}, f32[2,128,256]{2,1,0:T(8,128)S(1)}, u32[]{:S(2)}, u32[]{:S(2)}) %collective-permute-start.22) | collective-permute-done | bytes 262176 | tf_op jit(solution)/shard_map/ppermute | solution.py:778
  125.3 4.0 %backward_128.1 = (f32[2,128,128]{2,1,0:T(8,128)S(1)}, f32[2,128,128]{2,1,0:T(8,128)S(1)}, f32[2,128,128]{2,1,0:T(8,128)S(1)}, f32[2,128,128]{2,1,0:T(8,128)}, f...) custom-call(bf16[4,1024,256]{2,1,0:T(8,128)(2,1)} %constant.9.clone.tab, ...), custom_call_target="tpu_custom_call" | custom-call | flops 805306368 | bytes 8388608 | tf_op jit(solution)/shard_map/backward_128/pallas_call | solution.py:731
  129.4 2.3 %collective-permute-start.23 = (f32[2,128,128]{2,1,0:T(8,128)S(1)}, f32[2,128,128]{2,1,0:T(8,128)S(1)}, u32[]{:S(2)}, u32[]{:S(2)}) collective-permute-start(f32[2,128,128]{2,1,0:T(8,128)S(1)} %get-tuple-element.86), channel_id=1, source_target_pairs={{0,4},{4,8},{8,12},{12,16},{16,20},{20,24},{24,28},{28,0},{1,5},{5... | collective-permute-start | bytes 393224 | tf_op jit(solution)/shard_map/ppermute | solution.py:769
  134.4 1.6 %collective-permute-start.27 = (f32[2,128,128]{2,1,0:T(8,128)}, f32[2,128,128]{2,1,0:T(8,128)S(1)}, u32[]{:S(2)}, u32[]{:S(2)}) collective-permute-start(f32[2,128,128]{2,1,0:T(8,128)} %get-tuple-element.90), channel_id=1, source_target_pairs={{0,20},{4,24},{8,28},{12,0},{16,4},{20,8},{24,12},{28,16},{1,21},{... | collective-permute-start | bytes 393224 | tf_op jit(solution)/shard_map/ppermute | solution.py:769
  137.1 12.6 %collective-permute-done.24.refs_2_ = f32[2,128,128]{2,1,0:T(8,128)S(1)} collective-permute-done((f32[2,128,128]{2,1,0:T(8,128)S(1)}, f32[2,128,128]{2,1,0:T(8,128)S(1)}, u32[]{:S(2)}, u32[]{:S(2)}) %collective-permute-start.24) | collective-permute-done | bytes 131104 | tf_op jit(solution)/shard_map/ppermute | solution.py:769
  149.7 3.5 %update_0.1.buffer = f32[65536,128]{1,0:T(8,128)} custom-call(s32[8]{0:T(128)S(1)} %copy-done.6, s32[8]{0:T(128)S(1)} %copy-done.8, s32[8]{0:T(128)S(1)} %copy-done.10, f32[65536,128]{1,0:T(8,128)} %bitcast.10, f32[65536,128]{1,0:T(8,128)} %get-tuple-element.79.buffer, f32[8,2,128,128]{3,2,1,0:T(8,128)S(1)} %all-to-all-done.1.refs_0_), custom_call_target="tpu_custom_call", output_to_operand_aliasing={{}: (4, {})} | custom-call | bytes 4194304 | tf_op jit(solution)/shard_map/update_0/pallas_call | solution.py:731
  153.3 2.3 %collective-permute-done.26.refs_4_ = f32[2,128,128]{2,1,0:T(8,128)S(1)} collective-permute-done((f32[2,128,128]{2,1,0:T(8,128)}, f32[2,128,128]{2,1,0:T(8,128)S(1)}, u32[]{:S(2)}, u32[]{:S(2)}) %collective-permute-start.26) | collective-permute-done | bytes 131104 | tf_op jit(solution)/shard_map/ppermute | solution.py:769
  157.3 3.8 %update_128.1 = f32[65536,128]{1,0:T(8,128)} custom-call(s32[8]{0:T(128)S(1)} %copy-done.6, s32[8]{0:T(128)S(1)} %copy-done.8, s32[8]{0:T(128)S(1)} %copy-done.10, f32[65536,128]{1,0:T(8,128)} %bitcast.11, f32[65536,128]{1,0:T(8,128)} %update_0.1.buffer, f32[2,128,128]{2,1,0:T(8,128)S(1)} %get-tuple-element.85.refs_0_, ...), custom_call_target="tpu_custom_call", output_to_operand_aliasing={{}: (4, {})} | custom-call | bytes 4194304 | tf_op jit(solution)/shard_map/update_128/pallas_call | solution.py:731
  (90 shorter events, 27.3 us)
Async XLA Ops:
  3.3 8.9 %collective-permute-start.7 = (f32[2,160,128]{2,1,0:T(8,128)}, f32[2,160,128]{2,1,0:T(8,128)S(1)}, u32[]{:S(2)}, u32[]{:S(2)}) collective-permute-start(f32[2,160,128]{2,1,0:T(8,128)} %get-tuple-element.60), channel_id=1, source_target_pairs={{0,4},{4,8},{8,12},{12,16},{16,20},{20,24},{24,28},{28,0},{1,5},{5... | collective-permute-start | bytes 491528 | tf_op jit(solution)/shard_map/ppermute | solution.py:769
  5.4 8.1 %collective-permute-start.8 = (f32[2,160,128]{2,1,0:T(8,128)}, f32[2,160,128]{2,1,0:T(8,128)S(1)}, u32[]{:S(2)}, u32[]{:S(2)}) collective-permute-start(f32[2,160,128]{2,1,0:T(8,128)} %get-tuple-element.61), channel_id=1, source_target_pairs={{0,8},{4,12},{8,16},{12,20},{16,24},{20,28},{24,0},{28,4},{1,9},{5... | collective-permute-start | bytes 491528 | tf_op jit(solution)/shard_map/ppermute | solution.py:769
  6.5 23.7 %collective-permute-start.9 = (f32[2,160,128]{2,1,0:T(8,128)}, f32[2,160,128]{2,1,0:T(8,128)S(1)}, u32[]{:S(2)}, u32[]{:S(2)}) collective-permute-start(f32[2,160,128]{2,1,0:T(8,128)} %get-tuple-element.62), channel_id=1, source_target_pairs={{0,12},{4,16},{8,20},{12,24},{16,28},{20,0},{24,4},{28,8},{1,13},{... | collective-permute-start | bytes 491528 | tf_op jit(solution)/shard_map/ppermute | solution.py:769
  6.5 27.2 %collective-permute-start.10 = (f32[2,160,128]{2,1,0:T(8,128)}, f32[2,160,128]{2,1,0:T(8,128)S(1)}, u32[]{:S(2)}, u32[]{:S(2)}) collective-permute-start(f32[2,160,128]{2,1,0:T(8,128)} %get-tuple-element.63), channel_id=1, source_target_pairs={{0,16},{4,20},{8,24},{12,28},{16,0},{20,4},{24,8},{28,12},{1,17},{... | collective-permute-start | bytes 491528 | tf_op jit(solution)/shard_map/ppermute | solution.py:769
  8.1 25.6 %collective-permute-start.11 = (f32[2,160,128]{2,1,0:T(8,128)}, f32[2,160,128]{2,1,0:T(8,128)S(1)}, u32[]{:S(2)}, u32[]{:S(2)}) collective-permute-start(f32[2,160,128]{2,1,0:T(8,128)} %get-tuple-element.64), channel_id=1, source_target_pairs={{0,20},{4,24},{8,28},{12,0},{16,4},{20,8},{24,12},{28,16},{1,21},{... | collective-permute-start | bytes 491528 | tf_op jit(solution)/shard_map/ppermute | solution.py:769
  12.3 23.1 %collective-permute-start.12 = (f32[2,160,128]{2,1,0:T(8,128)S(1)}, f32[2,160,128]{2,1,0:T(8,128)S(1)}, u32[]{:S(2)}, u32[]{:S(2)}) collective-permute-start(f32[2,160,128]{2,1,0:T(8,128)S(1)} %copy-done.17), channel_id=1, source_target_pairs={{0,24},{4,28},{8,0},{12,4},{16,8},{20,12},{24,16},{28,20},{1,25},{... | collective-permute-start | bytes 491528 | tf_op jit(solution)/shard_map/ppermute | solution.py:769
  13.5 22.0 %collective-permute-start.13 = (f32[2,160,128]{2,1,0:T(8,128)S(1)}, f32[2,160,128]{2,1,0:T(8,128)S(1)}, u32[]{:S(2)}, u32[]{:S(2)}) collective-permute-start(f32[2,160,128]{2,1,0:T(8,128)S(1)} %copy-done.16), channel_id=1, source_target_pairs={{0,28},{4,0},{8,4},{12,8},{16,12},{20,16},{24,20},{28,24},{1,29},{... | collective-permute-start | bytes 491528 | tf_op jit(solution)/shard_map/ppermute | solution.py:769
  39.9 39.0 %all-to-all-start = ((f32[4,2,160,256]{3,2,1,0:T(8,128)}), f32[4,2,160,256]{3,2,1,0:T(8,128)}, u32[]{:S(2)}, u32[]{:S(2)}) async-start(f32[4,2,160,256]{3,2,1,0:T(8,128)} %forward_0.1.after), calls=%async_computation | async-start | bytes 2621440 | tf_op jit(solution)/shard_map/all_to_all | solution.py:775
  44.2 5.2 %collective-permute-start = (f32[2,96,128]{2,1,0:T(8,128)}, f32[2,96,128]{2,1,0:T(8,128)S(1)}, u32[]{:S(2)}, u32[]{:S(2)}) collective-permute-start(f32[2,96,128]{2,1,0:T(8,128)} %get-tuple-element.52), channel_id=1, source_target_pairs={{0,4},{4,8},{8,12},{12,16},{16,20},{20,24},{24,28},{28,0},{1,5},{5... | collective-permute-start | bytes 294920 | tf_op jit(solution)/shard_map/ppermute | solution.py:769
  44.2 6.1 %collective-permute-start.1 = (f32[2,96,128]{2,1,0:T(8,128)}, f32[2,96,128]{2,1,0:T(8,128)S(1)}, u32[]{:S(2)}, u32[]{:S(2)}) collective-permute-start(f32[2,96,128]{2,1,0:T(8,128)} %get-tuple-element.53), channel_id=1, source_target_pairs={{0,8},{4,12},{8,16},{12,20},{16,24},{20,28},{24,0},{28,4},{1,9},{5... | collective-permute-start | bytes 294920 | tf_op jit(solution)/shard_map/ppermute | solution.py:769
  44.3 14.7 %collective-permute-start.2 = (f32[2,96,128]{2,1,0:T(8,128)}, f32[2,96,128]{2,1,0:T(8,128)S(1)}, u32[]{:S(2)}, u32[]{:S(2)}) collective-permute-start(f32[2,96,128]{2,1,0:T(8,128)} %get-tuple-element.54), channel_id=1, source_target_pairs={{0,12},{4,16},{8,20},{12,24},{16,28},{20,0},{24,4},{28,8},{1,13},{... | collective-permute-start | bytes 294920 | tf_op jit(solution)/shard_map/ppermute | solution.py:769
  46.3 14.8 %collective-permute-start.3 = (f32[2,96,128]{2,1,0:T(8,128)S(1)}, f32[2,96,128]{2,1,0:T(8,128)S(1)}, u32[]{:S(2)}, u32[]{:S(2)}) collective-permute-start(f32[2,96,128]{2,1,0:T(8,128)S(1)} %copy-done.21), channel_id=1, source_target_pairs={{0,16},{4,20},{8,24},{12,28},{16,0},{20,4},{24,8},{28,12},{1,17},{... | collective-permute-start | bytes 294920 | tf_op jit(solution)/shard_map/ppermute | solution.py:769
  47.4 13.8 %collective-permute-start.4 = (f32[2,96,128]{2,1,0:T(8,128)S(1)}, f32[2,96,128]{2,1,0:T(8,128)S(1)}, u32[]{:S(2)}, u32[]{:S(2)}) collective-permute-start(f32[2,96,128]{2,1,0:T(8,128)S(1)} %copy-done.20), channel_id=1, source_target_pairs={{0,20},{4,24},{8,28},{12,0},{16,4},{20,8},{24,12},{28,16},{1,21},{... | collective-permute-start | bytes 294920 | tf_op jit(solution)/shard_map/ppermute | solution.py:769
  49.4 14.5 %collective-permute-start.5 = (f32[2,96,128]{2,1,0:T(8,128)S(1)}, f32[2,96,128]{2,1,0:T(8,128)S(1)}, u32[]{:S(2)}, u32[]{:S(2)}) collective-permute-start(f32[2,96,128]{2,1,0:T(8,128)S(1)} %copy-done.19), channel_id=1, source_target_pairs={{0,24},{4,28},{8,0},{12,4},{16,8},{20,12},{24,16},{28,20},{1,25},{... | collective-permute-start | bytes 294920 | tf_op jit(solution)/shard_map/ppermute | solution.py:769
  50.3 13.6 %collective-permute-start.6 = (f32[2,96,128]{2,1,0:T(8,128)S(1)}, f32[2,96,128]{2,1,0:T(8,128)S(1)}, u32[]{:S(2)}, u32[]{:S(2)}) collective-permute-start(f32[2,96,128]{2,1,0:T(8,128)S(1)} %copy-done.18), channel_id=1, source_target_pairs={{0,28},{4,0},{8,4},{12,8},{16,12},{20,16},{24,20},{28,24},{1,29},{... | collective-permute-start | bytes 294920 | tf_op jit(solution)/shard_map/ppermute | solution.py:769
  67.7 9.3 %collective-permute-start.14 = (f32[2,96,256]{2,1,0:T(8,128)}, f32[2,96,256]{2,1,0:T(8,128)S(1)}, u32[]{:S(2)}, u32[]{:S(2)}) collective-permute-start(f32[2,96,256]{2,1,0:T(8,128)} %get-tuple-element.68), channel_id=1, source_target_pairs={{0,1},{1,0},{2,3},{3,2},{4,5},{5,4},{6,7},{7,6},{8,9},{9,8},{10,11... | collective-permute-start | bytes 589832 | tf_op jit(solution)/shard_map/ppermute | solution.py:778
  67.9 10.0 %collective-permute-start.15 = (f32[2,96,256]{2,1,0:T(8,128)}, f32[2,96,256]{2,1,0:T(8,128)S(1)}, u32[]{:S(2)}, u32[]{:S(2)}) collective-permute-start(f32[2,96,256]{2,1,0:T(8,128)} %get-tuple-element.69), channel_id=1, source_target_pairs={{0,2},{1,3},{2,0},{3,1},{4,6},{5,7},{6,4},{7,5},{8,10},{9,11},{10,... | collective-permute-start | bytes 589832 | tf_op jit(solution)/shard_map/ppermute | solution.py:778
  69.2 9.7 %collective-permute-start.16 = (f32[2,96,256]{2,1,0:T(8,128)}, f32[2,96,256]{2,1,0:T(8,128)}, u32[]{:S(2)}, u32[]{:S(2)}) collective-permute-start(f32[2,96,256]{2,1,0:T(8,128)} %get-tuple-element.70), channel_id=1, source_target_pairs={{0,3},{1,2},{2,1},{3,0},{4,7},{5,6},{6,5},{7,4},{8,11},{9,10},{10,... | collective-permute-start | bytes 589832 | tf_op jit(solution)/shard_map/ppermute | solution.py:778
  86.0 9.4 %collective-permute-start.17 = (f32[2,128,256]{2,1,0:T(8,128)S(1)}, f32[2,128,256]{2,1,0:T(8,128)S(1)}, u32[]{:S(2)}, u32[]{:S(2)}) collective-permute-start(f32[2,128,256]{2,1,0:T(8,128)S(1)} %get-tuple-element.72), channel_id=1, source_target_pairs={{0,1},{1,0},{2,3},{3,2},{4,5},{5,4},{6,7},{7,6},{8,9},{9,8},{10,11... | collective-permute-start | bytes 786440 | tf_op jit(solution)/shard_map/ppermute | solution.py:778
  87.4 12.0 %collective-permute-start.18 = (f32[2,128,256]{2,1,0:T(8,128)S(1)}, f32[2,128,256]{2,1,0:T(8,128)S(1)}, u32[]{:S(2)}, u32[]{:S(2)}) collective-permute-start(f32[2,128,256]{2,1,0:T(8,128)S(1)} %get-tuple-element.73), channel_id=1, source_target_pairs={{0,2},{1,3},{2,0},{3,1},{4,6},{5,7},{6,4},{7,5},{8,10},{9,11},{10,... | collective-permute-start | bytes 786440 | tf_op jit(solution)/shard_map/ppermute | solution.py:778
  88.6 12.5 %collective-permute-start.19 = (f32[2,128,256]{2,1,0:T(8,128)S(1)}, f32[2,128,256]{2,1,0:T(8,128)S(1)}, u32[]{:S(2)}, u32[]{:S(2)}) collective-permute-start(f32[2,128,256]{2,1,0:T(8,128)S(1)} %get-tuple-element.74), channel_id=1, source_target_pairs={{0,3},{1,2},{2,1},{3,0},{4,7},{5,6},{6,5},{7,4},{8,11},{9,10},{10,... | collective-permute-start | bytes 786440 | tf_op jit(solution)/shard_map/ppermute | solution.py:778
  105.2 44.6 %all-to-all-start.1 = ((f32[8,2,128,128]{3,2,1,0:T(8,128)}), f32[8,2,128,128]{3,2,1,0:T(8,128)S(1)}, u32[]{:S(2)}, u32[]{:S(2)}) async-start(f32[8,2,128,128]{3,2,1,0:T(8,128)} %get-tuple-element.80), calls=%async_computation.1 | async-start | bytes 2097152 | tf_op jit(solution)/shard_map/all_to_all | solution.py:765
  110.1 7.7 %collective-permute-start.20 = (f32[2,128,256]{2,1,0:T(8,128)}, f32[2,128,256]{2,1,0:T(8,128)S(1)}, u32[]{:S(2)}, u32[]{:S(2)}) collective-permute-start(f32[2,128,256]{2,1,0:T(8,128)} %get-tuple-element.82), channel_id=1, source_target_pairs={{0,1},{1,0},{2,3},{3,2},{4,5},{5,4},{6,7},{7,6},{8,9},{9,8},{10,11... | collective-permute-start | bytes 786440 | tf_op jit(solution)/shard_map/ppermute | solution.py:778
  111.0 7.4 %collective-permute-start.21 = (f32[2,128,256]{2,1,0:T(8,128)}, f32[2,128,256]{2,1,0:T(8,128)S(1)}, u32[]{:S(2)}, u32[]{:S(2)}) collective-permute-start(f32[2,128,256]{2,1,0:T(8,128)} %get-tuple-element.83), channel_id=1, source_target_pairs={{0,2},{1,3},{2,0},{3,1},{4,6},{5,7},{6,4},{7,5},{8,10},{9,11},{10,... | collective-permute-start | bytes 786440 | tf_op jit(solution)/shard_map/ppermute | solution.py:778
  111.6 12.8 %collective-permute-start.22 = (f32[2,128,256]{2,1,0:T(8,128)}, f32[2,128,256]{2,1,0:T(8,128)S(1)}, u32[]{:S(2)}, u32[]{:S(2)}) collective-permute-start(f32[2,128,256]{2,1,0:T(8,128)} %get-tuple-element.84), channel_id=1, source_target_pairs={{0,3},{1,2},{2,1},{3,0},{4,7},{5,6},{6,5},{7,4},{8,11},{9,10},{10,... | collective-permute-start | bytes 786440 | tf_op jit(solution)/shard_map/ppermute | solution.py:778
  129.4 6.7 %collective-permute-start.23 = (f32[2,128,128]{2,1,0:T(8,128)S(1)}, f32[2,128,128]{2,1,0:T(8,128)S(1)}, u32[]{:S(2)}, u32[]{:S(2)}) collective-permute-start(f32[2,128,128]{2,1,0:T(8,128)S(1)} %get-tuple-element.86), channel_id=1, source_target_pairs={{0,4},{4,8},{8,12},{12,16},{16,20},{20,24},{24,28},{28,0},{1,5},{5... | collective-permute-start | bytes 393224 | tf_op jit(solution)/shard_map/ppermute | solution.py:769
  131.7 18.0 %collective-permute-start.24 = (f32[2,128,128]{2,1,0:T(8,128)S(1)}, f32[2,128,128]{2,1,0:T(8,128)S(1)}, u32[]{:S(2)}, u32[]{:S(2)}) collective-permute-start(f32[2,128,128]{2,1,0:T(8,128)S(1)} %get-tuple-element.87), channel_id=1, source_target_pairs={{0,8},{4,12},{8,16},{12,20},{16,24},{20,28},{24,0},{28,4},{1,9},{5... | collective-permute-start | bytes 393224 | tf_op jit(solution)/shard_map/ppermute | solution.py:769
  132.8 20.5 %collective-permute-start.25 = (f32[2,128,128]{2,1,0:T(8,128)}, f32[2,128,128]{2,1,0:T(8,128)S(1)}, u32[]{:S(2)}, u32[]{:S(2)}) collective-permute-start(f32[2,128,128]{2,1,0:T(8,128)} %get-tuple-element.88), channel_id=1, source_target_pairs={{0,12},{4,16},{8,20},{12,24},{16,28},{20,0},{24,4},{28,8},{1,13},{... | collective-permute-start | bytes 393224 | tf_op jit(solution)/shard_map/ppermute | solution.py:769
  133.0 22.6 %collective-permute-start.26 = (f32[2,128,128]{2,1,0:T(8,128)}, f32[2,128,128]{2,1,0:T(8,128)S(1)}, u32[]{:S(2)}, u32[]{:S(2)}) collective-permute-start(f32[2,128,128]{2,1,0:T(8,128)} %get-tuple-element.89), channel_id=1, source_target_pairs={{0,16},{4,20},{8,24},{12,28},{16,0},{20,4},{24,8},{28,12},{1,17},{... | collective-permute-start | bytes 393224 | tf_op jit(solution)/shard_map/ppermute | solution.py:769
  134.4 21.2 %collective-permute-start.27 = (f32[2,128,128]{2,1,0:T(8,128)}, f32[2,128,128]{2,1,0:T(8,128)S(1)}, u32[]{:S(2)}, u32[]{:S(2)}) collective-permute-start(f32[2,128,128]{2,1,0:T(8,128)} %get-tuple-element.90), channel_id=1, source_target_pairs={{0,20},{4,24},{8,28},{12,0},{16,4},{20,8},{24,12},{28,16},{1,21},{... | collective-permute-start | bytes 393224 | tf_op jit(solution)/shard_map/ppermute | solution.py:769
  136.1 20.8 %collective-permute-start.28 = (f32[2,128,128]{2,1,0:T(8,128)S(1)}, f32[2,128,128]{2,1,0:T(8,128)S(1)}, u32[]{:S(2)}, u32[]{:S(2)}) collective-permute-start(f32[2,128,128]{2,1,0:T(8,128)S(1)} %get-tuple-element.91), channel_id=1, source_target_pairs={{0,24},{4,28},{8,0},{12,4},{16,8},{20,12},{24,16},{28,20},{1,25},{... | collective-permute-start | bytes 393224 | tf_op jit(solution)/shard_map/ppermute | solution.py:769
  149.7 7.6 %collective-permute-start.29 = (f32[2,128,128]{2,1,0:T(8,128)S(1)}, f32[2,128,128]{2,1,0:T(8,128)S(1)}, u32[]{:S(2)}, u32[]{:S(2)}) collective-permute-start(f32[2,128,128]{2,1,0:T(8,128)S(1)} %get-tuple-element.92), channel_id=1, source_target_pairs={{0,28},{4,0},{8,4},{12,8},{16,12},{20,16},{24,20},{28,24},{1,29},{... | collective-permute-start | bytes 393224 | tf_op jit(solution)/shard_map/ppermute | solution.py:769
  (22 other events, 403.9 us)

commit v4 on v3

--- a/solution.py
+++ b/solution.py
@@ -202,7 +202,7 @@
 BACKWARD_TILE = (False, False)
 BACKWARD_CUTS = (4, 4)
 MIDDLE_VMEM = 20
-ROW_VMEM = 14
+ROW_VMEM = 18
 ANY = pl.ANY
 HBM = pltpu.HBM
 TABLES = HBM
@@ -219,29 +219,18 @@
 
 
 def quarter_tables():
-    grid_b = np.arange(QUARTER)[:, None]
-    grid_k = np.arange(QUARTER)[None, :]
-    swapped = grid_k ^ HALF_LANES
-    row_fwd, row_bwd, col_fwd, col_bwd = [], [], [], []
-    for step in range(4):
-        lanes = swapped if step % 2 else grid_k
-        angle = 2.0 * math.pi * (grid_b * (step + 4 * lanes) % M) / M
-        cos, sin = np.cos(angle) / 32.0, np.sin(angle) / 32.0
-        for stacked, out in (
-            (np.concatenate([cos, sin], 0), row_fwd),
-            (np.concatenate([cos.T, -sin.T], 0), row_bwd),
-        ):
-            high, low = split_table(stacked)
-            out.append(np.concatenate([high, low], 0))
-        angle = 2.0 * math.pi * (grid_b * (step + 4 * grid_k) % M) / M
-        cos, sin = np.cos(angle) / 32.0, np.sin(angle) / 32.0
-        for stacked, out in (
-            (np.concatenate([cos.T, sin.T], 1), col_fwd),
-            (np.concatenate([cos, -sin], 1), col_bwd),
-        ):
-            high, low = split_table(stacked)
-            out.append(np.concatenate([high, low], 1))
-    return [np.stack(t) for t in (row_fwd, row_bwd, col_fwd, col_bwd)]
+    run = np.arange(QUARTER)
+    angle = 2.0 * math.pi * (run[:, None] * run[None, :] % QUARTER) / QUARTER
+    cos, sin = np.cos(angle) / 32.0, np.sin(angle) / 32.0
+    right = np.concatenate(split_table(np.concatenate([cos, sin], 0)), 0)
+    left = np.concatenate(split_table(np.concatenate([cos, sin], 1)), 1)
+    turns = 2.0 * math.pi * run[None, :] * np.arange(4)[:, None] / M
+    twiddles = np.stack([np.cos(turns), np.sin(turns)], 1).reshape(8, QUARTER).astype(np.float32)
+    return right, left, twiddles, np.ascontiguousarray(twiddles.T)
+
+
+def times(re, im, cos, sin):
+    return re * cos - im * sin, re * sin + im * cos
 
 
 def halves(x):
@@ -419,13 +408,13 @@
             pupil[(1,) + where] = gate * sine
 
 
-def forward_kernel(sizes, run, packed, piece_count, early, table, pupil, *refs):
+def forward_kernel(sizes, run, packed, piece_count, early, table, twiddles, pupil, *refs):
     leds, tiles, band = sizes
     run_first, rows = run
     pieces, refs = refs[:piece_count], refs[piece_count + early :]
     count = 1 if packed else tiles
     outs, refs = refs[:count], refs[count:]
-    table_v, pupil_v, window, result, sems, sems_out = refs
+    table_v, twiddles_v, pupil_v, window, result, sems, sems_out = refs
     me, tile = lax.axis_index("led"), lax.axis_index("tile")
     copies = []
     for shift in range(leds):
@@ -440,31 +429,34 @@
     copies.append(
         pltpu.make_async_copy(pupil.at[:, run_first : run_first + rows], pupil_v, sems.at[leds])
     )
-    tables = [pltpu.make_async_copy(table.at[k], table_v.at[k], sems.at[leds + 1 + k]) for k in range(4)]
-    start_all(copies + tables)
+    copies.append(pltpu.make_async_copy(table, table_v, sems.at[leds + 1]))
+    copies.append(pltpu.make_async_copy(twiddles, twiddles_v, sems.at[leds + 2]))
+    start_all(copies)
     wait_all(copies)
     parts = []
     for a in range(4):
         cells = slice(a * QUARTER, (a + 1) * QUARTER)
-        gate_re, gate_im = pupil_v[0, :, cells], pupil_v[1, :, cells]
-        cell_re, cell_im = window[0, :, cells], window[1, :, cells]
-        parts.append((gate_re * cell_re - gate_im * cell_im, gate_re * cell_im + gate_im * cell_re))
-    mixed = butterfly(parts, 1)
+        parts.append(times(window[0, :, cells], window[1, :, cells], pupil_v[0, :, cells], pupil_v[1, :, cells]))
+    mixed = [
+        times(re, im, twiddles_v[2 * k : 2 * k + 1], twiddles_v[2 * k + 1 : 2 * k + 2])
+        for k, (re, im) in enumerate(butterfly(parts, 1))
+    ]
+    lines = right_product(
+        jnp.concatenate([re for re, _ in mixed], axis=0),
+        jnp.concatenate([im for _, im in mixed], axis=0),
+        table_v[...],
+    )
     lane = lax.broadcasted_iota(jnp.int32, (rows, LANES), 1)
-    lines, leaving = [], []
-    for k in range(4):
-        tables[k].wait()
-        lines.append(right_product(*mixed[k], table_v[k]))
-        if k % 2 == 0:
-            continue
+    leaving = []
+    for k in (1, 3):
         places = slice((k // 2) * LANES, (k // 2 + 1) * LANES)
-        for other in range(tiles):
-            block = slice((other // 2) * LANES, (other // 2 + 1) * LANES)
+        for side in range(tiles // 2):
+            block = slice(side * LANES, (side + 1) * LANES)
             for part in range(2):
-                first, second = lines[k - 1][part][:, block], lines[k][part][:, block]
-                if other % 2:
-                    first, second = second, first
-                result[other, part, :, places] = jnp.where(lane < HALF_LANES, first, second)
+                first = lines[part][(k - 1) * rows : k * rows, block]
+                second = pltpu.roll(lines[part][k * rows : (k + 1) * rows, block], HALF_LANES, 1)
+                result[2 * side, part, :, places] = jnp.where(lane < HALF_LANES, first, second)
+                result[2 * side + 1, part, :, places] = jnp.where(lane < HALF_LANES, second, first)
         for shift in range(tiles):
             if packed:
                 source, target = result.at[shift], outs[0].at[shift]
@@ -487,38 +479,38 @@
     return [stack.at[tile ^ shift, :, cells] for shift in range(tiles)]
 
 
-def middle_kernel(sizes, runs_in, runs_out, table, table_back, images, copied, *refs):
+def middle_kernel(sizes, runs_in, runs_out, table, twiddles, images, copied, *refs):
     leds, tiles, band = sizes
     tile = lax.axis_index("tile")
-    table_v, back_v, images_v, field, residual, sems, sems_out = refs[-7:]
+    table_v, twiddles_v, images_v, field, residual, sems, sems_out = refs[-7:]
     views = [v for run, packed in runs_in for v in tile_views(field, run, packed, tile, tiles)]
     leaving = [v for run, packed in runs_out for v in tile_views(field, run, packed, tile, tiles)]
     blocks, outs = refs[: len(views)], refs[len(views) : -7]
     count = len(views)
     copies = [pltpu.make_async_copy(b, v, sems.at[n]) for n, (b, v) in enumerate(zip(blocks, views))]
+    copies.append(pltpu.make_async_copy(table, table_v, sems.at[count]))
+    copies.append(pltpu.make_async_copy(twiddles, twiddles_v, sems.at[count + 1]))
     later = [
-        [
-            pltpu.make_async_copy(table.at[k], table_v.at[k], sems.at[count + k]),
-            pltpu.make_async_copy(
-                images.at[k * QUARTER : (k + 1) * QUARTER],
-                images_v.at[k * QUARTER : (k + 1) * QUARTER],
-                sems.at[count + 4 + k],
-            ),
-            pltpu.make_async_copy(table_back.at[k], back_v.at[k], sems.at[count + 8 + k]),
-        ]
+        pltpu.make_async_copy(
+            images.at[k * QUARTER : (k + 1) * QUARTER],
+            images_v.at[k * QUARTER : (k + 1) * QUARTER],
+            sems.at[count + 2 + k],
+        )
         for k in range(4)
     ]
     start_all(copies)
-    for group in later:
-        start_all(group)
+    start_all(later)
     wait_all(copies)
     mixed = butterfly([(field[a, 0], field[a, 1]) for a in range(4)], 1)
     for k, (re, im) in enumerate(mixed):
-        wait_all(later[k])
-        wave_re, wave_im = left_product(re, im, table_v[k])
+        cos, sin = twiddles_v[:, 2 * k : 2 * k + 1], twiddles_v[:, 2 * k + 1 : 2 * k + 2]
+        wave_re, wave_im = left_product(*times(re, im, cos, sin), table_v[...])
+        later[k].wait()
         measured = images_v[k * QUARTER : (k + 1) * QUARTER, :]
         excess = wave_re * wave_re + wave_im * wave_im - measured
-        back_re, back_im = left_product(excess * wave_re, excess * wave_im, back_v[k])
+        back_re, back_im = left_product(excess * wave_re, -(excess * wave_im), table_v[...])
+        back_re, back_im = times(back_re, back_im, cos, sin)
+        back_im = -back_im
         residual[k, 0] = back_re
         residual[k, 1] = back_im
     mixed = butterfly([(residual[k, 0], residual[k, 1]) for k in range(4)], -1)
@@ -530,36 +522,45 @@
     wait_all(copies)
 
 
-def backward_kernel(sizes, run, packed, led_packed, held, table, pupil, *refs):
+def backward_kernel(sizes, run, packed, led_packed, held, table, twiddles, pupil, *refs):
     leds, tiles, band = sizes
     run_first, rows = run
     count = 1 if packed else tiles
     blocks, refs = refs[:count], refs[count + held :]
     sent = 1 if led_packed else leds
     outs, refs = refs[:sent], refs[sent + held :]
-    table_v, pupil_v, lines, result, sems, sems_out = refs
+    table_v, twiddles_v, pupil_v, lines, result, sems, sems_out = refs
     me, tile = lax.axis_index("led"), lax.axis_index("tile")
     views = tile_views(lines, (0, rows), packed, tile, tiles)
     copies = [pltpu.make_async_copy(b, v, sems.at[n]) for n, (b, v) in enumerate(zip(blocks, views))]
     gate = pltpu.make_async_copy(pupil.at[:, run_first : run_first + rows], pupil_v, sems.at[tiles])
-    tables = [pltpu.make_async_copy(table.at[k], table_v.at[k], sems.at[tiles + 1 + k]) for k in range(4)]
-    start_all(copies + tables + [gate])
+    copies.append(pltpu.make_async_copy(table, table_v, sems.at[tiles + 1]))
+    copies.append(pltpu.make_async_copy(twiddles, twiddles_v, sems.at[tiles + 2]))
+    start_all(copies + [gate])
     wait_all(copies)
     lane = lax.broadcasted_iota(jnp.int32, (rows, LANES), 1)
-    parts = []
+    stacked = [[], []]
     for k in range(4):
         cells = slice((k // 2) * LANES, (k // 2 + 1) * LANES)
-        both = []
         for part in range(2):
             joined = []
             for pair in range(tiles // 2):
                 first, second = lines[2 * pair, part, :, cells], lines[2 * pair + 1, part, :, cells]
                 if k % 2:
-                    first, second = second, first
-                joined.append(jnp.where(lane < HALF_LANES, first, second))
-            both.append(jnp.concatenate(joined, axis=1))
-        tables[k].wait()
-        parts.append(right_product(both[0], both[1], table_v[k]))
+                    joined.append(pltpu.roll(jnp.where(lane < HALF_LANES, second, first), HALF_LANES, 1))
+                else:
+                    joined.append(jnp.where(lane < HALF_LANES, first, second))
+            stacked[part].append(jnp.concatenate(joined, axis=1))
+    all_re, all_im = right_product(
+        jnp.concatenate(stacked[0], axis=0), -jnp.concatenate(stacked[1], axis=0), table_v[...]
+    )
+    parts = []
+    for k in range(4):
+        step = slice(k * rows, (k + 1) * rows)
+        re, im = times(
+            all_re[step], all_im[step], twiddles_v[2 * k : 2 * k + 1], twiddles_v[2 * k + 1 : 2 * k + 2]
+        )
+        parts.append((re, -im))
     gate.wait()
     copies = []
     for a, (re, im) in enumerate(butterfly(parts, -1)):
@@ -751,7 +752,7 @@
     backward_runs = runs_of(band, BACKWARD_CUTS)
     forward_packed = FORWARD_TILE
     backward_packed = BACKWARD_TILE
-    row_fwd, row_bwd, col_fwd, col_bwd = (jnp.asarray(t) for t in quarter_tables())
+    right, left, twiddles, twiddles_down = (jnp.asarray(t) for t in quarter_tables())
     flat = spectrum.reshape(-1, LANES)
     smem, vmem = pltpu.SMEM, pltpu.VMEM
     dma = pltpu.SemaphoreType.DMA
@@ -819,7 +820,8 @@
             moved=2 * flat.size, aliases={2: 0} if so_far else None, vmem=16,
         )(after, flat, *so_far, *also)
 
-    table_shape = (4, 4 * QUARTER, QUARTER)
+    right_v = [pltpu.VMEM(right.shape, BF16), pltpu.VMEM(twiddles.shape, F32)]
+    left_v = [pltpu.VMEM(left.shape, BF16), pltpu.VMEM(twiddles_down.shape, F32)]
     received, copied = [], None
     for number, (run, packed, pieces) in enumerate(zip(forward_runs, forward_packed, arrived)):
         rows = run[1]
@@ -828,15 +830,15 @@
         early = [copied]
         pieces_count = len(pieces)
         lines = call(
-            part(forward_kernel, sizes, run, packed, pieces_count, len(early)), f"forward_{run[0]}", [TABLES, ANY] + own_first(pieces_count) + [HBM] * len(early),
+            part(forward_kernel, sizes, run, packed, pieces_count, len(early)), f"forward_{run[0]}", [TABLES] * 2 + [ANY] + own_first(pieces_count) + [HBM] * len(early),
             blocks_of(run, packed),
             [
-                pltpu.VMEM(table_shape, BF16), pltpu.VMEM((2, rows, M), F32),
+                *right_v, pltpu.VMEM((2, rows, M), F32),
                 pltpu.VMEM((2, rows, M), F32), pltpu.VMEM((tiles, 2, rows, band), F32),
                 dma((leds + 5,)), dma((tiles, 2)),
             ],
             flops=24 * rows * M * QUARTER, moved=2**23, vmem=ROW_VMEM,
-        )(row_fwd, pupil, *pieces, *early)
+        )(right, twiddles, pupil, *pieces, *early)
         received += over_tile(lines, packed)
 
     copied = copy_part(2, lines[0], [copied])
@@ -846,12 +848,12 @@
         "middle", [TABLES] * 2 + [ANY, HBM] + [HBM] * arrays_in,
         [b for run, packed in zip(backward_runs, backward_packed) for b in blocks_of(run, packed)],
         [
-            pltpu.VMEM((4, QUARTER, 4 * QUARTER), BF16), pltpu.VMEM((4, QUARTER, 4 * QUARTER), BF16),
+            *left_v,
             pltpu.VMEM((M, band), F32), pltpu.VMEM((4, 2, QUARTER, band), F32),
             pltpu.VMEM((4, 2, QUARTER, band), F32), dma((arrays_in + 12,)), dma((arrays_out,)),
         ],
         flops=48 * band * M * QUARTER, moved=2**24, vmem=MIDDLE_VMEM, free=FREE_MIDDLE,
-    )(col_fwd, col_bwd, images, copied, *received)
+    )(left, twiddles_down, images, copied, *received)
     updated = copy_part(3, returned[0], [copied], ANY if FREE_MIDDLE else HBM)
     count = 1 if backward_packed[0] else tiles
     returned, later = returned[:count], returned[count:]
@@ -863,16 +865,16 @@
         count = len(lines)
         results = call(
             part(backward_kernel, sizes, run, packed, led_packed, len(held + through)), f"backward_{run[0]}",
-            [TABLES, ANY] + own_first(count, FREE_MIDDLE) + [ANY] * len(held) + [HBM] * len(through),
+            [TABLES] * 2 + [ANY] + own_first(count, FREE_MIDDLE) + [ANY] * len(held) + [HBM] * len(through),
             pieces_of(run, led_packed) + [f32(*h.shape) for h in held + through],
             [
-                pltpu.VMEM(table_shape, BF16), pltpu.VMEM((2, rows, M), F32),
+                *right_v, pltpu.VMEM((2, rows, M), F32),
                 pltpu.VMEM((tiles, 2, rows, band), F32), pltpu.VMEM((2, rows, M), F32),
                 dma((tiles + 5,)), dma((leds,)),
             ],
             flops=24 * rows * M * QUARTER, moved=2**23, vmem=ROW_VMEM, free=FREE_BACKWARD and not (led_packed or through),
-            aliases={2 + count + n: sent + n for n in range(len(held + through))},
-        )(row_bwd, pupil, *lines, *held, *through)
+            aliases={3 + count + n: sent + n for n in range(len(held + through))},
+        )(right, twiddles, pupil, *lines, *held, *through)
         pieces, later = over_led(results[:sent], led_packed), results[sent : sent + len(held)]
         updated = results[-1] if through else updated
         spans = len(spans_of(run))

time: 163 us -> 161 us (0.988)
  Pallas kernels: 66.5 us -> 64 us
    pallas_call x13, Pallas kernels: 62.9 us -> 60.4 us  [pinned(): run(*(pltpu.with_memory_space_constraint(x, HBM) if place == HBM else x f...]
  transfers between devices with their start and end apart: 32 -> 32, of which waited for: 18 -> 19; matrix products, arithmetic and copies ran while one was open for 0% -> 0% of each run, Pallas kernels for 27% -> 27%
where the time goes in v4:
time: 161 us; the launch traced here: 160 us
  Pallas kernels  64 us (40%)
  waiting for transfers between devices  54.6 us (34%)
  starting transfers between devices  39.5 us (25%)
    pallas_call x13, Pallas kernels, pinned(): run(*(pltpu.with_memory_space_constraint(x, HBM) if place == HBM else x f...  60.4 us
    ppermute x21, waiting for transfers between devices, over_led(): lax.ppermute(arrays[shift], 'led', [(i, (i + shift) % leds) for i in rang...  35.2 us
    ppermute x21, starting transfers between devices, over_led(): lax.ppermute(arrays[shift], 'led', [(i, (i + shift) % leds) for i in rang...  22 us
    ppermute x9, waiting for transfers between devices, over_tile(): lax.ppermute(arrays[shift], 'tile', [(i, i ^ shift) for i in range(tiles)])  19.3 us
    ppermute x9, starting transfers between devices, over_tile(): lax.ppermute(arrays[shift], 'tile', [(i, i ^ shift) for i in range(tiles)])  8.08 us
    all_to_all x1, starting transfers between devices, over_led(): lax.all_to_all(arrays[0], 'led', split_axis=0, concat_axis=0, tiled=True)  5.08 us
    all_to_all x1, starting transfers between devices, over_tile(): lax.all_to_all(arrays[0], 'tile', split_axis=0, concat_axis=0, tiled=True)  4.29 us
    pallas_call x1, Pallas kernels, unit_shards(): pl.pallas_call(part(prepare_kernel, sizes), name='prepare', out_shape=[f3...  3.59 us
  transfers between devices with their start and end apart: 32, of which 19 were waited for; matrix products, arithmetic and copies ran while one was open for 0% of the time, Pallas kernels for 27%

profile of v4, /device:TPU:11, one launch (start us, length us, event | category | flops | bytes accessed | tf_op | source)
XLA Modules:
  0.0 159.5 jit_solution(767173427902638741)
XLA Ops:
  0.0 3.2 %gather_0.1 = (f32[2,160,128]{2,1,0:T(8,128)}, f32[2,160,128]{2,1,0:T(8,128)}, f32[2,160,128]{2,1,0:T(8,128)}, f32[2,160,128]{2,1,0:T(8,128)}, f32[2,160,128]{2,...) custom-call(s32[8]{0:T(128)} %lead.9, s32[8]{0:T(128)} %row_off.9, ...), custom_call_target="tpu_custom_call" | custom-call | bytes 4194304 | tf_op jit(solution)/shard_map/gather_0/pallas_call | solution.py:732
  3.3 1.9 %collective-permute-start.7 = (f32[2,160,128]{2,1,0:T(8,128)}, f32[2,160,128]{2,1,0:T(8,128)S(1)}, u32[]{:S(2)}, u32[]{:S(2)}) collective-permute-start(f32[2,160,128]{2,1,0:T(8,128)} %get-tuple-element.60), channel_id=1, source_target_pairs={{0,4},{4,8},{8,12},{12,16},{16,20},{20,24},{24,28},{28,0},{1,5},{5... | collective-permute-start | bytes 491528 | tf_op jit(solution)/shard_map/ppermute | solution.py:770
  9.5 2.7 %gather_1.1 = (f32[2,96,128]{2,1,0:T(8,128)}, f32[2,96,128]{2,1,0:T(8,128)}, f32[2,96,128]{2,1,0:T(8,128)}, f32[2,96,128]{2,1,0:T(8,128)}, f32[2,96,128]{2,1,0:T...) custom-call(s32[8]{0:T(128)} %lead.9, s32[8]{0:T(128)} %row_off.9, s32[8]{0:T(128)} %col_off.9, ...), custom_call_target="tpu_custom_call" | custom-call | bytes 4194304 | tf_op jit(solution)/shard_map/gather_1/pallas_call | solution.py:732
  13.9 3.6 %prepare.1 = (f32[2,256,1024]{2,1,0:T(8,128)S(1)}, f32[1024,256]{1,0:T(8,128)S(1)}) custom-call(s32[8]{0:T(128)S(1)} %copy-done.5, s32[8]{0:T(128)S(1)} %copy-done.6, s32[8]{0:T(128)S(1)} %copy-done.7, s32[8,8,8]{2,1,0:T(8,128)S(1)} %copy-done.9, f32[5]{0:T(128)S(1)} %copy-done.10, bf16[256,1024]{1,0:T(8,128)(2,1)S(1)} %bitcast.3), custom_call_target="tpu_custom_call" | custom-call | flops 2000000000 | bytes 4000000 | tf_op jit(solution)/shard_map/prepare/pallas_call | solution.py:804
  17.5 6.6 %copy_0.1.refs_8_.refs_0_ = f32[65536,128]{1,0:T(8,128)} custom-call(f32[2,160,128]{2,1,0:T(8,128)S(1)} %collective-permute-done.8.after.refs_2_, f32[65536,128]{1,0:T(8,128)} %bitcast.6, f32[2,96,128]{2,1,0:T(8,128)} %get-tuple-element.51.refs_0_), custom_call_target="tpu_custom_call" | custom-call | bytes 16777216 | tf_op jit(solution)/shard_map/copy_0/pallas_call | solution.py:732
  24.2 5.9 %collective-permute-done.9.refs_3_ = f32[2,160,128]{2,1,0:T(8,128)S(1)} collective-permute-done((f32[2,160,128]{2,1,0:T(8,128)}, f32[2,160,128]{2,1,0:T(8,128)S(1)}, u32[]{:S(2)}, u32[]{:S(2)}) %collective-permute-start.9) | collective-permute-done | bytes 163872 | tf_op jit(solution)/shard_map/ppermute | solution.py:770
  30.0 3.5 %collective-permute-done.10.refs_4_ = f32[2,160,128]{2,1,0:T(8,128)S(1)} collective-permute-done((f32[2,160,128]{2,1,0:T(8,128)}, f32[2,160,128]{2,1,0:T(8,128)S(1)}, u32[]{:S(2)}, u32[]{:S(2)}) %collective-permute-start.10) | collective-permute-done | bytes 163872 | tf_op jit(solution)/shard_map/ppermute | solution.py:770
  33.5 1.8 %collective-permute-done.12.refs_6_ = f32[2,160,128]{2,1,0:T(8,128)S(1)} collective-permute-done((f32[2,160,128]{2,1,0:T(8,128)S(1)}, f32[2,160,128]{2,1,0:T(8,128)S(1)}, u32[]{:S(2)}, u32[]{:S(2)}) %collective-permute-start.12) | collective-permute-done | bytes 163872 | tf_op jit(solution)/shard_map/ppermute | solution.py:770
  35.5 4.0 %forward_0.1.after = f32[4,2,160,256]{3,2,1,0:T(8,128)} custom-call(bf16[1024,256]{1,0:T(8,128)(2,1)} %constant.8.clone.table, f32[8,256]{1,0:T(8,128)} %constant.10.clone.twiddles, f32[2,256,1024]{2,1,0:T(8,128)S(1)} %get-tuple-element.49.pupil, f32[2,160,128]{2,1,0:T(8,128)} %get-tuple-element.59.refs_0_, ...), custom_call_target="tpu_custom_call" | custom-call | flops 1006632960 | bytes 8388608 | tf_op jit(solution)/shard_map/forward_0/pallas_call | solution.py:732
  39.5 4.3 %all-to-all-start = ((f32[4,2,160,256]{3,2,1,0:T(8,128)}), f32[4,2,160,256]{3,2,1,0:T(8,128)}, u32[]{:S(2)}, u32[]{:S(2)}) async-start(f32[4,2,160,256]{3,2,1,0:T(8,128)} %forward_0.1.after), calls=%async_computation | async-start | bytes 2621440 | tf_op jit(solution)/shard_map/all_to_all | solution.py:776
  43.9 1.9 %collective-permute-start.2 = (f32[2,96,128]{2,1,0:T(8,128)}, f32[2,96,128]{2,1,0:T(8,128)S(1)}, u32[]{:S(2)}, u32[]{:S(2)}) collective-permute-start(f32[2,96,128]{2,1,0:T(8,128)} %get-tuple-element.54), channel_id=1, source_target_pairs={{0,12},{4,16},{8,20},{12,24},{16,28},{20,0},{24,4},{28,8},{1,13},{... | collective-permute-start | bytes 294920 | tf_op jit(solution)/shard_map/ppermute | solution.py:770
  46.8 2.0 %collective-permute-start.4 = (f32[2,96,128]{2,1,0:T(8,128)S(1)}, f32[2,96,128]{2,1,0:T(8,128)S(1)}, u32[]{:S(2)}, u32[]{:S(2)}) collective-permute-start(f32[2,96,128]{2,1,0:T(8,128)S(1)} %copy-done.17), channel_id=1, source_target_pairs={{0,20},{4,24},{8,28},{12,0},{16,4},{20,8},{24,12},{28,16},{1,21},{... | collective-permute-start | bytes 294920 | tf_op jit(solution)/shard_map/ppermute | solution.py:770
  50.6 6.6 %copy_1.1.refs_8_.refs_0_ = f32[65536,128]{1,0:T(8,128)} custom-call(f32[4,2,160,256]{3,2,1,0:T(8,128)} %forward_0.1.after, f32[65536,128]{1,0:T(8,128)} %bitcast.7, f32[65536,128]{1,0:T(8,128)} %copy_0.1.refs_8_.refs_0_), custom_call_target="tpu_custom_call", output_to_operand_aliasing={{}: (2, {})} | custom-call | bytes 16777216 | tf_op jit(solution)/shard_map/copy_1/pallas_call | solution.py:732
  58.7 2.1 %collective-permute-done.3.refs_4_ = f32[2,96,128]{2,1,0:T(8,128)S(1)} collective-permute-done((f32[2,96,128]{2,1,0:T(8,128)S(1)}, f32[2,96,128]{2,1,0:T(8,128)S(1)}, u32[]{:S(2)}, u32[]{:S(2)}) %collective-permute-start.3) | collective-permute-done | bytes 98336 | tf_op jit(solution)/shard_map/ppermute | solution.py:770
  60.8 2.6 %collective-permute-done.5.refs_6_ = f32[2,96,128]{2,1,0:T(8,128)S(1)} collective-permute-done((f32[2,96,128]{2,1,0:T(8,128)S(1)}, f32[2,96,128]{2,1,0:T(8,128)S(1)}, u32[]{:S(2)}, u32[]{:S(2)}) %collective-permute-start.5) | collective-permute-done | bytes 98336 | tf_op jit(solution)/shard_map/ppermute | solution.py:770
  63.4 3.3 %forward_160.1 = (f32[2,96,256]{2,1,0:T(8,128)}, f32[2,96,256]{2,1,0:T(8,128)}, f32[2,96,256]{2,1,0:T(8,128)}, f32[2,96,256]{2,1,0:T(8,128)}) custom-call(bf16[1024,256]{1,0:T(8,128)(2,1)} %constant.8.clone.table, f32[8,256]{1,0:T(8,128)} %constant.10.clone.twiddles, f32[2,256,1024]{2,1,0:T(8,128)S(1)} %get-tuple-element.49.pupil, ...), custom_call_target="tpu_custom_call" | custom-call | flops 603979776 | bytes 8388608 | tf_op jit(solution)/shard_map/forward_160/pallas_call | solution.py:732
  69.4 6.6 %copy_2.1.copied.refs_0_ = f32[65536,128]{1,0:T(8,128)} custom-call(f32[2,96,256]{2,1,0:T(8,128)} %get-tuple-element.67.after.refs_1_, f32[65536,128]{1,0:T(8,128)} %bitcast.8, f32[65536,128]{1,0:T(8,128)} %copy_1.1.refs_8_.refs_0_), custom_call_target="tpu_custom_call", output_to_operand_aliasing={{}: (2, {})} | custom-call | bytes 16777216 | tf_op jit(solution)/shard_map/copy_2/pallas_call | solution.py:732
  77.9 6.8 %middle.1 = (f32[2,128,256]{2,1,0:T(8,128)S(1)}, f32[2,128,256]{2,1,0:T(8,128)S(1)}, f32[2,128,256]{2,1,0:T(8,128)S(1)}, f32[2,128,256]{2,1,0:T(8,128)S(1)}, f32...) custom-call(bf16[256,1024]{1,0:T(8,128)(2,1)} %constant.9.clone.tabl, ...), custom_call_target="tpu_custom_call" | custom-call | flops 3221225472 | bytes 16777216 | tf_op jit(solution)/shard_map/middle/pallas_call | solution.py:732
  87.5 6.6 %copy_3.1.refs_8_ = f32[65536,128]{1,0:T(8,128)} custom-call(f32[2,128,256]{2,1,0:T(8,128)S(1)} %get-tuple-element.71.after.refs_0_, f32[65536,128]{1,0:T(8,128)} %bitcast.9, f32[65536,128]{1,0:T(8,128)} %copy_2.1.copied.refs_0_), custom_call_target="tpu_custom_call", output_to_operand_aliasing={{}: (2, {})} | custom-call | bytes 16777216 | tf_op jit(solution)/shard_map/copy_3/pallas_call | solution.py:732
  94.1 4.1 %collective-permute-done.18.refs_2_ = f32[2,128,256]{2,1,0:T(8,128)S(1)} collective-permute-done((f32[2,128,256]{2,1,0:T(8,128)S(1)}, f32[2,128,256]{2,1,0:T(8,128)S(1)}, u32[]{:S(2)}, u32[]{:S(2)}) %collective-permute-start.18) | collective-permute-done | bytes 262176 | tf_op jit(solution)/shard_map/ppermute | solution.py:779
  98.2 1.7 %collective-permute-done.19.refs_3_ = f32[2,128,256]{2,1,0:T(8,128)S(1)} collective-permute-done((f32[2,128,256]{2,1,0:T(8,128)S(1)}, f32[2,128,256]{2,1,0:T(8,128)S(1)}, u32[]{:S(2)}, u32[]{:S(2)}) %collective-permute-start.19) | collective-permute-done | bytes 262176 | tf_op jit(solution)/shard_map/ppermute | solution.py:779
  99.9 3.5 %backward_0.1 = (f32[8,2,128,128]{3,2,1,0:T(8,128)}, f32[2,128,256]{2,1,0:T(8,128)}, f32[2,128,256]{2,1,0:T(8,128)}, f32[2,128,256]{2,1,0:T(8,128)}, f32[2,128,256]{2,1,0:T(8,128)}, /*index=5*/f32[65536,128]{1,0:T(8,128)}) custom-call(bf16[1024,256]{1,0:T(8,128)(2,1)} %constant.8.clone.tabl, ...), custom_call_target="tpu_custom_call", output_to_operand_aliasing={{1}: (7, {}), {2}: (8, {}), {3}: (9, {}), {4}: (10, {}), {5... | custom-call | flops 805306368 | bytes 8388608 | tf_op jit(solution)/shard_map/backward_0/pallas_call | solution.py:732
  103.4 5.1 %all-to-all-start.1 = ((f32[8,2,128,128]{3,2,1,0:T(8,128)}), f32[8,2,128,128]{3,2,1,0:T(8,128)S(1)}, u32[]{:S(2)}, u32[]{:S(2)}) async-start(f32[8,2,128,128]{3,2,1,0:T(8,128)} %get-tuple-element.80), calls=%async_computation.1 | async-start | bytes 2097152 | tf_op jit(solution)/shard_map/all_to_all | solution.py:766
  111.1 5.1 %collective-permute-done.20.refs_1_ = f32[2,128,256]{2,1,0:T(8,128)S(1)} collective-permute-done((f32[2,128,256]{2,1,0:T(8,128)}, f32[2,128,256]{2,1,0:T(8,128)S(1)}, u32[]{:S(2)}, u32[]{:S(2)}) %collective-permute-start.20) | collective-permute-done | bytes 262176 | tf_op jit(solution)/shard_map/ppermute | solution.py:779
  116.9 5.9 %collective-permute-done.22.refs_3_ = f32[2,128,256]{2,1,0:T(8,128)S(1)} collective-permute-done((f32[2,128,256]{2,1,0:T(8,128)}, f32[2,128,256]{2,1,0:T(8,128)S(1)}, u32[]{:S(2)}, u32[]{:S(2)}) %collective-permute-start.22) | collective-permute-done | bytes 262176 | tf_op jit(solution)/shard_map/ppermute | solution.py:779
  123.7 3.5 %backward_128.1 = (f32[2,128,128]{2,1,0:T(8,128)S(1)}, f32[2,128,128]{2,1,0:T(8,128)S(1)}, f32[2,128,128]{2,1,0:T(8,128)S(1)}, f32[2,128,128]{2,1,0:T(8,128)}, f...) custom-call(bf16[1024,256]{1,0:T(8,128)(2,1)} %constant.8.clone.table, ...), custom_call_target="tpu_custom_call" | custom-call | flops 805306368 | bytes 8388608 | tf_op jit(solution)/shard_map/backward_128/pallas_call | solution.py:732
  127.2 2.3 %collective-permute-start.23 = (f32[2,128,128]{2,1,0:T(8,128)S(1)}, f32[2,128,128]{2,1,0:T(8,128)S(1)}, u32[]{:S(2)}, u32[]{:S(2)}) collective-permute-start(f32[2,128,128]{2,1,0:T(8,128)S(1)} %get-tuple-element.86), channel_id=1, source_target_pairs={{0,4},{4,8},{8,12},{12,16},{16,20},{20,24},{24,28},{28,0},{1,5},{5... | collective-permute-start | bytes 393224 | tf_op jit(solution)/shard_map/ppermute | solution.py:770
  132.2 1.7 %collective-permute-start.27 = (f32[2,128,128]{2,1,0:T(8,128)}, f32[2,128,128]{2,1,0:T(8,128)S(1)}, u32[]{:S(2)}, u32[]{:S(2)}) collective-permute-start(f32[2,128,128]{2,1,0:T(8,128)} %get-tuple-element.90), channel_id=1, source_target_pairs={{0,20},{4,24},{8,28},{12,0},{16,4},{20,8},{24,12},{28,16},{1,21},{... | collective-permute-start | bytes 393224 | tf_op jit(solution)/shard_map/ppermute | solution.py:770
  134.9 13.3 %collective-permute-done.24.refs_2_ = f32[2,128,128]{2,1,0:T(8,128)S(1)} collective-permute-done((f32[2,128,128]{2,1,0:T(8,128)S(1)}, f32[2,128,128]{2,1,0:T(8,128)S(1)}, u32[]{:S(2)}, u32[]{:S(2)}) %collective-permute-start.24) | collective-permute-done | bytes 131104 | tf_op jit(solution)/shard_map/ppermute | solution.py:770
  148.3 3.4 %update_0.1.buffer = f32[65536,128]{1,0:T(8,128)} custom-call(s32[8]{0:T(128)S(1)} %copy-done.5, s32[8]{0:T(128)S(1)} %copy-done.6, s32[8]{0:T(128)S(1)} %copy-done.7, f32[65536,128]{1,0:T(8,128)} %bitcast.10, f32[65536,128]{1,0:T(8,128)} %get-tuple-element.79.buffer, f32[8,2,128,128]{3,2,1,0:T(8,128)S(1)} %all-to-all-done.1.refs_0_), custom_call_target="tpu_custom_call", output_to_operand_aliasing={{}: (4, {})} | custom-call | bytes 4194304 | tf_op jit(solution)/shard_map/update_0/pallas_call | solution.py:732
  151.7 2.3 %collective-permute-done.26.refs_4_ = f32[2,128,128]{2,1,0:T(8,128)S(1)} collective-permute-done((f32[2,128,128]{2,1,0:T(8,128)}, f32[2,128,128]{2,1,0:T(8,128)S(1)}, u32[]{:S(2)}, u32[]{:S(2)}) %collective-permute-start.26) | collective-permute-done | bytes 131104 | tf_op jit(solution)/shard_map/ppermute | solution.py:770
  155.7 3.6 %update_128.1 = f32[65536,128]{1,0:T(8,128)} custom-call(s32[8]{0:T(128)S(1)} %copy-done.5, s32[8]{0:T(128)S(1)} %copy-done.6, s32[8]{0:T(128)S(1)} %copy-done.7, f32[65536,128]{1,0:T(8,128)} %bitcast.11, f32[65536,128]{1,0:T(8,128)} %update_0.1.buffer, f32[2,128,128]{2,1,0:T(8,128)S(1)} %get-tuple-element.85.refs_0_, ...), custom_call_target="tpu_custom_call", output_to_operand_aliasing={{}: (4, {})} | custom-call | bytes 4194304 | tf_op jit(solution)/shard_map/update_128/pallas_call | solution.py:732
  (84 shorter events, 27.5 us)
Async XLA Ops:
  3.3 8.9 %collective-permute-start.7 = (f32[2,160,128]{2,1,0:T(8,128)}, f32[2,160,128]{2,1,0:T(8,128)S(1)}, u32[]{:S(2)}, u32[]{:S(2)}) collective-permute-start(f32[2,160,128]{2,1,0:T(8,128)} %get-tuple-element.60), channel_id=1, source_target_pairs={{0,4},{4,8},{8,12},{12,16},{16,20},{20,24},{24,28},{28,0},{1,5},{5... | collective-permute-start | bytes 491528 | tf_op jit(solution)/shard_map/ppermute | solution.py:770
  5.2 8.2 %collective-permute-start.8 = (f32[2,160,128]{2,1,0:T(8,128)}, f32[2,160,128]{2,1,0:T(8,128)S(1)}, u32[]{:S(2)}, u32[]{:S(2)}) collective-permute-start(f32[2,160,128]{2,1,0:T(8,128)} %get-tuple-element.61), channel_id=1, source_target_pairs={{0,8},{4,12},{8,16},{12,20},{16,24},{20,28},{24,0},{28,4},{1,9},{5... | collective-permute-start | bytes 491528 | tf_op jit(solution)/shard_map/ppermute | solution.py:770
  6.5 23.5 %collective-permute-start.9 = (f32[2,160,128]{2,1,0:T(8,128)}, f32[2,160,128]{2,1,0:T(8,128)S(1)}, u32[]{:S(2)}, u32[]{:S(2)}) collective-permute-start(f32[2,160,128]{2,1,0:T(8,128)} %get-tuple-element.62), channel_id=1, source_target_pairs={{0,12},{4,16},{8,20},{12,24},{16,28},{20,0},{24,4},{28,8},{1,13},{... | collective-permute-start | bytes 491528 | tf_op jit(solution)/shard_map/ppermute | solution.py:770
  6.5 27.0 %collective-permute-start.10 = (f32[2,160,128]{2,1,0:T(8,128)}, f32[2,160,128]{2,1,0:T(8,128)S(1)}, u32[]{:S(2)}, u32[]{:S(2)}) collective-permute-start(f32[2,160,128]{2,1,0:T(8,128)} %get-tuple-element.63), channel_id=1, source_target_pairs={{0,16},{4,20},{8,24},{12,28},{16,0},{20,4},{24,8},{28,12},{1,17},{... | collective-permute-start | bytes 491528 | tf_op jit(solution)/shard_map/ppermute | solution.py:770
  7.9 25.6 %collective-permute-start.11 = (f32[2,160,128]{2,1,0:T(8,128)}, f32[2,160,128]{2,1,0:T(8,128)S(1)}, u32[]{:S(2)}, u32[]{:S(2)}) collective-permute-start(f32[2,160,128]{2,1,0:T(8,128)} %get-tuple-element.64), channel_id=1, source_target_pairs={{0,20},{4,24},{8,28},{12,0},{16,4},{20,8},{24,12},{28,16},{1,21},{... | collective-permute-start | bytes 491528 | tf_op jit(solution)/shard_map/ppermute | solution.py:770
  12.2 23.1 %collective-permute-start.12 = (f32[2,160,128]{2,1,0:T(8,128)S(1)}, f32[2,160,128]{2,1,0:T(8,128)S(1)}, u32[]{:S(2)}, u32[]{:S(2)}) collective-permute-start(f32[2,160,128]{2,1,0:T(8,128)S(1)} %copy-done.14), channel_id=1, source_target_pairs={{0,24},{4,28},{8,0},{12,4},{16,8},{20,12},{24,16},{28,20},{1,25},{... | collective-permute-start | bytes 491528 | tf_op jit(solution)/shard_map/ppermute | solution.py:770
  13.5 22.0 %collective-permute-start.13 = (f32[2,160,128]{2,1,0:T(8,128)S(1)}, f32[2,160,128]{2,1,0:T(8,128)S(1)}, u32[]{:S(2)}, u32[]{:S(2)}) collective-permute-start(f32[2,160,128]{2,1,0:T(8,128)S(1)} %copy-done.13), channel_id=1, source_target_pairs={{0,28},{4,0},{8,4},{12,8},{16,12},{20,16},{24,20},{28,24},{1,29},{... | collective-permute-start | bytes 491528 | tf_op jit(solution)/shard_map/ppermute | solution.py:770
  39.5 38.4 %all-to-all-start = ((f32[4,2,160,256]{3,2,1,0:T(8,128)}), f32[4,2,160,256]{3,2,1,0:T(8,128)}, u32[]{:S(2)}, u32[]{:S(2)}) async-start(f32[4,2,160,256]{3,2,1,0:T(8,128)} %forward_0.1.after), calls=%async_computation | async-start | bytes 2621440 | tf_op jit(solution)/shard_map/all_to_all | solution.py:776
  43.8 5.0 %collective-permute-start = (f32[2,96,128]{2,1,0:T(8,128)}, f32[2,96,128]{2,1,0:T(8,128)S(1)}, u32[]{:S(2)}, u32[]{:S(2)}) collective-permute-start(f32[2,96,128]{2,1,0:T(8,128)} %get-tuple-element.52), channel_id=1, source_target_pairs={{0,4},{4,8},{8,12},{12,16},{16,20},{20,24},{24,28},{28,0},{1,5},{5... | collective-permute-start | bytes 294920 | tf_op jit(solution)/shard_map/ppermute | solution.py:770
  43.9 5.9 %collective-permute-start.1 = (f32[2,96,128]{2,1,0:T(8,128)}, f32[2,96,128]{2,1,0:T(8,128)S(1)}, u32[]{:S(2)}, u32[]{:S(2)}) collective-permute-start(f32[2,96,128]{2,1,0:T(8,128)} %get-tuple-element.53), channel_id=1, source_target_pairs={{0,8},{4,12},{8,16},{12,20},{16,24},{20,28},{24,0},{28,4},{1,9},{5... | collective-permute-start | bytes 294920 | tf_op jit(solution)/shard_map/ppermute | solution.py:770
  43.9 14.7 %collective-permute-start.2 = (f32[2,96,128]{2,1,0:T(8,128)}, f32[2,96,128]{2,1,0:T(8,128)S(1)}, u32[]{:S(2)}, u32[]{:S(2)}) collective-permute-start(f32[2,96,128]{2,1,0:T(8,128)} %get-tuple-element.54), channel_id=1, source_target_pairs={{0,12},{4,16},{8,20},{12,24},{16,28},{20,0},{24,4},{28,8},{1,13},{... | collective-permute-start | bytes 294920 | tf_op jit(solution)/shard_map/ppermute | solution.py:770
  45.8 15.0 %collective-permute-start.3 = (f32[2,96,128]{2,1,0:T(8,128)S(1)}, f32[2,96,128]{2,1,0:T(8,128)S(1)}, u32[]{:S(2)}, u32[]{:S(2)}) collective-permute-start(f32[2,96,128]{2,1,0:T(8,128)S(1)} %copy-done.18), channel_id=1, source_target_pairs={{0,16},{4,20},{8,24},{12,28},{16,0},{20,4},{24,8},{28,12},{1,17},{... | collective-permute-start | bytes 294920 | tf_op jit(solution)/shard_map/ppermute | solution.py:770
  46.8 14.0 %collective-permute-start.4 = (f32[2,96,128]{2,1,0:T(8,128)S(1)}, f32[2,96,128]{2,1,0:T(8,128)S(1)}, u32[]{:S(2)}, u32[]{:S(2)}) collective-permute-start(f32[2,96,128]{2,1,0:T(8,128)S(1)} %copy-done.17), channel_id=1, source_target_pairs={{0,20},{4,24},{8,28},{12,0},{16,4},{20,8},{24,12},{28,16},{1,21},{... | collective-permute-start | bytes 294920 | tf_op jit(solution)/shard_map/ppermute | solution.py:770
  48.9 14.5 %collective-permute-start.5 = (f32[2,96,128]{2,1,0:T(8,128)S(1)}, f32[2,96,128]{2,1,0:T(8,128)S(1)}, u32[]{:S(2)}, u32[]{:S(2)}) collective-permute-start(f32[2,96,128]{2,1,0:T(8,128)S(1)} %copy-done.16), channel_id=1, source_target_pairs={{0,24},{4,28},{8,0},{12,4},{16,8},{20,12},{24,16},{28,20},{1,25},{... | collective-permute-start | bytes 294920 | tf_op jit(solution)/shard_map/ppermute | solution.py:770
  49.8 13.6 %collective-permute-start.6 = (f32[2,96,128]{2,1,0:T(8,128)S(1)}, f32[2,96,128]{2,1,0:T(8,128)S(1)}, u32[]{:S(2)}, u32[]{:S(2)}) collective-permute-start(f32[2,96,128]{2,1,0:T(8,128)S(1)} %copy-done.15), channel_id=1, source_target_pairs={{0,28},{4,0},{8,4},{12,8},{16,12},{20,16},{24,20},{28,24},{1,29},{... | collective-permute-start | bytes 294920 | tf_op jit(solution)/shard_map/ppermute | solution.py:770
  66.7 9.3 %collective-permute-start.14 = (f32[2,96,256]{2,1,0:T(8,128)}, f32[2,96,256]{2,1,0:T(8,128)S(1)}, u32[]{:S(2)}, u32[]{:S(2)}) collective-permute-start(f32[2,96,256]{2,1,0:T(8,128)} %get-tuple-element.68), channel_id=1, source_target_pairs={{0,1},{1,0},{2,3},{3,2},{4,5},{5,4},{6,7},{7,6},{8,9},{9,8},{10,11... | collective-permute-start | bytes 589832 | tf_op jit(solution)/shard_map/ppermute | solution.py:779
  66.9 10.0 %collective-permute-start.15 = (f32[2,96,256]{2,1,0:T(8,128)}, f32[2,96,256]{2,1,0:T(8,128)S(1)}, u32[]{:S(2)}, u32[]{:S(2)}) collective-permute-start(f32[2,96,256]{2,1,0:T(8,128)} %get-tuple-element.69), channel_id=1, source_target_pairs={{0,2},{1,3},{2,0},{3,1},{4,6},{5,7},{6,4},{7,5},{8,10},{9,11},{10,... | collective-permute-start | bytes 589832 | tf_op jit(solution)/shard_map/ppermute | solution.py:779
  68.2 9.7 %collective-permute-start.16 = (f32[2,96,256]{2,1,0:T(8,128)}, f32[2,96,256]{2,1,0:T(8,128)}, u32[]{:S(2)}, u32[]{:S(2)}) collective-permute-start(f32[2,96,256]{2,1,0:T(8,128)} %get-tuple-element.70), channel_id=1, source_target_pairs={{0,3},{1,2},{2,1},{3,0},{4,7},{5,6},{6,5},{7,4},{8,11},{9,10},{10,... | collective-permute-start | bytes 589832 | tf_op jit(solution)/shard_map/ppermute | solution.py:779
  84.8 9.3 %collective-permute-start.17 = (f32[2,128,256]{2,1,0:T(8,128)S(1)}, f32[2,128,256]{2,1,0:T(8,128)S(1)}, u32[]{:S(2)}, u32[]{:S(2)}) collective-permute-start(f32[2,128,256]{2,1,0:T(8,128)S(1)} %get-tuple-element.72), channel_id=1, source_target_pairs={{0,1},{1,0},{2,3},{3,2},{4,5},{5,4},{6,7},{7,6},{8,9},{9,8},{10,11... | collective-permute-start | bytes 786440 | tf_op jit(solution)/shard_map/ppermute | solution.py:779
  86.2 12.0 %collective-permute-start.18 = (f32[2,128,256]{2,1,0:T(8,128)S(1)}, f32[2,128,256]{2,1,0:T(8,128)S(1)}, u32[]{:S(2)}, u32[]{:S(2)}) collective-permute-start(f32[2,128,256]{2,1,0:T(8,128)S(1)} %get-tuple-element.73), channel_id=1, source_target_pairs={{0,2},{1,3},{2,0},{3,1},{4,6},{5,7},{6,4},{7,5},{8,10},{9,11},{10,... | collective-permute-start | bytes 786440 | tf_op jit(solution)/shard_map/ppermute | solution.py:779
  87.4 12.5 %collective-permute-start.19 = (f32[2,128,256]{2,1,0:T(8,128)S(1)}, f32[2,128,256]{2,1,0:T(8,128)S(1)}, u32[]{:S(2)}, u32[]{:S(2)}) collective-permute-start(f32[2,128,256]{2,1,0:T(8,128)S(1)} %get-tuple-element.74), channel_id=1, source_target_pairs={{0,3},{1,2},{2,1},{3,0},{4,7},{5,6},{6,5},{7,4},{8,11},{9,10},{10,... | collective-permute-start | bytes 786440 | tf_op jit(solution)/shard_map/ppermute | solution.py:779
  103.4 44.9 %all-to-all-start.1 = ((f32[8,2,128,128]{3,2,1,0:T(8,128)}), f32[8,2,128,128]{3,2,1,0:T(8,128)S(1)}, u32[]{:S(2)}, u32[]{:S(2)}) async-start(f32[8,2,128,128]{3,2,1,0:T(8,128)} %get-tuple-element.80), calls=%async_computation.1 | async-start | bytes 2097152 | tf_op jit(solution)/shard_map/all_to_all | solution.py:766
  108.5 7.7 %collective-permute-start.20 = (f32[2,128,256]{2,1,0:T(8,128)}, f32[2,128,256]{2,1,0:T(8,128)S(1)}, u32[]{:S(2)}, u32[]{:S(2)}) collective-permute-start(f32[2,128,256]{2,1,0:T(8,128)} %get-tuple-element.82), channel_id=1, source_target_pairs={{0,1},{1,0},{2,3},{3,2},{4,5},{5,4},{6,7},{7,6},{8,9},{9,8},{10,11... | collective-permute-start | bytes 786440 | tf_op jit(solution)/shard_map/ppermute | solution.py:779
  109.4 7.4 %collective-permute-start.21 = (f32[2,128,256]{2,1,0:T(8,128)}, f32[2,128,256]{2,1,0:T(8,128)S(1)}, u32[]{:S(2)}, u32[]{:S(2)}) collective-permute-start(f32[2,128,256]{2,1,0:T(8,128)} %get-tuple-element.83), channel_id=1, source_target_pairs={{0,2},{1,3},{2,0},{3,1},{4,6},{5,7},{6,4},{7,5},{8,10},{9,11},{10,... | collective-permute-start | bytes 786440 | tf_op jit(solution)/shard_map/ppermute | solution.py:779
  110.0 12.8 %collective-permute-start.22 = (f32[2,128,256]{2,1,0:T(8,128)}, f32[2,128,256]{2,1,0:T(8,128)S(1)}, u32[]{:S(2)}, u32[]{:S(2)}) collective-permute-start(f32[2,128,256]{2,1,0:T(8,128)} %get-tuple-element.84), channel_id=1, source_target_pairs={{0,3},{1,2},{2,1},{3,0},{4,7},{5,6},{6,5},{7,4},{8,11},{9,10},{10,... | collective-permute-start | bytes 786440 | tf_op jit(solution)/shard_map/ppermute | solution.py:779
  127.2 7.0 %collective-permute-start.23 = (f32[2,128,128]{2,1,0:T(8,128)S(1)}, f32[2,128,128]{2,1,0:T(8,128)S(1)}, u32[]{:S(2)}, u32[]{:S(2)}) collective-permute-start(f32[2,128,128]{2,1,0:T(8,128)S(1)} %get-tuple-element.86), channel_id=1, source_target_pairs={{0,4},{4,8},{8,12},{12,16},{16,20},{20,24},{24,28},{28,0},{1,5},{5... | collective-permute-start | bytes 393224 | tf_op jit(solution)/shard_map/ppermute | solution.py:770
  129.5 18.7 %collective-permute-start.24 = (f32[2,128,128]{2,1,0:T(8,128)S(1)}, f32[2,128,128]{2,1,0:T(8,128)S(1)}, u32[]{:S(2)}, u32[]{:S(2)}) collective-permute-start(f32[2,128,128]{2,1,0:T(8,128)S(1)} %get-tuple-element.87), channel_id=1, source_target_pairs={{0,8},{4,12},{8,16},{12,20},{16,24},{20,28},{24,0},{28,4},{1,9},{5... | collective-permute-start | bytes 393224 | tf_op jit(solution)/shard_map/ppermute | solution.py:770
  130.7 21.0 %collective-permute-start.25 = (f32[2,128,128]{2,1,0:T(8,128)}, f32[2,128,128]{2,1,0:T(8,128)S(1)}, u32[]{:S(2)}, u32[]{:S(2)}) collective-permute-start(f32[2,128,128]{2,1,0:T(8,128)} %get-tuple-element.88), channel_id=1, source_target_pairs={{0,12},{4,16},{8,20},{12,24},{16,28},{20,0},{24,4},{28,8},{1,13},{... | collective-permute-start | bytes 393224 | tf_op jit(solution)/shard_map/ppermute | solution.py:770
  130.8 23.1 %collective-permute-start.26 = (f32[2,128,128]{2,1,0:T(8,128)}, f32[2,128,128]{2,1,0:T(8,128)S(1)}, u32[]{:S(2)}, u32[]{:S(2)}) collective-permute-start(f32[2,128,128]{2,1,0:T(8,128)} %get-tuple-element.89), channel_id=1, source_target_pairs={{0,16},{4,20},{8,24},{12,28},{16,0},{20,4},{24,8},{28,12},{1,17},{... | collective-permute-start | bytes 393224 | tf_op jit(solution)/shard_map/ppermute | solution.py:770
  132.2 21.7 %collective-permute-start.27 = (f32[2,128,128]{2,1,0:T(8,128)}, f32[2,128,128]{2,1,0:T(8,128)S(1)}, u32[]{:S(2)}, u32[]{:S(2)}) collective-permute-start(f32[2,128,128]{2,1,0:T(8,128)} %get-tuple-element.90), channel_id=1, source_target_pairs={{0,20},{4,24},{8,28},{12,0},{16,4},{20,8},{24,12},{28,16},{1,21},{... | collective-permute-start | bytes 393224 | tf_op jit(solution)/shard_map/ppermute | solution.py:770
  134.2 21.1 %collective-permute-start.28 = (f32[2,128,128]{2,1,0:T(8,128)S(1)}, f32[2,128,128]{2,1,0:T(8,128)S(1)}, u32[]{:S(2)}, u32[]{:S(2)}) collective-permute-start(f32[2,128,128]{2,1,0:T(8,128)S(1)} %get-tuple-element.91), channel_id=1, source_target_pairs={{0,24},{4,28},{8,0},{12,4},{16,8},{20,12},{24,16},{28,20},{1,25},{... | collective-permute-start | bytes 393224 | tf_op jit(solution)/shard_map/ppermute | solution.py:770
  148.3 7.5 %collective-permute-start.29 = (f32[2,128,128]{2,1,0:T(8,128)S(1)}, f32[2,128,128]{2,1,0:T(8,128)S(1)}, u32[]{:S(2)}, u32[]{:S(2)}) collective-permute-start(f32[2,128,128]{2,1,0:T(8,128)S(1)} %get-tuple-element.92), channel_id=1, source_target_pairs={{0,28},{4,0},{8,4},{12,8},{16,12},{20,16},{24,20},{28,24},{1,29},{... | collective-permute-start | bytes 393224 | tf_op jit(solution)/shard_map/ppermute | solution.py:770
  (19 other events, 238.6 us)

commit v5 on v4

--- a/solution.py
+++ b/solution.py
@@ -197,9 +197,9 @@
 SUB = 128
 FORWARD_CUTS = (5, 3)
 FORWARD_LED = (False, False)
-BACKWARD_LED = (True, False)
+BACKWARD_LED = (False, False)
 FORWARD_TILE = (True, False)
-BACKWARD_TILE = (False, False)
+BACKWARD_TILE = (False, True)
 BACKWARD_CUTS = (4, 4)
 MIDDLE_VMEM = 20
 ROW_VMEM = 18

time: 161 us -> 160 us (level)
  starting transfers between devices: 39.5 us -> 43.1 us
  waiting for transfers between devices: 54.6 us -> 51.3 us
    ppermute x9 -> x6, waiting for transfers between devices: 19.3 us -> 7.71 us  [over_tile(): lax.ppermute(arrays[shift], 'tile', [(i, i ^ shift) for i in range(tiles)])]
    ppermute x21 -> x28, starting transfers between devices: 22 us -> 29.2 us  [over_led(): lax.ppermute(arrays[shift], 'led', [(i, (i + shift) % leds) for i in rang...]
    all_to_all x1 -> x2, waiting for transfers between devices: 0.01 us -> 5.91 us  [over_tile(): lax.all_to_all(arrays[0], 'tile', split_axis=0, concat_axis=0, tiled=True)]
    all_to_all x1 -> x0, starting transfers between devices: 5.08 us -> none  [over_led(): lax.all_to_all(arrays[0], 'led', split_axis=0, concat_axis=0, tiled=True)]
    all_to_all x1 -> x2, starting transfers between devices: 4.29 us -> 8.49 us  [over_tile(): lax.all_to_all(arrays[0], 'tile', split_axis=0, concat_axis=0, tiled=True)]
    ppermute x9 -> x6, starting transfers between devices: 8.08 us -> 5.46 us  [over_tile(): lax.ppermute(arrays[shift], 'tile', [(i, i ^ shift) for i in range(tiles)])]
    ppermute x21 -> x28, waiting for transfers between devices: 35.2 us -> 37.7 us  [over_led(): lax.ppermute(arrays[shift], 'led', [(i, (i + shift) % leds) for i in rang...]
  transfers between devices with their start and end apart: 32 -> 36, of which waited for: 19 -> 19; matrix products, arithmetic and copies ran while one was open for 0% -> 0% of each run, Pallas kernels for 27% -> 26%
where the time goes in v5:
time: 160 us; the launch traced here: 159 us
  Pallas kernels  63.5 us (40%)
  waiting for transfers between devices  51.3 us (32%)
  starting transfers between devices  43.1 us (27%)
    pallas_call x13, Pallas kernels, pinned(): run(*(pltpu.with_memory_space_constraint(x, HBM) if place == HBM else x f...  59.9 us
    ppermute x28, waiting for transfers between devices, over_led(): lax.ppermute(arrays[shift], 'led', [(i, (i + shift) % leds) for i in rang...  37.7 us
    ppermute x28, starting transfers between devices, over_led(): lax.ppermute(arrays[shift], 'led', [(i, (i + shift) % leds) for i in rang...  29.2 us
    all_to_all x2, starting transfers between devices, over_tile(): lax.all_to_all(arrays[0], 'tile', split_axis=0, concat_axis=0, tiled=True)  8.49 us
    ppermute x6, waiting for transfers between devices, over_tile(): lax.ppermute(arrays[shift], 'tile', [(i, i ^ shift) for i in range(tiles)])  7.71 us
    all_to_all x2, waiting for transfers between devices, over_tile(): lax.all_to_all(arrays[0], 'tile', split_axis=0, concat_axis=0, tiled=True)  5.91 us
    ppermute x6, starting transfers between devices, over_tile(): lax.ppermute(arrays[shift], 'tile', [(i, i ^ shift) for i in range(tiles)])  5.46 us
    pallas_call x1, Pallas kernels, unit_shards(): pl.pallas_call(part(prepare_kernel, sizes), name='prepare', out_shape=[f3...  3.59 us
  transfers between devices with their start and end apart: 36, of which 19 were waited for; matrix products, arithmetic and copies ran while one was open for 0% of the time, Pallas kernels for 26%

profile of v5, /device:TPU:11, one launch (start us, length us, event | category | flops | bytes accessed | tf_op | source)
XLA Modules:
  0.0 159.4 jit_solution(7194529582790572729)
XLA Ops:
  0.0 3.3 %gather_0.1 = (f32[2,160,128]{2,1,0:T(8,128)}, f32[2,160,128]{2,1,0:T(8,128)}, f32[2,160,128]{2,1,0:T(8,128)}, f32[2,160,128]{2,1,0:T(8,128)}, f32[2,160,128]{2,...) custom-call(s32[8]{0:T(128)} %lead.9, s32[8]{0:T(128)} %row_off.9, ...), custom_call_target="tpu_custom_call" | custom-call | bytes 4194304 | tf_op jit(solution)/shard_map/gather_0/pallas_call | solution.py:732
  3.3 1.9 %collective-permute-start.7 = (f32[2,160,128]{2,1,0:T(8,128)}, f32[2,160,128]{2,1,0:T(8,128)S(1)}, u32[]{:S(2)}, u32[]{:S(2)}) collective-permute-start(f32[2,160,128]{2,1,0:T(8,128)} %get-tuple-element.61), channel_id=1, source_target_pairs={{0,4},{4,8},{8,12},{12,16},{16,20},{20,24},{24,28},{28,0},{1,5},{5... | collective-permute-start | bytes 491528 | tf_op jit(solution)/shard_map/ppermute | solution.py:770
  9.5 2.7 %gather_1.1 = (f32[2,96,128]{2,1,0:T(8,128)}, f32[2,96,128]{2,1,0:T(8,128)}, f32[2,96,128]{2,1,0:T(8,128)}, f32[2,96,128]{2,1,0:T(8,128)}, f32[2,96,128]{2,1,0:T...) custom-call(s32[8]{0:T(128)} %lead.9, s32[8]{0:T(128)} %row_off.9, s32[8]{0:T(128)} %col_off.9, ...), custom_call_target="tpu_custom_call" | custom-call | bytes 4194304 | tf_op jit(solution)/shard_map/gather_1/pallas_call | solution.py:732
  14.0 3.6 %prepare.1 = (f32[2,256,1024]{2,1,0:T(8,128)S(1)}, f32[1024,256]{1,0:T(8,128)S(1)}) custom-call(s32[8]{0:T(128)S(1)} %copy-done.2, s32[8]{0:T(128)S(1)} %copy-done.3, s32[8]{0:T(128)S(1)} %copy-done.4, s32[8,8,8]{2,1,0:T(8,128)S(1)} %copy-done.6, f32[5]{0:T(128)S(1)} %copy-done.7, bf16[256,1024]{1,0:T(8,128)(2,1)S(1)} %bitcast.3), custom_call_target="tpu_custom_call" | custom-call | flops 2000000000 | bytes 4000000 | tf_op jit(solution)/shard_map/prepare/pallas_call | solution.py:804
  17.5 6.6 %copy_0.1.refs_8_.refs_0_ = f32[65536,128]{1,0:T(8,128)} custom-call(f32[2,160,128]{2,1,0:T(8,128)S(1)} %collective-permute-done.8.after.refs_2_, f32[65536,128]{1,0:T(8,128)} %bitcast.6, f32[2,96,128]{2,1,0:T(8,128)} %get-tuple-element.52.refs_0_), custom_call_target="tpu_custom_call" | custom-call | bytes 16777216 | tf_op jit(solution)/shard_map/copy_0/pallas_call | solution.py:732
  24.2 5.9 %collective-permute-done.9.refs_3_ = f32[2,160,128]{2,1,0:T(8,128)S(1)} collective-permute-done((f32[2,160,128]{2,1,0:T(8,128)}, f32[2,160,128]{2,1,0:T(8,128)S(1)}, u32[]{:S(2)}, u32[]{:S(2)}) %collective-permute-start.9) | collective-permute-done | bytes 163872 | tf_op jit(solution)/shard_map/ppermute | solution.py:770
  30.0 3.5 %collective-permute-done.10.refs_4_ = f32[2,160,128]{2,1,0:T(8,128)S(1)} collective-permute-done((f32[2,160,128]{2,1,0:T(8,128)}, f32[2,160,128]{2,1,0:T(8,128)S(1)}, u32[]{:S(2)}, u32[]{:S(2)}) %collective-permute-start.10) | collective-permute-done | bytes 163872 | tf_op jit(solution)/shard_map/ppermute | solution.py:770
  35.5 4.1 %forward_0.1.after = f32[4,2,160,256]{3,2,1,0:T(8,128)} custom-call(bf16[1024,256]{1,0:T(8,128)(2,1)} %constant.8.clone.table, f32[8,256]{1,0:T(8,128)} %constant.10.clone.twiddles, f32[2,256,1024]{2,1,0:T(8,128)S(1)} %get-tuple-element.50.pupil, f32[2,160,128]{2,1,0:T(8,128)} %get-tuple-element.60.refs_0_, ...), custom_call_target="tpu_custom_call" | custom-call | flops 1006632960 | bytes 8388608 | tf_op jit(solution)/shard_map/forward_0/pallas_call | solution.py:732
  39.5 4.3 %all-to-all-start = ((f32[4,2,160,256]{3,2,1,0:T(8,128)}), f32[4,2,160,256]{3,2,1,0:T(8,128)}, u32[]{:S(2)}, u32[]{:S(2)}) async-start(f32[4,2,160,256]{3,2,1,0:T(8,128)} %forward_0.1.after), calls=%async_computation | async-start | bytes 2621440 | tf_op jit(solution)/shard_map/all_to_all | solution.py:776
  44.0 1.9 %collective-permute-start.2 = (f32[2,96,128]{2,1,0:T(8,128)}, f32[2,96,128]{2,1,0:T(8,128)S(1)}, u32[]{:S(2)}, u32[]{:S(2)}) collective-permute-start(f32[2,96,128]{2,1,0:T(8,128)} %get-tuple-element.55), channel_id=1, source_target_pairs={{0,12},{4,16},{8,20},{12,24},{16,28},{20,0},{24,4},{28,8},{1,13},{... | collective-permute-start | bytes 294920 | tf_op jit(solution)/shard_map/ppermute | solution.py:770
  46.9 2.0 %collective-permute-start.4 = (f32[2,96,128]{2,1,0:T(8,128)S(1)}, f32[2,96,128]{2,1,0:T(8,128)S(1)}, u32[]{:S(2)}, u32[]{:S(2)}) collective-permute-start(f32[2,96,128]{2,1,0:T(8,128)S(1)} %copy-done.14), channel_id=1, source_target_pairs={{0,20},{4,24},{8,28},{12,0},{16,4},{20,8},{24,12},{28,16},{1,21},{... | collective-permute-start | bytes 294920 | tf_op jit(solution)/shard_map/ppermute | solution.py:770
  50.7 6.6 %copy_1.1.refs_8_.refs_0_ = f32[65536,128]{1,0:T(8,128)} custom-call(f32[4,2,160,256]{3,2,1,0:T(8,128)} %forward_0.1.after, f32[65536,128]{1,0:T(8,128)} %bitcast.7, f32[65536,128]{1,0:T(8,128)} %copy_0.1.refs_8_.refs_0_), custom_call_target="tpu_custom_call", output_to_operand_aliasing={{}: (2, {})} | custom-call | bytes 16777216 | tf_op jit(solution)/shard_map/copy_1/pallas_call | solution.py:732
  58.7 2.1 %collective-permute-done.3.refs_4_ = f32[2,96,128]{2,1,0:T(8,128)S(1)} collective-permute-done((f32[2,96,128]{2,1,0:T(8,128)S(1)}, f32[2,96,128]{2,1,0:T(8,128)S(1)}, u32[]{:S(2)}, u32[]{:S(2)}) %collective-permute-start.3) | collective-permute-done | bytes 98336 | tf_op jit(solution)/shard_map/ppermute | solution.py:770
  60.8 2.6 %collective-permute-done.5.refs_6_ = f32[2,96,128]{2,1,0:T(8,128)S(1)} collective-permute-done((f32[2,96,128]{2,1,0:T(8,128)S(1)}, f32[2,96,128]{2,1,0:T(8,128)S(1)}, u32[]{:S(2)}, u32[]{:S(2)}) %collective-permute-start.5) | collective-permute-done | bytes 98336 | tf_op jit(solution)/shard_map/ppermute | solution.py:770
  63.5 3.3 %forward_160.1 = (f32[2,96,256]{2,1,0:T(8,128)}, f32[2,96,256]{2,1,0:T(8,128)}, f32[2,96,256]{2,1,0:T(8,128)}, f32[2,96,256]{2,1,0:T(8,128)}) custom-call(bf16[1024,256]{1,0:T(8,128)(2,1)} %constant.8.clone.table, f32[8,256]{1,0:T(8,128)} %constant.10.clone.twiddles, f32[2,256,1024]{2,1,0:T(8,128)S(1)} %get-tuple-element.50.pupil, ...), custom_call_target="tpu_custom_call" | custom-call | flops 603979776 | bytes 8388608 | tf_op jit(solution)/shard_map/forward_160/pallas_call | solution.py:732
  69.4 6.6 %copy_2.1.copied.refs_0_ = f32[65536,128]{1,0:T(8,128)} custom-call(f32[2,96,256]{2,1,0:T(8,128)} %get-tuple-element.68.after.refs_1_, f32[65536,128]{1,0:T(8,128)} %bitcast.8, f32[65536,128]{1,0:T(8,128)} %copy_1.1.refs_8_.refs_0_), custom_call_target="tpu_custom_call", output_to_operand_aliasing={{}: (2, {})} | custom-call | bytes 16777216 | tf_op jit(solution)/shard_map/copy_2/pallas_call | solution.py:732
  78.0 6.8 %middle.1 = (f32[2,128,256]{2,1,0:T(8,128)S(1)}, f32[2,128,256]{2,1,0:T(8,128)S(1)}, f32[2,128,256]{2,1,0:T(8,128)S(1)}, f32[2,128,256]{2,1,0:T(8,128)S(1)}, f32[4,2,128,256]{3,2,1,0:T(8,128)S(1)}) custom-call(bf16[256,1024]{1,0:T(8,128)(2,1)} %constant.9.clone.table, f32[256,8]{1,0:T(8,128)} %constant.11.clone.twiddles, ...), custom_call_target="tpu_custom_call" | custom-call | flops 3221225472 | bytes 16777216 | tf_op jit(solution)/shard_map/middle/pallas_call | solution.py:732
  87.5 6.6 %copy_3.1.refs_5_ = f32[65536,128]{1,0:T(8,128)} custom-call(f32[2,128,256]{2,1,0:T(8,128)S(1)} %get-tuple-element.72.after.refs_0_, f32[65536,128]{1,0:T(8,128)} %bitcast.9, f32[65536,128]{1,0:T(8,128)} %copy_2.1.copied.refs_0_), custom_call_target="tpu_custom_call", output_to_operand_aliasing={{}: (2, {})} | custom-call | bytes 16777216 | tf_op jit(solution)/shard_map/copy_3/pallas_call | solution.py:732
  94.1 4.1 %collective-permute-done.18.refs_2_ = f32[2,128,256]{2,1,0:T(8,128)S(1)} collective-permute-done((f32[2,128,256]{2,1,0:T(8,128)S(1)}, f32[2,128,256]{2,1,0:T(8,128)S(1)}, u32[]{:S(2)}, u32[]{:S(2)}) %collective-permute-start.18) | collective-permute-done | bytes 262176 | tf_op jit(solution)/shard_map/ppermute | solution.py:779
  99.9 3.6 %backward_0.1 = (f32[2,128,128]{2,1,0:T(8,128)}, f32[2,128,128]{2,1,0:T(8,128)}, f32[2,128,128]{2,1,0:T(8,128)}, f32[2,128,128]{2,1,0:T(8,128)}, f32[2,128,128]{...) custom-call(bf16[1024,256]{1,0:T(8,128)(2,1)} %constant.8.clone.tabl, ...), custom_call_target="tpu_custom_call", output_to_operand_aliasing={{8}: (7, {}), {9}: (8, {})} | custom-call | flops 805306368 | bytes 8388608 | tf_op jit(solution)/shard_map/backward_0/pallas_call | solution.py:732
  103.5 4.2 %all-to-all-start.1 = ((f32[4,2,128,256]{3,2,1,0:T(8,128)}), f32[4,2,128,256]{3,2,1,0:T(8,128)S(1)}, u32[]{:S(2)}, u32[]{:S(2)}) async-start(f32[4,2,128,256]{3,2,1,0:T(8,128)} %get-tuple-element.86), calls=%async_computation.1 | async-start | bytes 2097152 | tf_op jit(solution)/shard_map/all_to_all | solution.py:776
  107.9 2.8 %collective-permute-start.21 = (f32[2,128,128]{2,1,0:T(8,128)}, f32[2,128,128]{2,1,0:T(8,128)S(1)}, u32[]{:S(2)}, u32[]{:S(2)}) collective-permute-start(f32[2,128,128]{2,1,0:T(8,128)} %get-tuple-element.80), channel_id=1, source_target_pairs={{0,8},{4,12},{8,16},{12,20},{16,24},{20,28},{24,0},{28,4},{1,9},{5... | collective-permute-start | bytes 393224 | tf_op jit(solution)/shard_map/ppermute | solution.py:770
  112.3 2.0 %collective-permute-start.24 = (f32[2,128,128]{2,1,0:T(8,128)}, f32[2,128,128]{2,1,0:T(8,128)}, u32[]{:S(2)}, u32[]{:S(2)}) collective-permute-start(f32[2,128,128]{2,1,0:T(8,128)} %get-tuple-element.83), channel_id=1, source_target_pairs={{0,20},{4,24},{8,28},{12,0},{16,4},{20,8},{24,12},{28,16},{1,21},{... | collective-permute-start | bytes 393224 | tf_op jit(solution)/shard_map/ppermute | solution.py:770
  114.3 5.9 %all-to-all-done.1.refs_0_ = f32[4,2,128,256]{3,2,1,0:T(8,128)S(1)} async-done(((f32[4,2,128,256]{3,2,1,0:T(8,128)}), f32[4,2,128,256]{3,2,1,0:T(8,128)S(1)}, u32[]{:S(2)}, u32[]{:S(2)}) %all-to-all-start.1) | async-done | bytes 1048608 | tf_op jit(solution)/shard_map/all_to_all | solution.py:776
  120.2 2.8 %backward_128.1 = (f32[2,128,128]{2,1,0:T(8,128)S(1)}, f32[2,128,128]{2,1,0:T(8,128)S(1)}, f32[2,128,128]{2,1,0:T(8,128)S(1)}, f32[2,128,128]{2,1,0:T(8,128)S(1)...) custom-call(bf16[1024,256]{1,0:T(8,128)(2,1)} %constant.8.clone.tabl, ...), custom_call_target="tpu_custom_call" | custom-call | flops 805306368 | bytes 8388608 | tf_op jit(solution)/shard_map/backward_128/pallas_call | solution.py:732
  127.8 2.7 %collective-permute-start.29 = (f32[2,128,128]{2,1,0:T(8,128)S(1)}, f32[2,128,128]{2,1,0:T(8,128)S(1)}, u32[]{:S(2)}, u32[]{:S(2)}) collective-permute-start(f32[2,128,128]{2,1,0:T(8,128)S(1)} %get-tuple-element.90), channel_id=1, source_target_pairs={{0,12},{4,16},{8,20},{12,24},{16,28},{20,0},{24,4},{28,8},{1,13},{... | collective-permute-start | bytes 393224 | tf_op jit(solution)/shard_map/ppermute | solution.py:770
  130.4 9.1 %collective-permute-done.25.refs_6_ = f32[2,128,128]{2,1,0:T(8,128)S(1)} collective-permute-done((f32[2,128,128]{2,1,0:T(8,128)}, f32[2,128,128]{2,1,0:T(8,128)S(1)}, u32[]{:S(2)}, u32[]{:S(2)}) %collective-permute-start.25) | collective-permute-done | bytes 131104 | tf_op jit(solution)/shard_map/ppermute | solution.py:770
  143.3 3.5 %update_0.1.buffer = f32[65536,128]{1,0:T(8,128)} custom-call(s32[8]{0:T(128)S(1)} %copy-done.2, s32[8]{0:T(128)S(1)} %copy-done.3, s32[8]{0:T(128)S(1)} %copy-done.4, f32[65536,128]{1,0:T(8,128)} %bitcast.10, f32[65536,128]{1,0:T(8,128)} %get-tuple-element.77.buffer, f32[2,128,128]{2,1,0:T(8,128)S(1)} %copy-done.1, ...), custom_call_target="tpu_custom_call", output_to_operand_aliasing={{}: (4, {})} | custom-call | bytes 4194304 | tf_op jit(solution)/shard_map/update_0/pallas_call | solution.py:732
  146.9 3.4 %collective-permute-done.29.refs_3_ = f32[2,128,128]{2,1,0:T(8,128)S(1)} collective-permute-done((f32[2,128,128]{2,1,0:T(8,128)S(1)}, f32[2,128,128]{2,1,0:T(8,128)S(1)}, u32[]{:S(2)}, u32[]{:S(2)}) %collective-permute-start.29) | collective-permute-done | bytes 131104 | tf_op jit(solution)/shard_map/ppermute | solution.py:770
  150.3 2.8 %collective-permute-done.30.refs_4_ = f32[2,128,128]{2,1,0:T(8,128)S(1)} collective-permute-done((f32[2,128,128]{2,1,0:T(8,128)S(1)}, f32[2,128,128]{2,1,0:T(8,128)S(1)}, u32[]{:S(2)}, u32[]{:S(2)}) %collective-permute-start.30) | collective-permute-done | bytes 131104 | tf_op jit(solution)/shard_map/ppermute | solution.py:770
  153.1 2.0 %collective-permute-done.32.refs_6_ = f32[2,128,128]{2,1,0:T(8,128)S(1)} collective-permute-done((f32[2,128,128]{2,1,0:T(8,128)S(1)}, f32[2,128,128]{2,1,0:T(8,128)S(1)}, u32[]{:S(2)}, u32[]{:S(2)}) %collective-permute-start.32) | collective-permute-done | bytes 131104 | tf_op jit(solution)/shard_map/ppermute | solution.py:770
  155.6 3.6 %update_128.1 = f32[65536,128]{1,0:T(8,128)} custom-call(s32[8]{0:T(128)S(1)} %copy-done.2, s32[8]{0:T(128)S(1)} %copy-done.3, s32[8]{0:T(128)S(1)} %copy-done.4, f32[65536,128]{1,0:T(8,128)} %bitcast.11, f32[65536,128]{1,0:T(8,128)} %update_0.1.buffer, f32[2,128,128]{2,1,0:T(8,128)S(1)} %get-tuple-element.87.refs_0_, ...), custom_call_target="tpu_custom_call", output_to_operand_aliasing={{}: (4, {})} | custom-call | bytes 4194304 | tf_op jit(solution)/shard_map/update_128/pallas_call | solution.py:732
  (86 shorter events, 32.0 us)
Async XLA Ops:
  6.5 23.5 %collective-permute-start.9 = (f32[2,160,128]{2,1,0:T(8,128)}, f32[2,160,128]{2,1,0:T(8,128)S(1)}, u32[]{:S(2)}, u32[]{:S(2)}) collective-permute-start(f32[2,160,128]{2,1,0:T(8,128)} %get-tuple-element.63), channel_id=1, source_target_pairs={{0,12},{4,16},{8,20},{12,24},{16,28},{20,0},{24,4},{28,8},{1,13},{... | collective-permute-start | bytes 491528 | tf_op jit(solution)/shard_map/ppermute | solution.py:770
  6.5 27.0 %collective-permute-start.10 = (f32[2,160,128]{2,1,0:T(8,128)}, f32[2,160,128]{2,1,0:T(8,128)S(1)}, u32[]{:S(2)}, u32[]{:S(2)}) collective-permute-start(f32[2,160,128]{2,1,0:T(8,128)} %get-tuple-element.64), channel_id=1, source_target_pairs={{0,16},{4,20},{8,24},{12,28},{16,0},{20,4},{24,8},{28,12},{1,17},{... | collective-permute-start | bytes 491528 | tf_op jit(solution)/shard_map/ppermute | solution.py:770
  7.9 25.6 %collective-permute-start.11 = (f32[2,160,128]{2,1,0:T(8,128)}, f32[2,160,128]{2,1,0:T(8,128)S(1)}, u32[]{:S(2)}, u32[]{:S(2)}) collective-permute-start(f32[2,160,128]{2,1,0:T(8,128)} %get-tuple-element.65), channel_id=1, source_target_pairs={{0,20},{4,24},{8,28},{12,0},{16,4},{20,8},{24,12},{28,16},{1,21},{... | collective-permute-start | bytes 491528 | tf_op jit(solution)/shard_map/ppermute | solution.py:770
  12.3 23.1 %collective-permute-start.12 = (f32[2,160,128]{2,1,0:T(8,128)S(1)}, f32[2,160,128]{2,1,0:T(8,128)S(1)}, u32[]{:S(2)}, u32[]{:S(2)}) collective-permute-start(f32[2,160,128]{2,1,0:T(8,128)S(1)} %copy-done.11), channel_id=1, source_target_pairs={{0,24},{4,28},{8,0},{12,4},{16,8},{20,12},{24,16},{28,20},{1,25},{... | collective-permute-start | bytes 491528 | tf_op jit(solution)/shard_map/ppermute | solution.py:770
  13.5 22.0 %collective-permute-start.13 = (f32[2,160,128]{2,1,0:T(8,128)S(1)}, f32[2,160,128]{2,1,0:T(8,128)S(1)}, u32[]{:S(2)}, u32[]{:S(2)}) collective-permute-start(f32[2,160,128]{2,1,0:T(8,128)S(1)} %copy-done.10), channel_id=1, source_target_pairs={{0,28},{4,0},{8,4},{12,8},{16,12},{20,16},{24,20},{28,24},{1,29},{... | collective-permute-start | bytes 491528 | tf_op jit(solution)/shard_map/ppermute | solution.py:770
  39.5 38.4 %all-to-all-start = ((f32[4,2,160,256]{3,2,1,0:T(8,128)}), f32[4,2,160,256]{3,2,1,0:T(8,128)}, u32[]{:S(2)}, u32[]{:S(2)}) async-start(f32[4,2,160,256]{3,2,1,0:T(8,128)} %forward_0.1.after), calls=%async_computation | async-start | bytes 2621440 | tf_op jit(solution)/shard_map/all_to_all | solution.py:776
  44.0 14.7 %collective-permute-start.2 = (f32[2,96,128]{2,1,0:T(8,128)}, f32[2,96,128]{2,1,0:T(8,128)S(1)}, u32[]{:S(2)}, u32[]{:S(2)}) collective-permute-start(f32[2,96,128]{2,1,0:T(8,128)} %get-tuple-element.55), channel_id=1, source_target_pairs={{0,12},{4,16},{8,20},{12,24},{16,28},{20,0},{24,4},{28,8},{1,13},{... | collective-permute-start | bytes 294920 | tf_op jit(solution)/shard_map/ppermute | solution.py:770
  45.9 15.0 %collective-permute-start.3 = (f32[2,96,128]{2,1,0:T(8,128)S(1)}, f32[2,96,128]{2,1,0:T(8,128)S(1)}, u32[]{:S(2)}, u32[]{:S(2)}) collective-permute-start(f32[2,96,128]{2,1,0:T(8,128)S(1)} %copy-done.15), channel_id=1, source_target_pairs={{0,16},{4,20},{8,24},{12,28},{16,0},{20,4},{24,8},{28,12},{1,17},{... | collective-permute-start | bytes 294920 | tf_op jit(solution)/shard_map/ppermute | solution.py:770
  46.9 14.0 %collective-permute-start.4 = (f32[2,96,128]{2,1,0:T(8,128)S(1)}, f32[2,96,128]{2,1,0:T(8,128)S(1)}, u32[]{:S(2)}, u32[]{:S(2)}) collective-permute-start(f32[2,96,128]{2,1,0:T(8,128)S(1)} %copy-done.14), channel_id=1, source_target_pairs={{0,20},{4,24},{8,28},{12,0},{16,4},{20,8},{24,12},{28,16},{1,21},{... | collective-permute-start | bytes 294920 | tf_op jit(solution)/shard_map/ppermute | solution.py:770
  48.9 14.5 %collective-permute-start.5 = (f32[2,96,128]{2,1,0:T(8,128)S(1)}, f32[2,96,128]{2,1,0:T(8,128)S(1)}, u32[]{:S(2)}, u32[]{:S(2)}) collective-permute-start(f32[2,96,128]{2,1,0:T(8,128)S(1)} %copy-done.13), channel_id=1, source_target_pairs={{0,24},{4,28},{8,0},{12,4},{16,8},{20,12},{24,16},{28,20},{1,25},{... | collective-permute-start | bytes 294920 | tf_op jit(solution)/shard_map/ppermute | solution.py:770
  49.9 13.6 %collective-permute-start.6 = (f32[2,96,128]{2,1,0:T(8,128)S(1)}, f32[2,96,128]{2,1,0:T(8,128)S(1)}, u32[]{:S(2)}, u32[]{:S(2)}) collective-permute-start(f32[2,96,128]{2,1,0:T(8,128)S(1)} %copy-done.12), channel_id=1, source_target_pairs={{0,28},{4,0},{8,4},{12,8},{16,12},{20,16},{24,20},{28,24},{1,29},{... | collective-permute-start | bytes 294920 | tf_op jit(solution)/shard_map/ppermute | solution.py:770
  66.7 9.3 %collective-permute-start.14 = (f32[2,96,256]{2,1,0:T(8,128)}, f32[2,96,256]{2,1,0:T(8,128)S(1)}, u32[]{:S(2)}, u32[]{:S(2)}) collective-permute-start(f32[2,96,256]{2,1,0:T(8,128)} %get-tuple-element.69), channel_id=1, source_target_pairs={{0,1},{1,0},{2,3},{3,2},{4,5},{5,4},{6,7},{7,6},{8,9},{9,8},{10,11... | collective-permute-start | bytes 589832 | tf_op jit(solution)/shard_map/ppermute | solution.py:779
  66.9 10.0 %collective-permute-start.15 = (f32[2,96,256]{2,1,0:T(8,128)}, f32[2,96,256]{2,1,0:T(8,128)S(1)}, u32[]{:S(2)}, u32[]{:S(2)}) collective-permute-start(f32[2,96,256]{2,1,0:T(8,128)} %get-tuple-element.70), channel_id=1, source_target_pairs={{0,2},{1,3},{2,0},{3,1},{4,6},{5,7},{6,4},{7,5},{8,10},{9,11},{10,... | collective-permute-start | bytes 589832 | tf_op jit(solution)/shard_map/ppermute | solution.py:779
  68.3 9.7 %collective-permute-start.16 = (f32[2,96,256]{2,1,0:T(8,128)}, f32[2,96,256]{2,1,0:T(8,128)}, u32[]{:S(2)}, u32[]{:S(2)}) collective-permute-start(f32[2,96,256]{2,1,0:T(8,128)} %get-tuple-element.71), channel_id=1, source_target_pairs={{0,3},{1,2},{2,1},{3,0},{4,7},{5,6},{6,5},{7,4},{8,11},{9,10},{10,... | collective-permute-start | bytes 589832 | tf_op jit(solution)/shard_map/ppermute | solution.py:779
  84.7 9.3 %collective-permute-start.17 = (f32[2,128,256]{2,1,0:T(8,128)S(1)}, f32[2,128,256]{2,1,0:T(8,128)S(1)}, u32[]{:S(2)}, u32[]{:S(2)}) collective-permute-start(f32[2,128,256]{2,1,0:T(8,128)S(1)} %get-tuple-element.73), channel_id=1, source_target_pairs={{0,1},{1,0},{2,3},{3,2},{4,5},{5,4},{6,7},{7,6},{8,9},{9,8},{10,11... | collective-permute-start | bytes 786440 | tf_op jit(solution)/shard_map/ppermute | solution.py:779
  86.2 12.0 %collective-permute-start.18 = (f32[2,128,256]{2,1,0:T(8,128)S(1)}, f32[2,128,256]{2,1,0:T(8,128)S(1)}, u32[]{:S(2)}, u32[]{:S(2)}) collective-permute-start(f32[2,128,256]{2,1,0:T(8,128)S(1)} %get-tuple-element.74), channel_id=1, source_target_pairs={{0,2},{1,3},{2,0},{3,1},{4,6},{5,7},{6,4},{7,5},{8,10},{9,11},{10,... | collective-permute-start | bytes 786440 | tf_op jit(solution)/shard_map/ppermute | solution.py:779
  87.4 12.5 %collective-permute-start.19 = (f32[2,128,256]{2,1,0:T(8,128)S(1)}, f32[2,128,256]{2,1,0:T(8,128)S(1)}, u32[]{:S(2)}, u32[]{:S(2)}) collective-permute-start(f32[2,128,256]{2,1,0:T(8,128)S(1)} %get-tuple-element.75), channel_id=1, source_target_pairs={{0,3},{1,2},{2,1},{3,0},{4,7},{5,6},{6,5},{7,4},{8,11},{9,10},{10,... | collective-permute-start | bytes 786440 | tf_op jit(solution)/shard_map/ppermute | solution.py:779
  103.5 16.7 %all-to-all-start.1 = ((f32[4,2,128,256]{3,2,1,0:T(8,128)}), f32[4,2,128,256]{3,2,1,0:T(8,128)S(1)}, u32[]{:S(2)}, u32[]{:S(2)}) async-start(f32[4,2,128,256]{3,2,1,0:T(8,128)} %get-tuple-element.86), calls=%async_computation.1 | async-start | bytes 2097152 | tf_op jit(solution)/shard_map/all_to_all | solution.py:776
  107.7 15.3 %collective-permute-start.20 = (f32[2,128,128]{2,1,0:T(8,128)}, f32[2,128,128]{2,1,0:T(8,128)S(1)}, u32[]{:S(2)}, u32[]{:S(2)}) collective-permute-start(f32[2,128,128]{2,1,0:T(8,128)} %get-tuple-element.79), channel_id=1, source_target_pairs={{0,4},{4,8},{8,12},{12,16},{16,20},{20,24},{24,28},{28,0},{1,5},{5... | collective-permute-start | bytes 393224 | tf_op jit(solution)/shard_map/ppermute | solution.py:770
  107.9 15.1 %collective-permute-start.21 = (f32[2,128,128]{2,1,0:T(8,128)}, f32[2,128,128]{2,1,0:T(8,128)S(1)}, u32[]{:S(2)}, u32[]{:S(2)}) collective-permute-start(f32[2,128,128]{2,1,0:T(8,128)} %get-tuple-element.80), channel_id=1, source_target_pairs={{0,8},{4,12},{8,16},{12,20},{16,24},{20,28},{24,0},{28,4},{1,9},{5... | collective-permute-start | bytes 393224 | tf_op jit(solution)/shard_map/ppermute | solution.py:770
  110.8 14.1 %collective-permute-start.22 = (f32[2,128,128]{2,1,0:T(8,128)}, f32[2,128,128]{2,1,0:T(8,128)S(1)}, u32[]{:S(2)}, u32[]{:S(2)}) collective-permute-start(f32[2,128,128]{2,1,0:T(8,128)} %get-tuple-element.81), channel_id=1, source_target_pairs={{0,12},{4,16},{8,20},{12,24},{16,28},{20,0},{24,4},{28,8},{1,13},{... | collective-permute-start | bytes 393224 | tf_op jit(solution)/shard_map/ppermute | solution.py:770
  110.8 17.0 %collective-permute-start.23 = (f32[2,128,128]{2,1,0:T(8,128)}, f32[2,128,128]{2,1,0:T(8,128)}, u32[]{:S(2)}, u32[]{:S(2)}) collective-permute-start(f32[2,128,128]{2,1,0:T(8,128)} %get-tuple-element.82), channel_id=1, source_target_pairs={{0,16},{4,20},{8,24},{12,28},{16,0},{20,4},{24,8},{28,12},{1,17},{... | collective-permute-start | bytes 393224 | tf_op jit(solution)/shard_map/ppermute | solution.py:770
  112.3 15.5 %collective-permute-start.24 = (f32[2,128,128]{2,1,0:T(8,128)}, f32[2,128,128]{2,1,0:T(8,128)}, u32[]{:S(2)}, u32[]{:S(2)}) collective-permute-start(f32[2,128,128]{2,1,0:T(8,128)} %get-tuple-element.83), channel_id=1, source_target_pairs={{0,20},{4,24},{8,28},{12,0},{16,4},{20,8},{24,12},{28,16},{1,21},{... | collective-permute-start | bytes 393224 | tf_op jit(solution)/shard_map/ppermute | solution.py:770
  123.0 16.6 %collective-permute-start.25 = (f32[2,128,128]{2,1,0:T(8,128)}, f32[2,128,128]{2,1,0:T(8,128)S(1)}, u32[]{:S(2)}, u32[]{:S(2)}) collective-permute-start(f32[2,128,128]{2,1,0:T(8,128)} %get-tuple-element.84), channel_id=1, source_target_pairs={{0,24},{4,28},{8,0},{12,4},{16,8},{20,12},{24,16},{28,20},{1,25},{... | collective-permute-start | bytes 393224 | tf_op jit(solution)/shard_map/ppermute | solution.py:770
  123.1 17.5 %collective-permute-start.26 = (f32[2,128,128]{2,1,0:T(8,128)}, f32[2,128,128]{2,1,0:T(8,128)S(1)}, u32[]{:S(2)}, u32[]{:S(2)}) collective-permute-start(f32[2,128,128]{2,1,0:T(8,128)} %get-tuple-element.85), channel_id=1, source_target_pairs={{0,28},{4,0},{8,4},{12,8},{16,12},{20,16},{24,20},{28,24},{1,29},{... | collective-permute-start | bytes 393224 | tf_op jit(solution)/shard_map/ppermute | solution.py:770
  124.9 15.7 %collective-permute-start.27 = (f32[2,128,128]{2,1,0:T(8,128)S(1)}, f32[2,128,128]{2,1,0:T(8,128)S(1)}, u32[]{:S(2)}, u32[]{:S(2)}) collective-permute-start(f32[2,128,128]{2,1,0:T(8,128)S(1)} %get-tuple-element.88), channel_id=1, source_target_pairs={{0,4},{4,8},{8,12},{12,16},{16,20},{20,24},{24,28},{28,0},{1,5},{5... | collective-permute-start | bytes 393224 | tf_op jit(solution)/shard_map/ppermute | solution.py:770
  127.8 14.4 %collective-permute-start.28 = (f32[2,128,128]{2,1,0:T(8,128)S(1)}, f32[2,128,128]{2,1,0:T(8,128)S(1)}, u32[]{:S(2)}, u32[]{:S(2)}) collective-permute-start(f32[2,128,128]{2,1,0:T(8,128)S(1)} %get-tuple-element.89), channel_id=1, source_target_pairs={{0,8},{4,12},{8,16},{12,20},{16,24},{20,28},{24,0},{28,4},{1,9},{5... | collective-permute-start | bytes 393224 | tf_op jit(solution)/shard_map/ppermute | solution.py:770
  127.8 22.5 %collective-permute-start.29 = (f32[2,128,128]{2,1,0:T(8,128)S(1)}, f32[2,128,128]{2,1,0:T(8,128)S(1)}, u32[]{:S(2)}, u32[]{:S(2)}) collective-permute-start(f32[2,128,128]{2,1,0:T(8,128)S(1)} %get-tuple-element.90), channel_id=1, source_target_pairs={{0,12},{4,16},{8,20},{12,24},{16,28},{20,0},{24,4},{28,8},{1,13},{... | collective-permute-start | bytes 393224 | tf_op jit(solution)/shard_map/ppermute | solution.py:770
  139.6 13.5 %collective-permute-start.30 = (f32[2,128,128]{2,1,0:T(8,128)S(1)}, f32[2,128,128]{2,1,0:T(8,128)S(1)}, u32[]{:S(2)}, u32[]{:S(2)}) collective-permute-start(f32[2,128,128]{2,1,0:T(8,128)S(1)} %get-tuple-element.91), channel_id=1, source_target_pairs={{0,16},{4,20},{8,24},{12,28},{16,0},{20,4},{24,8},{28,12},{1,17},{... | collective-permute-start | bytes 393224 | tf_op jit(solution)/shard_map/ppermute | solution.py:770
  140.6 12.5 %collective-permute-start.31 = (f32[2,128,128]{2,1,0:T(8,128)S(1)}, f32[2,128,128]{2,1,0:T(8,128)S(1)}, u32[]{:S(2)}, u32[]{:S(2)}) collective-permute-start(f32[2,128,128]{2,1,0:T(8,128)S(1)} %get-tuple-element.92), channel_id=1, source_target_pairs={{0,20},{4,24},{8,28},{12,0},{16,4},{20,8},{24,12},{28,16},{1,21},{... | collective-permute-start | bytes 393224 | tf_op jit(solution)/shard_map/ppermute | solution.py:770
  140.6 14.5 %collective-permute-start.32 = (f32[2,128,128]{2,1,0:T(8,128)S(1)}, f32[2,128,128]{2,1,0:T(8,128)S(1)}, u32[]{:S(2)}, u32[]{:S(2)}) collective-permute-start(f32[2,128,128]{2,1,0:T(8,128)S(1)} %get-tuple-element.93), channel_id=1, source_target_pairs={{0,24},{4,28},{8,0},{12,4},{16,8},{20,12},{24,16},{28,20},{1,25},{... | collective-permute-start | bytes 393224 | tf_op jit(solution)/shard_map/ppermute | solution.py:770
  142.2 13.4 %collective-permute-start.33 = (f32[2,128,128]{2,1,0:T(8,128)S(1)}, f32[2,128,128]{2,1,0:T(8,128)S(1)}, u32[]{:S(2)}, u32[]{:S(2)}) collective-permute-start(f32[2,128,128]{2,1,0:T(8,128)S(1)} %get-tuple-element.94), channel_id=1, source_target_pairs={{0,28},{4,0},{8,4},{12,8},{16,12},{20,16},{24,20},{28,24},{1,29},{... | collective-permute-start | bytes 393224 | tf_op jit(solution)/shard_map/ppermute | solution.py:770
  (20 other events, 238.8 us)
